TPU v7x, 128 devices: a whole 4x4x4 slice. The times are simulated.
128 devices in a mesh: ctx: 8 (over x_hi, z), batch: 16 (over x_lo, y, core).
Axes of the slice: x: 4 (x_hi: 2, x_lo: 2; x = x_hi * 2 + x_lo), y: 4, z: 4, core: 2. Of those that a mesh axis runs over, the one named last changes fastest.
Arguments:
- queries: bfloat16 [768, 8192], P('batch', 'ctx'), may hold values from -24 to 24
- new_key: bfloat16 [768, 1024], P('batch', 'ctx'), may hold values from -16 to 16
- new_value: bfloat16 [768, 1024], P('batch', 'ctx'), may hold values from -6 to 6
- prefix_keys: bfloat16 [16384, 1024], P('ctx'), may hold values from -9 to 9
- prefix_values: bfloat16 [16384, 1024], P('ctx'), may hold values from -8 to 8
- suffix_keys: bfloat16 [768, 128, 1024], P('batch', None, 'ctx'), may hold values from -16 to 16
- suffix_values: bfloat16 [768, 128, 1024], P('batch', None, 'ctx'), may hold values from -6 to 6
- suffix_lengths: int32 [768], P('batch'), may hold values from 1 to 128, as said below
- out_weight: bfloat16 [8192, 8192], P('ctx', 'batch'), may hold values from -0.0625 to 0.0625
- residual: bfloat16 [768, 8192], P(None, 'batch'), may hold values from -8 to 8
- norm_gain: bfloat16 [8192], P('batch'), may hold values from 0.3984375 to 1.1953125
- gate_weight: bfloat16 [8192, 28672], P('batch', 'ctx'), may hold values from -0.0625 to 0.0625
- up_weight: bfloat16 [8192, 28672], P('batch', 'ctx'), may hold values from -0.0625 to 0.0625
Outputs:
- stream: bfloat16 [768, 8192], P(None, 'batch')
- activation: bfloat16 [768, 28672], P('batch', 'ctx')
Inputs may be any that keep to these rules, and one draw needn't show every extreme that they name: `suffix_lengths`: each leaf has between 1 and 128 filled suffix slots, the first ones; some leaf has exactly 128 and some leaf exactly 1.
All inputs are finite; a program needn't handle non-finite values.
Results may differ from a plain program's by a relative error of at most 0.025.
Values may be sent and summed in bfloat16 or wider, within the bound.
No kernel may reach another device: no remote copies, remote signals or barrier semaphores. Data moves between devices by JAX's collectives and lax.ppermute only.
A program may use at most 128 MiB of HBM per device.

v0:
```python
import jax
import jax.numpy as jnp
from jax import lax
from jax.sharding import PartitionSpec as P

D = 8192
KV = 8
HD = 128
SUF = 128
GROUP = 8


def on_device(
    queries,
    new_key,
    new_value,
    prefix_keys,
    prefix_values,
    suffix_keys,
    suffix_values,
    suffix_lengths,
    out_weight,
    residual,
    norm_gain,
    gate_weight,
    up_weight,
):
    leaves = queries.shape[0]
    kv_local = new_key.shape[1] // HD
    score_scale = 1.0 / jnp.sqrt(jnp.float32(HD))
    query_everywhere = lax.all_gather(queries, "ctx", axis=1, tiled=True)
    query_all = query_everywhere.reshape(leaves, KV, GROUP, HD)
    keys_here = prefix_keys.reshape(-1, KV, HD)
    values_here = prefix_values.reshape(-1, KV, HD)
    scores = (
        jnp.einsum("lkgd,pkd->klgp", query_all, keys_here, preferred_element_type=jnp.float32)
        * score_scale
    )
    local_max = jnp.max(scores, -1)
    local_w = jnp.exp(scores - local_max[..., None])
    local_total = jnp.sum(local_w, -1)
    local_out = jnp.einsum(
        "klgp,pkd->klgd",
        local_w.astype(jnp.bfloat16),
        values_here,
        preferred_element_type=jnp.float32,
    )
    highest = lax.pmax(local_max, "ctx")
    factor = jnp.exp(local_max - highest)
    summed_out, summed_total = (
        lax.psum_scatter(local_out * factor[..., None], "ctx", scatter_dimension=0, tiled=True),
        lax.psum_scatter(local_total * factor, "ctx", scatter_dimension=0, tiled=True),
    )
    own_max = lax.dynamic_slice_in_dim(highest, lax.axis_index("ctx") * kv_local, kv_local, 0)
    part_max = own_max[None]
    part_total = summed_total[None]
    part_out = summed_out[None]
    query_mine = queries.reshape(leaves, kv_local, GROUP, HD)
    keys_suffix = suffix_keys.reshape(leaves, SUF, kv_local, HD)
    values_suffix = suffix_values.reshape(leaves, SUF, kv_local, HD)
    suf_scores = (
        jnp.einsum("lkgd,lskd->klgs", query_mine, keys_suffix, preferred_element_type=jnp.float32)
        * score_scale
    )
    valid = jnp.arange(SUF, dtype=jnp.int32)[None, :] < suffix_lengths[:, None]
    suf_scores = jnp.where(valid[None, :, None, :], suf_scores, jnp.float32(-1e30))
    fresh_scores = (
        jnp.einsum(
            "lkgd,lkd->klg",
            query_mine,
            new_key.reshape(leaves, kv_local, HD),
            preferred_element_type=jnp.float32,
        )
        * score_scale
    )
    top = jnp.maximum(jnp.maximum(jnp.max(part_max, 0), jnp.max(suf_scores, -1)), fresh_scores)
    pre_w = jnp.exp(part_max - top[None])
    suf_w = jnp.exp(suf_scores - top[..., None])
    new_w = jnp.exp(fresh_scores - top)
    total = jnp.sum(part_total * pre_w, 0) + jnp.sum(suf_w, -1) + new_w
    numer = jnp.sum(part_out * pre_w[..., None], 0)
    numer = numer + jnp.einsum(
        "klgs,lskd->klgd",
        suf_w.astype(jnp.bfloat16),
        values_suffix,
        preferred_element_type=jnp.float32,
    )
    value_new = (
        new_value.reshape(leaves, kv_local, HD)
        .astype(jnp.float32)
        .transpose(1, 0, 2)[:, :, None, :]
    )
    numer = numer + new_w.astype(jnp.bfloat16).astype(jnp.float32)[..., None] * value_new
    attended = (numer / total[..., None]).astype(jnp.bfloat16)
    attended = attended.transpose(1, 0, 2, 3).reshape(leaves, kv_local * GROUP * HD)
    partial_sums = jnp.dot(
        lax.all_gather(attended, "batch", axis=0, tiled=True),
        out_weight,
        preferred_element_type=jnp.float32,
    )
    mixed = lax.psum(partial_sums, "ctx")
    stream = (residual.astype(jnp.float32) + mixed).astype(jnp.bfloat16)
    wide = stream.astype(jnp.float32)
    squares = jnp.sum(wide * wide, axis=1)
    scaled = (wide * norm_gain.astype(jnp.float32)[None, :]).astype(jnp.bfloat16)
    hidden_here = gate_weight.shape[1]
    square_all = lax.psum(squares, "batch")
    summed = lax.psum_scatter(
        jnp.concatenate(
            [
                jnp.dot(scaled, gate_weight, preferred_element_type=jnp.float32),
                jnp.dot(scaled, up_weight, preferred_element_type=jnp.float32),
            ],
            axis=1,
        ),
        "batch",
        scatter_dimension=0,
        tiled=True,
    )
    squared_row_sums = lax.dynamic_slice_in_dim(
        square_all, lax.axis_index("batch") * leaves, leaves, 0
    )
    rms = jnp.sqrt(squared_row_sums / D + 1e-05)
    gate = summed[:, :hidden_here] / rms[:, None]
    up = summed[:, hidden_here:] / rms[:, None]
    activation = (jax.nn.silu(gate) * up).astype(jnp.bfloat16)
    return (stream, activation)


def solution(mesh):
    in_specs = (
        P("batch", "ctx"),
        P("batch", "ctx"),
        P("batch", "ctx"),
        P("ctx", None),
        P("ctx", None),
        P("batch", None, "ctx"),
        P("batch", None, "ctx"),
        P("batch"),
        P("ctx", "batch"),
        P(None, "batch"),
        P("batch"),
        P("batch", "ctx"),
        P("batch", "ctx"),
    )
    out_specs = (P(None, "batch"), P("batch", "ctx"))
    return jax.shard_map(
        on_device, mesh=mesh, in_specs=in_specs, out_specs=out_specs, check_vma=False
    )
```

profile of v0, /device:TPU:0, one launch (start us, length us, event | category | flops | bytes accessed | tf_op | source)
XLA Modules:
  0.0 536.2 jit_solution(6679195347141762144)
XLA Ops:
  7.2 37.0 %all_gather.6 = bf16[48,8192]{1,0:T(8,128)(2,1)S(1)} all-gather(bf16[48,1024]{1,0:T(8,128)(2,1)} %param.13), channel_id=1, replica_groups=mesh['ctx'=8,'batch'=16] {'ctx'}, dimensions={1}, use_global_device_ids=true | all-gather | bytes 884736 | tf_op jit(solution)/shard_map/all_gather | solution.py:31
  44.4 3.3 copy.29
  47.7 10.1 %multiply_reduce_fusion = (f32[8,48,8]{2,1,0:T(8,128)S(1)}, f32[8,48,8,2048]{3,2,1,0:T(8,128)}) fusion(bf16[2048,8,128,1]{2,1,0,3:T(8,128)(2,1)S(1)} %bitcast.48, bf16[48,8,8,128]{3,2,1,0:T(8,128)(2,1)S(1)} %bitcast.52), kind=kOutput, calls=%fused_computation.1 | convolution fusion | flops 1623192576 | bytes 30158848 | tf_op jit(solution)/shard_map/lkgd,pkd->klgp/dot_general | solution.py:36
  57.8 44.2 %pmax.7 = f32[8,48,8]{2,1,0:T(8,128)S(1)} all-reduce(f32[8,48,8]{2,1,0:T(8,128)S(1)} %get-tuple-element.10), channel_id=1, replica_groups=mesh['ctx'=8,'batch'=16] {'ctx'}, use_global_device_ids=true, to_apply=%region_1.0 | all-reduce | flops 3072 | bytes 24576 | tf_op jit(solution)/shard_map/pmax | solution.py:48
  102.0 10.8 %fusion = f32[8,48,8]{2,1,0:T(8,128)S(1)} fusion(f32[8,48,8,2048]{3,2,1,0:T(8,128)} %get-tuple-element.11, f32[8,48,8]{2,1,0:T(8,128)S(1)} %get-tuple-element.10), kind=kLoop, calls=%fused_computation.3 | loop fusion | flops 18871296 | bytes 25190400 | tf_op jit(solution)/shard_map/reduce_sum | solution.py:41
  112.8 0.7 fusion.39
  113.6 3.3 copy.30
  116.9 11.6 %fusion.11 = f32[8,48,8,128]{3,2,1,0:T(8,128)} fusion(bf16[2048,8,128,1]{2,1,0,3:T(8,128)(2,1)S(1)} %bitcast.51, f32[8,48,8,2048]{3,2,1,0:T(8,128)} %get-tuple-element.11, f32[8,48,8]{2,1,0:T(8,128)S(1)} %get-tuple-element.10, f32[8,48,8]{2,1,0:T(8,128)S(1)} %get-tuple-element.7), kind=kOutput, calls=%fused_computation.16 | convolution fusion | flops 1629880320 | bytes 30957568 | tf_op jit(solution)/shard_map/klgp,pkd->klgd/dot_general | solution.py:42
  128.9 1.0 fusion.40
  130.2 50.5 %reduce-scatter.6.cloned.1.call-done = f32[1,48,8]{2,1,0:T(8,128)} async-done(((f32[8,48,8]{2,1,0:T(8,128)}), f32[1,48,8]{2,1,0:T(8,128)}) %reduce-scatter.6.cloned.1.call-update) | async-done | bytes 1552 | tf_op jit(solution)/shard_map/reduce_scatter | solution.py:52
  180.7 0.8 convert_convert_fusion
  181.4 75.6 %reduce-scatter.4.cloned.1.call-done = f32[1,48,8,128]{3,2,1,0:T(8,128)} async-done(((f32[8,48,8,128]{3,2,1,0:T(8,128)}), f32[1,48,8,128]{3,2,1,0:T(8,128)}) %reduce-scatter.4.cloned.1.call-update) | async-done | bytes 196624 | tf_op jit(solution)/shard_map/reduce_scatter | solution.py:51
  257.0 2.0 fusion.19
  259.0 0.7 copy.48
  259.8 32.1 %all-gather.2.cloned.1.call-done = bf16[768,1024]{1,0:T(8,128)(2,1)} async-done(((bf16[48,1024]{1,0:T(8,128)(2,1)}), bf16[768,1024]{1,0:T(8,128)(2,1)}) %all-gather.2.cloned.1.call-update) | async-done | bytes 1572880 | tf_op jit(solution)/shard_map/all_gather | solution.py:97
  291.9 3.8 fusion.41
  296.0 90.4 %all-reduce.2.cloned.1.call-done = f32[768,512]{1,0:T(8,128)} async-done(((f32[768,512]{1,0:T(8,128)}), f32[768,512]{1,0:T(8,128)}) %all-reduce.2.cloned.1.call-update) | async-done | bytes 1572880 | tf_op jit(solution)/shard_map/psum | solution.py:101
  386.4 1.7 fusion.10
  388.1 5.4 %fusion.21 = f32[768,3584]{1,0:T(8,128)S(1)} fusion(bf16[512,3584]{1,0:T(8,128)(2,1)} %param.25, bf16[768,512]{1,0:T(8,128)(2,1)S(1)} %get-tuple-element.3, f32[512]{0:T(512)S(1)} %convert_element_type.50), kind=kOutput, calls=%fused_computation.24 | convolution fusion | flops 2819751936 | bytes 15468544 | tf_op jit(solution)/shard_map/dot_general | solution.py:112
  393.5 3.0 fusion.23
  396.5 7.6 %pad_maximum_fusion = f32[768,7168]{1,0:T(8,128)} fusion(f32[768,3584]{1,0:T(8,128)S(1)} %fusion.21, f32[768,3584]{1,0:T(8,128)S(1)} %fusion.23), kind=kLoop, calls=%fused_computation.2 | loop fusion | flops 5505024 | bytes 44040192 | tf_op jit(solution)/shard_map/concatenate | solution.py:109
  404.2 27.9 %psum.15 = f32[768]{0:T(1024)S(1)} all-reduce(f32[768]{0:T(1024)S(1)} %get-tuple-element.2), channel_id=1, replica_groups=mesh['ctx'=8,'batch'=16] {'batch'}, use_global_device_ids=true, to_apply=%region_10.11 | all-reduce | flops 768 | bytes 6144 | tf_op jit(solution)/shard_map/psum | solution.py:107
  432.1 95.3 %reduce-scatter.8.cloned.1.call-done = f32[48,7168]{1,0:T(8,128)} async-done(((f32[768,7168]{1,0:T(8,128)}), f32[48,7168]{1,0:T(8,128)}) %reduce-scatter.8.cloned.1.call-update) | async-done | bytes 1376272 | tf_op jit(solution)/shard_map/reduce_scatter | solution.py:108
  527.4 2.3 fusion.26
  (39 shorter events, 1.3 us)
Async XLA Ops:
  7.2 121.8 %copy-start = (bf16[48,128,128]{2,1,0:T(8,128)(2,1)S(1)}, bf16[48,128,128]{2,1,0:T(8,128)(2,1)}, u32[]{:S(2)}) copy-start(bf16[48,128,128]{2,1,0:T(8,128)(2,1)} %param.18) | copy-start | bytes 4718596
  7.2 173.5 %reduce-scatter.6.cloned.1.call-start = ((), (), s32[]{:S(2)}) async-start(), calls=%async_computation.4 | async-start | bytes 221184 | tf_op jit(solution)/shard_map/reduce_scatter | solution.py:52
  113.5 143.5 %reduce-scatter.4.cloned.1.call-start = ((), (), s32[]{:S(2)}) async-start(), calls=%async_computation.3 | async-start | bytes 1769472 | tf_op jit(solution)/shard_map/reduce_scatter | solution.py:51
  116.9 11.7 %copy-start.5 = (bf16[48,128]{1,0:T(8,128)(2,1)S(1)}, bf16[48,128]{1,0:T(8,128)(2,1)}, u32[]{:S(2)}) copy-start(bf16[48,128]{1,0:T(8,128)(2,1)} %param.15) | copy-start | bytes 36868
  116.9 11.7 %copy-start.4 = (bf16[48,1024]{1,0:T(8,128)(2,1)S(1)}, bf16[48,1024]{1,0:T(8,128)(2,1)}, u32[]{:S(2)}) copy-start(bf16[48,1024]{1,0:T(8,128)(2,1)} %param.13) | copy-start | bytes 294916
  116.9 11.7 %copy-start.7 = (s32[48]{0:T(128)S(1)}, s32[48]{0:T(128)}, u32[]{:S(2)}) copy-start(s32[48]{0:T(128)} %param.20) | copy-start | bytes 580
  116.9 11.8 %copy-start.9 = (bf16[48,128]{1,0:T(8,128)(2,1)S(1)}, bf16[48,128]{1,0:T(8,128)(2,1)}, u32[]{:S(2)}) copy-start(bf16[48,128]{1,0:T(8,128)(2,1)} %param.14) | copy-start | bytes 36868
  128.5 163.3 %all-gather.2.cloned.1.call-start = ((), (), s32[]{:S(2)}) async-start(), calls=%async_computation.5 | async-start | bytes 1671168 | tf_op jit(solution)/shard_map/all_gather | solution.py:97
  259.7 36.2 %copy-start.6 = (bf16[512]{0:T(512)(128)(2,1)S(1)}, bf16[512]{0:T(512)(128)(2,1)}, u32[]{:S(2)}) copy-start(bf16[512]{0:T(512)(128)(2,1)} %param.23) | copy-start | bytes 3076
  259.7 126.6 %copy-start.2 = (bf16[768,512]{1,0:T(8,128)(2,1)S(1)}, bf16[768,512]{1,0:T(8,128)(2,1)}, u32[]{:S(2)}) copy-start(bf16[768,512]{1,0:T(8,128)(2,1)} %param.22) | copy-start | bytes 2359300
  259.7 126.6 %all-reduce.2.cloned.1.call-start = ((), (), s32[]{:S(2)}) async-start(), calls=%async_computation.6 | async-start | bytes 3145728 | tf_op jit(solution)/shard_map/psum | solution.py:101
  295.7 231.7 %reduce-scatter.8.cloned.1.call-start = ((), (), s32[]{:S(2)}) async-start(), calls=%async_computation.7 | async-start | bytes 23396352 | tf_op jit(solution)/shard_map/reduce_scatter | solution.py:108
  388.1 5.4 %copy-start.3 = (bf16[768,512]{1,0:T(8,128)(2,1)}, bf16[768,512]{1,0:T(8,128)(2,1)S(1)}, u32[]{:S(2)}) copy-start(bf16[768,512]{1,0:T(8,128)(2,1)S(1)} %get-tuple-element.3) | copy-start | bytes 2359300
  388.1 5.4 %copy-start.8 = (bf16[512,3584]{1,0:T(8,128)(2,1)S(1)}, bf16[512,3584]{1,0:T(8,128)(2,1)}, u32[]{:S(2)}) copy-start(bf16[512,3584]{1,0:T(8,128)(2,1)} %param.24) | copy-start | bytes 11010052
  404.2 125.5 %copy-start.1 = (bf16[48,128,128]{2,1,0:T(8,128)(2,1)S(1)}, bf16[48,128,128]{2,1,0:T(8,128)(2,1)}, u32[]{:S(2)}) copy-start(bf16[48,128,128]{2,1,0:T(8,128)(2,1)} %param.18) | copy-start | bytes 4718596
Sparse Core Ops, SparseCore 0:
  113.7 66.9 reduce-scatter.5
  184.4 72.6 reduce-scatter.3
  259.8 31.9 all-gather.1
  295.8 90.4 all-reduce.1
  404.3 123.0 reduce-scatter.7
where the time goes:
time: 537 us; the launch traced here: 536 us
  waiting for transfers between devices  344 us (64%)
  blocking collectives  109 us (20%)
  matrix products  37 us (7%)
  other arithmetic  24.3 us (5%)
  between operations  14 us (3%)
  local copies, waits for them, and re-layouts  7.49 us (1%)
    reduce_scatter x1, waiting for transfers between devices, on_device(): lax.psum_scatter(jnp.concatenate([jnp.dot(scaled, gate_weight, preferred_...  95.3 us
    psum x1, waiting for transfers between devices, on_device(): mixed = lax.psum(partial_sums, 'ctx')  90.4 us
    reduce_scatter x1, waiting for transfers between devices, on_device(): lax.psum_scatter(local_out * factor[..., None], 'ctx', scatter_dimension=...  75.6 us
    reduce_scatter x1, waiting for transfers between devices, on_device(): lax.psum_scatter(local_total * factor, 'ctx', scatter_dimension=0, tiled=...  50.5 us
    pmax x1, blocking collectives, on_device(): highest = lax.pmax(local_max, 'ctx')  44.2 us
    all_gather x1, blocking collectives, on_device(): query_everywhere = lax.all_gather(queries, 'ctx', axis=1, tiled=True)  37 us
    all_gather x1, waiting for transfers between devices, on_device(): lax.all_gather(attended, 'batch', axis=0, tiled=True)  32.1 us
    psum x1, blocking collectives, on_device(): square_all = lax.psum(squares, 'batch')  27.9 us
  transfers between devices with their start and end apart: 5, of which 5 were waited for; matrix products, arithmetic and copies ran while one was open for 3% of the time, Pallas kernels for 0%

commit v1 on v0

v1 whole, which is shorter than its diff:
```python
import jax
import jax.numpy as jnp
from jax import lax
from jax.experimental import pallas as pl
from jax.experimental.pallas import tpu as pltpu
from jax.sharding import PartitionSpec as P

D = 8192
KV = 8
HD = 128
SUF = 128
GROUP = 8
ROWS = 48
QROWS = ROWS * GROUP
META = 16
PAYLOAD = QROWS + QROWS // 128 * META
PRE = 2048
HALF = 512
HIDDEN = 3584
A_COLS = 1536
B_COLS = HIDDEN - A_COLS
TILE = 512
BF = jnp.bfloat16
F32 = jnp.float32
VMEM = 48 * 1024 * 1024


def ctx_perm(flip, s):
    return [(x * 4 + z, (x ^ flip) * 4 + (z + s) % 4) for x in range(2) for z in range(4)]


def batch_perm(flip_x, s, flip_core):
    return [
        (x * 8 + y * 2 + k, (x ^ flip_x) * 8 + (y + s) % 4 * 2 + (k ^ flip_core))
        for x in range(2)
        for y in range(4)
        for k in range(2)
    ]


def over_ctx(v, flip, s):
    return lax.ppermute(v, "ctx", ctx_perm(flip, s))


def over_batch(v, flip_x, s, flip_core=0):
    return lax.ppermute(v, "batch", batch_perm(flip_x, s, flip_core))


def nt_dot(a, b):
    return lax.dot_general(a, b, (((1,), (1,)), ((), ())), preferred_element_type=F32)


def heads_as_rows(q):
    return jnp.concatenate([q[:, h * HD : (h + 1) * HD] for h in range(GROUP)], axis=0)


def split3(v):
    hi = v.astype(BF).astype(F32)
    rest = v - hi
    mid = rest.astype(BF).astype(F32)
    return hi, mid, rest - mid


def prefix_kernel(group_ref, q_ref, k_ref, v_ref, first_ref, second_ref):
    scale = 1.0 / (HD**0.5)
    q = heads_as_rows(q_ref[0])
    k = k_ref[...]
    v = v_ref[...]
    outs, metas = [], []
    column = lax.broadcasted_iota(jnp.int32, (128, 128), 1)
    for t in range(QROWS // 128):
        s = nt_dot(q[t * 128 : (t + 1) * 128], k)
        top = jnp.max(s, axis=1, keepdims=True)
        w = jnp.exp((s - top) * scale)
        total = jnp.sum(w, axis=1, keepdims=True)
        o = jnp.dot(w.astype(BF), v, preferred_element_type=F32)
        outs.append((o / total).astype(BF))
        hi, mid, lo = split3(top * scale + jnp.log(total))
        parts = jnp.where(column == 0, hi, jnp.where(column == 1, mid, jnp.where(column == 2, lo, 0.0)))
        metas.append(parts.T[:META].astype(BF))

    def put(ref):
        for t in range(QROWS // 128):
            ref[t * 128 : (t + 1) * 128, :] = outs[t]
            ref[QROWS + t * META : QROWS + (t + 1) * META, :] = metas[t]

    @pl.when(pl.program_id(0) == 0)
    def _():
        put(first_ref)

    @pl.when(pl.program_id(0) == 1)
    def _():
        put(second_ref)


def prefix_pair(groups, q2, keys, values):
    shape = jax.ShapeDtypeStruct((PAYLOAD, HD), BF)
    return pl.pallas_call(
        prefix_kernel,
        grid_spec=pltpu.PrefetchScalarGridSpec(
            num_scalar_prefetch=1,
            grid=(2,),
            in_specs=[
                pl.BlockSpec((1, ROWS, GROUP * HD), lambda i, g: (i, 0, 0)),
                pl.BlockSpec((PRE, HD), lambda i, g: (0, g[i])),
                pl.BlockSpec((PRE, HD), lambda i, g: (0, g[i])),
            ],
            out_specs=[pl.BlockSpec((PAYLOAD, HD), lambda i, g: (0, 0))] * 2,
        ),
        out_shape=[shape, shape],
        compiler_params=pltpu.CompilerParams(vmem_limit_bytes=VMEM),
        cost_estimate=pl.CostEstimate(
            flops=2 * 4 * QROWS * PRE * HD, bytes_accessed=2 * 2 * 2 * PRE * HD, transcendentals=2 * QROWS * PRE
        ),
        name="prefix_pair",
    )(groups, q2, keys, values)


SUF_LEAVES = 16


def suffix_kernel(q_ref, k_ref, v_ref, nk_ref, nv_ref, len_ref, o_ref, lse_ref):
    scale = 1.0 / (HD**0.5)
    n = SUF_LEAVES * GROUP
    q = heads_as_rows(q_ref[...])
    s = nt_dot(q, k_ref[...]) * scale
    lengths = jnp.concatenate([len_ref[...][:, :1]] * GROUP, axis=0)
    row = lax.broadcasted_iota(jnp.int32, (n, 1), 0) % SUF_LEAVES
    slot = lax.broadcasted_iota(jnp.int32, s.shape, 1) - row * SUF
    s = jnp.where((slot >= 0) & (slot < lengths), s, -1e30)
    fresh_key = jnp.concatenate([nk_ref[...].astype(F32)] * GROUP, axis=0)
    fresh = jnp.sum(q.astype(F32) * fresh_key, axis=1, keepdims=True) * scale
    top = jnp.maximum(jnp.max(s, axis=1, keepdims=True), fresh)
    w = jnp.exp(s - top)
    wn = jnp.exp(fresh - top)
    total = jnp.sum(w, axis=1, keepdims=True) + wn
    o = jnp.dot(w.astype(BF), v_ref[...], preferred_element_type=F32)
    fresh_value = jnp.concatenate([nv_ref[...].astype(F32)] * GROUP, axis=0)
    o = (o + wn.astype(BF).astype(F32) * fresh_value) / total
    lse = jnp.broadcast_to(top + jnp.log(total), o.shape)
    for h in range(GROUP):
        o_ref[h] = o[h * SUF_LEAVES : (h + 1) * SUF_LEAVES]
        lse_ref[h] = lse[h * SUF_LEAVES : (h + 1) * SUF_LEAVES]


def suffix_part(q, keys, values, new_key, new_value, lengths):
    shape = jax.ShapeDtypeStruct((GROUP, ROWS, HD), F32)
    leaf = lambda w: pl.BlockSpec((SUF_LEAVES, w), lambda i: (i, 0))
    cached = pl.BlockSpec((SUF_LEAVES * SUF, HD), lambda i: (i, 0))
    return pl.pallas_call(
        suffix_kernel,
        grid=(ROWS // SUF_LEAVES,),
        in_specs=[leaf(GROUP * HD), cached, cached, leaf(HD), leaf(HD), leaf(HD)],
        out_specs=[pl.BlockSpec((GROUP, SUF_LEAVES, HD), lambda i: (0, i, 0))] * 2,
        out_shape=[shape, shape],
        compiler_params=pltpu.CompilerParams(vmem_limit_bytes=VMEM),
        cost_estimate=pl.CostEstimate(flops=4 * QROWS * 2048 * HD, bytes_accessed=4 << 20, transcendentals=QROWS * 2048),
        name="suffix_part",
    )(
        q,
        keys.reshape(ROWS * SUF, HD),
        values.reshape(ROWS * SUF, HD),
        new_key,
        new_value,
        jnp.broadcast_to(lengths[:, None], (ROWS, HD)),
    )


def merge_kernel(*refs):
    parts, (so_ref, sl_ref, out_ref, held) = refs[:8], refs[8:]
    for t in range(QROWS // 128):
        rows = []
        for p in parts:
            m = p[QROWS + t * META : QROWS + (t + 1) * META, :].astype(F32)
            rows.append(m[0:1] + m[1:2] + m[2:3])
        lse = jnp.concatenate(rows, axis=0).T
        suf_lse = sl_ref[t * 128 : (t + 1) * 128, :1]
        top = jnp.maximum(jnp.max(lse, axis=1, keepdims=True), suf_lse)
        w = jnp.exp(lse - top)
        ws = jnp.exp(suf_lse - top)
        total = jnp.sum(w, axis=1, keepdims=True) + ws
        o = so_ref[t * 128 : (t + 1) * 128, :] * ws
        for i, p in enumerate(parts):
            o = o + p[t * 128 : (t + 1) * 128, :].astype(F32) * w[:, i : i + 1]
        held[t * 128 : (t + 1) * 128, :] = (o / total).astype(BF)
    for h in range(GROUP):
        out_ref[:, h * HD : (h + 1) * HD] = held[h * ROWS : (h + 1) * ROWS, :]


def merge_parts(parts, suffix_out, suffix_lse):
    return pl.pallas_call(
        merge_kernel,
        out_shape=jax.ShapeDtypeStruct((ROWS, GROUP * HD), BF),
        scratch_shapes=[pltpu.VMEM((QROWS, HD), BF)],
        compiler_params=pltpu.CompilerParams(vmem_limit_bytes=VMEM),
        cost_estimate=pl.CostEstimate(flops=QROWS * HD * 20, bytes_accessed=2 << 20, transcendentals=QROWS * 10),
        name="merge_parts",
    )(*parts, suffix_out.reshape(QROWS, HD), suffix_lse.reshape(QROWS, HD))


def project_kernel(z_ref, a_ref, own_w_ref, other_w_ref, mine_ref, *send_refs):
    z = z_ref[0]
    pieces = [a_ref[pl.ds(pl.multiple_of((z + s) % 4 * 96, 16), 96), :] for s in range(4)]
    a = jnp.concatenate(pieces, axis=0)
    for half, w_ref in enumerate((own_w_ref, other_w_ref)):
        y = jnp.dot(a, w_ref[...], preferred_element_type=F32)
        at = slice(half * HALF, (half + 1) * HALF)
        mine_ref[:, at] = y[:96]
        for s, ref in enumerate(send_refs):
            ref[:, at] = y[(s + 1) * 96 : (s + 2) * 96].astype(BF)


def project(z, attended, own_w, other_w):
    vmem = pl.BlockSpec(memory_space=pltpu.VMEM)
    return pl.pallas_call(
        project_kernel,
        in_specs=[pl.BlockSpec(memory_space=pltpu.SMEM), vmem, vmem, vmem],
        out_specs=[vmem] * 4,
        out_shape=[jax.ShapeDtypeStruct((96, 2 * HALF), F32)] + [jax.ShapeDtypeStruct((96, 2 * HALF), BF)] * 3,
        compiler_params=pltpu.CompilerParams(vmem_limit_bytes=VMEM),
        cost_estimate=pl.CostEstimate(flops=2 * 384 * 1024 * 1024, bytes_accessed=4 << 20, transcendentals=0),
        name="project",
    )(z, attended, own_w, other_w)


def fill_kernel(place_ref, *refs):
    pieces, (gain_ref, scaled_ref, squares_ref) = refs[:4], refs[4:]
    for j, piece in enumerate(pieces):
        for e in range(2):
            at = pl.multiple_of(place_ref[j * 2 + e] * ROWS, 16)
            wide = piece[e * ROWS : (e + 1) * ROWS, :].astype(F32)
            scaled_ref[pl.ds(at, ROWS), :] = (wide * gain_ref[...]).astype(BF)
            squares_ref[pl.ds(at, ROWS), :] = jnp.broadcast_to(jnp.sum(wide * wide, axis=1, keepdims=True), (ROWS, HD))


def fill(place, pieces, gain):
    vmem = pl.BlockSpec(memory_space=pltpu.VMEM)
    return pl.pallas_call(
        fill_kernel,
        in_specs=[pl.BlockSpec(memory_space=pltpu.SMEM)] + [vmem] * 5,
        out_specs=[vmem] * 2,
        out_shape=[jax.ShapeDtypeStruct((384, 2 * HALF), BF), jax.ShapeDtypeStruct((384, HD), F32)],
        compiler_params=pltpu.CompilerParams(vmem_limit_bytes=VMEM),
        cost_estimate=pl.CostEstimate(flops=384 * 4096, bytes_accessed=2 << 20, transcendentals=0),
        name="scale_rows",
    )(place, *pieces, gain)


def hidden_sums(s_ref, weights):
    s = s_ref[...]
    out = []
    for own, other in (weights[:2], weights[2:]):
        y = jnp.dot(s[:, :HALF], own[...], preferred_element_type=F32)
        out.append(y + jnp.dot(s[:, HALF:], other[...], preferred_element_type=F32))
    return out


def x_first_kernel(s_ref, g0, g1, u0, u1, keep_ref, send_ref):
    for n, y in enumerate(hidden_sums(s_ref, (g0, g1, u0, u1))):
        for k in range(4):
            keep_ref[k, n] = y[k * ROWS : (k + 1) * ROWS]
            send_ref[k, n] = y[(4 + k) * ROWS : (5 + k) * ROWS].astype(BF)


def y_first_kernel(s_ref, g0, g1, u0, u1, here_ref, up_ref, down_ref, far_gate_ref, far_up_ref):
    for n, y in enumerate(hidden_sums(s_ref, (g0, g1, u0, u1))):
        for x in range(2):
            at = slice(x * ROWS, (x + 1) * ROWS)
            part = [y[(x * 4 + k) * ROWS : (x * 4 + k + 1) * ROWS] for k in range(4)]
            here_ref[n, at, :] = part[0]
            up_ref[n, at, :] = part[1]
            down_ref[n, at, :] = part[3]
            (far_gate_ref, far_up_ref)[n][at, :] = part[2].astype(BF)


def hidden_call(kernel, first_tile, tiles, scaled, weights, out_specs, out_shape, name):
    weight = pl.BlockSpec((HALF, TILE), lambda j: (0, j + first_tile))
    return pl.pallas_call(
        kernel,
        grid=(tiles,),
        in_specs=[pl.BlockSpec((384, 2 * HALF), lambda j: (0, 0))] + [weight] * 4,
        out_specs=out_specs,
        out_shape=out_shape,
        compiler_params=pltpu.CompilerParams(vmem_limit_bytes=VMEM),
        cost_estimate=pl.CostEstimate(
            flops=2 * 384 * 1024 * 1024 * tiles, bytes_accessed=(4 << 20) * tiles, transcendentals=0
        ),
        name=name,
    )(scaled, *weights)


def x_first(scaled, weights):
    spec = pl.BlockSpec((4, 2, ROWS, TILE), lambda j: (0, 0, 0, j))
    shape = lambda t: jax.ShapeDtypeStruct((4, 2, ROWS, A_COLS), t)
    return hidden_call(
        x_first_kernel, 0, A_COLS // TILE, scaled, weights, [spec] * 2, [shape(F32), shape(BF)], "hidden_x_first"
    )


def y_first(scaled, weights):
    both = pl.BlockSpec((2, 2 * ROWS, TILE), lambda j: (0, 0, j))
    one = pl.BlockSpec((2 * ROWS, TILE), lambda j: (0, j))
    shapes = [jax.ShapeDtypeStruct((2, 2 * ROWS, B_COLS), F32)] * 3 + [jax.ShapeDtypeStruct((2 * ROWS, B_COLS), BF)] * 2
    return hidden_call(
        y_first_kernel,
        A_COLS // TILE,
        B_COLS // TILE,
        scaled,
        weights,
        [both] * 3 + [one] * 2,
        shapes,
        "hidden_y_first",
    )


def y_sums(here, up, down, far_gate, far_up):
    from_below = over_batch(far_gate, 0, 1)
    from_above = over_batch(far_up, 0, -1)
    to_above = jnp.stack([(up[0] + from_below.astype(F32)).astype(BF), up[1].astype(BF)])
    to_below = jnp.stack([down[0].astype(BF), (down[1] + from_above.astype(F32)).astype(BF)])
    below = over_batch(to_above, 0, 1)
    above = over_batch(to_below, 0, -1)
    return here + below.astype(F32) + above.astype(F32)


def on_device(
    queries,
    new_key,
    new_value,
    prefix_keys,
    prefix_values,
    suffix_keys,
    suffix_values,
    suffix_lengths,
    out_weight,
    residual,
    norm_gain,
    gate_weight,
    up_weight,
):
    c = lax.axis_index("ctx")
    b = lax.axis_index("batch")
    xh, z = c // 4, c % 4
    xl, y, core = b // 8, b // 2 % 4, b % 2

    q_across = over_ctx(queries, 1, 0)
    suffix_out, suffix_lse = suffix_part(queries, suffix_keys, suffix_values, new_key, new_value, suffix_lengths)
    q2 = jnp.stack([queries, q_across])
    arrived = {s: over_ctx(q2, 0, s) for s in (1, 3, 2)}

    def groups(from_z):
        return jnp.stack([xh * 4 + from_z, (1 - xh) * 4 + from_z]).astype(jnp.int32)

    own, across = prefix_pair(groups(z), q2, prefix_keys, prefix_values)
    parts = [own, over_ctx(across, 1, 0)]
    for s in (1, 3, 2):
        same, other = prefix_pair(groups((z - s) % 4), arrived[s], prefix_keys, prefix_values)
        parts += [over_ctx(same, 0, -s), over_ctx(other, 1, -s)]
    attended = merge_parts(parts, suffix_out, suffix_lse)

    other_out = over_batch(out_weight, 0, 0, 1)
    other_gate = over_batch(gate_weight, 0, 0, 1)
    other_up = over_batch(up_weight, 0, 0, 1)
    blocks = residual.reshape(4, 2, 2, ROWS, HALF)
    take = lambda k: lax.dynamic_slice(blocks, (z, 0, k, 0, 0), (1, 2, 1, ROWS, HALF)).reshape(96, HALF)
    other_residual = over_batch(take(1 - core), 0, 0, 1)
    own_residual = take(core)

    everyone = lax.all_to_all(
        jnp.broadcast_to(attended[None], (8, ROWS, 1024)),
        "batch",
        0,
        0,
        axis_index_groups=[list(range(0, 16, 2)), list(range(1, 16, 2))],
        tiled=True,
    ).reshape(384, 1024)
    mine, *send = project(z.astype(jnp.int32).reshape(1), everyone, out_weight, other_out)
    for s in (1, 3, 2):
        mine = mine + over_ctx(send[s - 1], 0, s).astype(F32)
    mine = mine.astype(BF)
    across = over_ctx(mine, 1, 0)
    mixed = mine.astype(F32) + across.astype(F32)
    chunk = (jnp.concatenate([own_residual, other_residual], axis=1).astype(F32) + mixed).astype(BF)
    pieces = [chunk] + [over_ctx(chunk, 0, s) for s in (1, 3, 2)]
    piece_z = [z, (z - 1) % 4, (z - 3) % 4, (z - 2) % 4]

    place = []
    for pz in piece_z:
        for e in range(2):
            block = 2 * pz + e
            place.append((block // 4 - xl) % 2 * 4 + (block % 4 - y) % 4)
    gain = jnp.concatenate([norm_gain, over_batch(norm_gain, 0, 0, 1)]).astype(F32).reshape(1, 2 * HALF)
    scaled, squares = fill(jnp.stack(place).astype(jnp.int32), pieces, gain)
    weights = (gate_weight, other_gate, up_weight, other_up)
    keep, send = x_first(scaled, weights)
    here, up, down, far_gate, far_up = y_first(scaled, weights)

    got = over_batch(send, 1, 0)
    total = lambda k: keep[k] + got[k].astype(F32)
    far = total(2).astype(BF)
    a_sums = y_sums(total(0), total(1), total(3), far[0], far[1])
    b_sums = y_sums(here, up, down, far_gate, far_up)
    b_sums = b_sums[:, :ROWS] + over_batch(b_sums[:, ROWS:].astype(BF), 1, 0).astype(F32)

    squares = squares[:, 0].reshape(2, 4, ROWS)
    squares = squares[0] + over_batch(squares[1], 1, 0)
    square_sums = squares[0]
    for s in (1, 2, 3):
        square_sums = square_sums + over_batch(squares[s], 0, s)
    rms = jnp.sqrt(square_sums / D + 1e-05)[:, None]

    def activate(sums):
        return (jax.nn.silu(sums[0] / rms) * (sums[1] / rms)).astype(BF)

    activation = jnp.concatenate([activate(a_sums), activate(b_sums)], axis=1)

    theirs = [over_batch(jnp.concatenate([p[:, HALF:] for p in pieces]), 0, 0, 1)]
    ordered = jnp.stack(
        [jnp.concatenate([p[:, :HALF] for p in pieces]).reshape(4, 2, ROWS, HALF), theirs[0].reshape(4, 2, ROWS, HALF)]
    )
    ordered = jnp.where(core == 0, ordered, ordered[::-1])
    stream = jnp.zeros((4, 2, 2, ROWS, HALF), BF)
    for j, pz in enumerate(piece_z):
        stream = lax.dynamic_update_slice(stream, ordered[:, j].transpose(1, 0, 2, 3)[None], (pz, 0, 0, 0, 0))
    return (stream.reshape(768, HALF), activation)


def solution(mesh):
    in_specs = (
        P("batch", "ctx"),
        P("batch", "ctx"),
        P("batch", "ctx"),
        P("ctx", None),
        P("ctx", None),
        P("batch", None, "ctx"),
        P("batch", None, "ctx"),
        P("batch"),
        P("ctx", "batch"),
        P(None, "batch"),
        P("batch"),
        P("batch", "ctx"),
        P("batch", "ctx"),
    )
    out_specs = (P(None, "batch"), P("batch", "ctx"))
    return jax.shard_map(
        on_device, mesh=mesh, in_specs=in_specs, out_specs=out_specs, check_vma=False
    )
```

time: 537 us -> 175 us (0.33)
  waiting for transfers between devices: 344 us -> 62.9 us
  blocking collectives: 109 us -> 0 us
  starting transfers between devices: 0.39 us -> 59 us
  Pallas kernels: 0 us -> 41.6 us
  matrix products: 37 us -> 0 us
  other arithmetic: 24.3 us -> 4 us
  between operations: 14 us -> 1.47 us
    reduce_scatter x3 -> x0, waiting for transfers between devices: 221 us -> none  [the longest x1 95.3 us: on_device(): lax.psum_scatter(jnp.concatenate([jnp.dot(scaled, gate_weight, preferred_...]
    psum x1 -> x0, waiting for transfers between devices: 90.4 us -> none  [on_device(): mixed = lax.psum(partial_sums, 'ctx')]
    ppermute x0 -> x38, starting transfers between devices: none -> 54.5 us  [the longest x18 33 us: over_ctx(): return lax.ppermute(v, 'ctx', ctx_perm(flip, s))]
    ppermute x0 -> x38, waiting for transfers between devices: none -> 53.4 us  [the longest x20 31 us: over_batch(): return lax.ppermute(v, 'batch', batch_perm(flip_x, s, flip_core))]
    pmax x1 -> x0, blocking collectives: 44.2 us -> none  [on_device(): highest = lax.pmax(local_max, 'ctx')]
    pallas_call x0 -> x10, Pallas kernels: none -> 41.6 us  [the longest x4 21.8 us: prefix_pair(): pl.pallas_call(prefix_kernel, grid_spec=pltpu.PrefetchScalarGridSpec(num_...]
    dot_general x8 -> x0, matrix products: 37 us -> none  [the longest x1 11.6 us: on_device(): jnp.einsum('klgp,pkd->klgd', local_w.astype(jnp.bfloat16), values_here, p...]
    all_gather x1 -> x0, blocking collectives: 37 us -> none  [on_device(): query_everywhere = lax.all_gather(queries, 'ctx', axis=1, tiled=True)]
  transfers between devices with their start and end apart: 5 -> 39, of which waited for: 5 -> 21; matrix products, arithmetic and copies ran while one was open for 3% -> 3% of each run, Pallas kernels for 0% -> 19%
where the time goes in v1:
time: 175 us; the launch traced here: 174 us
  waiting for transfers between devices  62.9 us (36%)
  starting transfers between devices  59 us (34%)
  Pallas kernels  41.6 us (24%)
  local copies, waits for them, and re-layouts  5.11 us (3%)
  other arithmetic  4 us (2%)
    ppermute x18, starting transfers between devices, over_ctx(): return lax.ppermute(v, 'ctx', ctx_perm(flip, s))  33 us
    ppermute x20, waiting for transfers between devices, over_batch(): return lax.ppermute(v, 'batch', batch_perm(flip_x, s, flip_core))  31 us
    ppermute x18, waiting for transfers between devices, over_ctx(): return lax.ppermute(v, 'ctx', ctx_perm(flip, s))  22.4 us
    pallas_call x4, Pallas kernels, prefix_pair(): pl.pallas_call(prefix_kernel, grid_spec=pltpu.PrefetchScalarGridSpec(num_...  21.8 us
    ppermute x20, starting transfers between devices, over_batch(): return lax.ppermute(v, 'batch', batch_perm(flip_x, s, flip_core))  21.5 us
    pallas_call x2, Pallas kernels, hidden_call(): pl.pallas_call(kernel, grid=(tiles,), in_specs=[pl.BlockSpec((384, 2 * HA...  12.8 us
    all_to_all x1, waiting for transfers between devices, on_device(): lax.all_to_all(jnp.broadcast_to(attended[None], (8, ROWS, 1024)), 'batch'...  9.47 us
    all_to_all x1, starting transfers between devices, on_device(): lax.all_to_all(jnp.broadcast_to(attended[None], (8, ROWS, 1024)), 'batch'...  4.5 us
  transfers between devices with their start and end apart: 39, of which 21 were waited for; matrix products, arithmetic and copies ran while one was open for 3% of the time, Pallas kernels for 19%

profile of v1, /device:TPU:0, one launch (start us, length us, event | category | flops | bytes accessed | tf_op | source)
XLA Modules:
  0.0 174.0 jit_solution(7854585660551131159)
XLA Ops:
  0.6 3.2 %collective-permute-start.1 = (bf16[48,1024]{1,0:T(8,128)(2,1)}, bf16[48,1024]{1,0:T(8,128)(2,1)S(1)}, u32[]{:S(2)}, u32[]{:S(2)}) collective-permute-start(bf16[48,1024]{1,0:T(8,128)(2,1)} %q_ref.1), channel_id=1, source_target_pairs={{0,64},{16,80},{32,96},{48,112},{64,0},{80,16},{96,32},{112,48},{1... | collective-permute-start | bytes 294920 | tf_op jit(solution)/shard_map/ppermute | solution.py:42
  4.0 3.1 %collective-permute-done.1 = bf16[48,1024]{1,0:T(8,128)(2,1)S(1)} collective-permute-done((bf16[48,1024]{1,0:T(8,128)(2,1)}, bf16[48,1024]{1,0:T(8,128)(2,1)S(1)}, u32[]{:S(2)}, u32[]{:S(2)}) %collective-permute-start.1) | collective-permute-done | bytes 98336 | tf_op jit(solution)/shard_map/ppermute | solution.py:42
  8.0 4.0 %collective-permute-start.9 = (bf16[2,48,1024]{2,1,0:T(8,128)(2,1)S(1)}, bf16[2,48,1024]{2,1,0:T(8,128)(2,1)S(1)}, u32[]{:S(2)}, u32[]{:S(2)}) collective-permute-start(bf16[2,48,1024]{2,1,0:T(8,128)(2,1)S(1)} %pad_maximum_fusion.8.q_ref), channel_id=1, source_target_pairs={{0,32},{16,48},{32,0},{48,16},{64,96},{80,112},{96,64},{112,80},{1... | collective-permute-start | bytes 589832 | tf_op jit(solution)/shard_map/ppermute | solution.py:42
  16.4 5.7 %prefix_pair.4 = (bf16[432,128]{1,0:T(8,128)(2,1)S(1)}, bf16[432,128]{1,0:T(8,128)(2,1)S(1)}) custom-call(s32[2]{0:T(128)S(1)} %pad_add_fusion.group_ref, bf16[2,48,1024]{2,1,0:T(8,128)(2,1)S(1)} %pad_maximum_fusion.8.q_ref, bf16[2048,1024]{1,0:T(8,128)(2,1)S(1)} %copy-done, bf16[2048,1024]{1,0:T(8,128)(2,1)} %v_ref.7), custom_call_target="tpu_custom_call" | custom-call | flops 805306368 | bytes 2097152 | tf_op jit(solution)/shard_map/prefix_pair/pallas_call | solution.py:98
  22.1 3.1 %collective-permute-start.2 = (bf16[432,128]{1,0:T(8,128)(2,1)S(1)}, bf16[432,128]{1,0:T(8,128)(2,1)S(1)}, u32[]{:S(2)}, u32[]{:S(2)}) collective-permute-start(bf16[432,128]{1,0:T(8,128)(2,1)S(1)} %get-tuple-element.26), channel_id=1, source_target_pairs={{0,64},{16,80},{32,96},{48,112},{64,0},{80,16},{96,32},{112,48},{1... | collective-permute-start | bytes 331784 | tf_op jit(solution)/shard_map/ppermute | solution.py:42
  25.2 5.4 %prefix_pair.7 = (bf16[432,128]{1,0:T(8,128)(2,1)S(1)}, bf16[432,128]{1,0:T(8,128)(2,1)S(1)}) custom-call(s32[2]{0:T(128)S(1)} %pad_add_fusion.3.group_ref, bf16[2,48,1024]{2,1,0:T(8,128)(2,1)S(1)} %collective-permute-done.9.q_ref, bf16[2048,1024]{1,0:T(8,128)(2,1)S(1)} %copy-done.1, bf16[2048,1024]{1,0:T(8,128)(2,1)} %v_ref.7), custom_call_target="tpu_custom_call" | custom-call | flops 805306368 | bytes 2097152 | tf_op jit(solution)/shard_map/prefix_pair/pallas_call | solution.py:98
  34.1 5.4 %prefix_pair.6 = (bf16[432,128]{1,0:T(8,128)(2,1)S(1)}, bf16[432,128]{1,0:T(8,128)(2,1)S(1)}) custom-call(s32[2]{0:T(128)S(1)} %pad_add_fusion.2.group_ref, bf16[2,48,1024]{2,1,0:T(8,128)(2,1)S(1)} %collective-permute-done.6.q_ref, bf16[2048,1024]{1,0:T(8,128)(2,1)S(1)} %copy-done.1, bf16[2048,1024]{1,0:T(8,128)(2,1)} %v_ref.7), custom_call_target="tpu_custom_call" | custom-call | flops 805306368 | bytes 2097152 | tf_op jit(solution)/shard_map/prefix_pair/pallas_call | solution.py:98
  40.7 5.4 %prefix_pair.5 = (bf16[432,128]{1,0:T(8,128)(2,1)S(1)}, bf16[432,128]{1,0:T(8,128)(2,1)S(1)}) custom-call(s32[2]{0:T(128)S(1)} %pad_add_fusion.1.group_ref, bf16[2,48,1024]{2,1,0:T(8,128)(2,1)S(1)} %collective-permute-done.3.q_ref, bf16[2048,1024]{1,0:T(8,128)(2,1)S(1)} %copy-done.1, bf16[2048,1024]{1,0:T(8,128)(2,1)} %v_ref.7), custom_call_target="tpu_custom_call" | custom-call | flops 805306368 | bytes 2097152 | tf_op jit(solution)/shard_map/prefix_pair/pallas_call | solution.py:98
  48.8 3.0 %collective-permute-start.4 = (bf16[432,128]{1,0:T(8,128)(2,1)S(1)}, bf16[432,128]{1,0:T(8,128)(2,1)S(1)}, u32[]{:S(2)}, u32[]{:S(2)}) collective-permute-start(bf16[432,128]{1,0:T(8,128)(2,1)S(1)} %get-tuple-element.27), channel_id=1, source_target_pairs={{0,48},{16,0},{32,16},{48,32},{64,112},{80,64},{96,80},{112,96},{1... | collective-permute-start | bytes 331784 | tf_op jit(solution)/shard_map/ppermute | solution.py:42
  55.6 3.4 %collective-permute-done.5.refs_3_ = bf16[432,128]{1,0:T(8,128)(2,1)S(1)} collective-permute-done((bf16[432,128]{1,0:T(8,128)(2,1)S(1)}, bf16[432,128]{1,0:T(8,128)(2,1)S(1)}, u32[]{:S(2)}, u32[]{:S(2)}) %collective-permute-start.5) | collective-permute-done | bytes 110624 | tf_op jit(solution)/shard_map/ppermute | solution.py:42
  61.7 4.5 %all-to-all-start = ((bf16[8,48,1024]{2,1,0:T(8,128)(2,1)}), bf16[8,48,1024]{2,1,0:T(8,128)(2,1)S(1)}, u32[]{:S(2)}, u32[]{:S(2)}) async-start(bf16[8,48,1024]{2,1,0:T(8,128)(2,1)} %broadcast_in_dim.30), calls=%async_computation | async-start | bytes 1572864 | tf_op jit(solution)/shard_map/all_to_all | solution.py:369
  66.2 9.5 %all-to-all-done = bf16[8,48,1024]{2,1,0:T(8,128)(2,1)S(1)} async-done(((bf16[8,48,1024]{2,1,0:T(8,128)(2,1)}), bf16[8,48,1024]{2,1,0:T(8,128)(2,1)S(1)}, u32[]{:S(2)}, u32[]{:S(2)}) %all-to-all-start) | async-done | bytes 786464 | tf_op jit(solution)/shard_map/all_to_all | solution.py:369
  77.4 3.2 %collective-permute-start.14 = (bf16[96,1024]{1,0:T(8,128)(2,1)}, bf16[96,1024]{1,0:T(8,128)(2,1)S(1)}, u32[]{:S(2)}, u32[]{:S(2)}) collective-permute-start(bf16[96,1024]{1,0:T(8,128)(2,1)} %get-tuple-element.37), channel_id=1, source_target_pairs={{0,48},{16,0},{32,16},{48,32},{64,112},{80,64},{96,80},{112,96},{1... | collective-permute-start | bytes 589832 | tf_op jit(solution)/shard_map/ppermute | solution.py:42
  81.5 2.9 %collective-permute-done.13 = bf16[96,1024]{1,0:T(8,128)(2,1)S(1)} collective-permute-done((bf16[96,1024]{1,0:T(8,128)(2,1)}, bf16[96,1024]{1,0:T(8,128)(2,1)S(1)}, u32[]{:S(2)}, u32[]{:S(2)}) %collective-permute-start.13) | collective-permute-done | bytes 196640 | tf_op jit(solution)/shard_map/ppermute | solution.py:42
  98.8 5.4 %collective-permute-done.17.refs_1_ = bf16[96,1024]{1,0:T(8,128)(2,1)S(1)} collective-permute-done((bf16[96,1024]{1,0:T(8,128)(2,1)S(1)}, bf16[96,1024]{1,0:T(8,128)(2,1)S(1)}, u32[]{:S(2)}, u32[]{:S(2)}) %collective-permute-start.17) | collective-permute-done | bytes 196640 | tf_op jit(solution)/shard_map/ppermute | solution.py:42
  119.8 7.3 %hidden_y_first.1 = (f32[2,96,2048]{2,1,0:T(8,128)S(1)}, f32[2,96,2048]{2,1,0:T(8,128)S(1)}, f32[2,96,2048]{2,1,0:T(8,128)}, bf16[96,2048]{1,0:T(8,128)(2,1)S(1)}, bf16[96,2048]{1,0:T(8,128)(2,1)S(1)}) custom-call(bf16[384,1024]{1,0:T(8,128)(2,1)S(1)} %get-tuple-element.39.s_ref, bf16[512,3584]{1,0:T(8,128)(2,1)} %g0.3, ...), custom_call_target="tpu_custom_call" | custom-call | flops 3221225472 | bytes 16777216 | tf_op jit(solution)/shard_map/hidden_y_first/pallas_call | solution.py:278
  127.2 5.5 %hidden_x_first.1 = (f32[4,2,48,1536]{3,2,1,0:T(8,128)S(1)}, bf16[4,2,48,1536]{3,2,1,0:T(8,128)(2,1)S(1)}) custom-call(bf16[384,1024]{1,0:T(8,128)(2,1)S(1)} %get-tuple-element.39.s_ref, bf16[512,3584]{1,0:T(8,128)(2,1)} %g0.3, bf16[512,3584]{1,0:T(8,128)(2,1)} %collective-permute-done.22.g1, bf16[512,3584]{1,0:T(8,128)(2,1)} %u0.3, ...), custom_call_target="tpu_custom_call" | custom-call | flops 2415919104 | bytes 12582912 | tf_op jit(solution)/shard_map/hidden_x_first/pallas_call | solution.py:278
  134.0 3.5 %collective-permute-start.35 = (bf16[96,2048]{1,0:T(8,128)(2,1)S(1)}, bf16[96,2048]{1,0:T(8,128)(2,1)S(1)}, u32[]{:S(2)}, u32[]{:S(2)}) collective-permute-start(bf16[96,2048]{1,0:T(8,128)(2,1)S(1)} %get-tuple-element.47), channel_id=1, source_target_pairs={{0,6},{1,7},{2,0},{3,1},{4,2},{5,3},{6,4},{7,5},{8,14},{9,15},{10,... | collective-permute-start | bytes 1179656 | tf_op jit(solution)/shard_map/ppermute | solution.py:46
  137.8 6.9 %collective-permute-done.35 = bf16[96,2048]{1,0:T(8,128)(2,1)S(1)} collective-permute-done((bf16[96,2048]{1,0:T(8,128)(2,1)S(1)}, bf16[96,2048]{1,0:T(8,128)(2,1)S(1)}, u32[]{:S(2)}, u32[]{:S(2)}) %collective-permute-start.35) | collective-permute-done | bytes 393248 | tf_op jit(solution)/shard_map/ppermute | solution.py:46
  144.9 3.8 %collective-permute-start.36 = (bf16[2,96,2048]{2,1,0:T(8,128)(2,1)S(1)}, bf16[2,96,2048]{2,1,0:T(8,128)(2,1)S(1)}, u32[]{:S(2)}, u32[]{:S(2)}) collective-permute-start(bf16[2,96,2048]{2,1,0:T(8,128)(2,1)S(1)} %pad_maximum_fusion.2), channel_id=1, source_target_pairs={{0,6},{1,7},{2,0},{3,1},{4,2},{5,3},{6,4},{7,5},{8,14},{9,15},{10,... | collective-permute-start | bytes 2359304 | tf_op jit(solution)/shard_map/ppermute | solution.py:46
  148.7 8.0 %collective-permute-done.24 = bf16[4,2,48,1536]{3,2,1,0:T(8,128)(2,1)S(1)} collective-permute-done((bf16[4,2,48,1536]{3,2,1,0:T(8,128)(2,1)S(1)}, bf16[4,2,48,1536]{3,2,1,0:T(8,128)(2,1)S(1)}, u32[]{:S(2)}, u32[]{:S(2)}) %collective-permute-start.24) | collective-permute-done | bytes 1179680 | tf_op jit(solution)/shard_map/ppermute | solution.py:46
  157.2 3.0 %collective-permute-start.27 = (bf16[48,1536]{1,0:T(8,128)(2,1)S(1)}, bf16[48,1536]{1,0:T(8,128)(2,1)S(1)}, u32[]{:S(2)}, u32[]{:S(2)}) collective-permute-start(bf16[48,1536]{1,0:T(8,128)(2,1)S(1)} %get-tuple-element.60), channel_id=1, source_target_pairs={{0,6},{1,7},{2,0},{3,1},{4,2},{5,3},{6,4},{7,5},{8,14},{9,15},{10,... | collective-permute-start | bytes 442376 | tf_op jit(solution)/shard_map/ppermute | solution.py:46
  165.1 3.3 %collective-permute-start.28 = (bf16[2,48,1536]{2,1,0:T(8,128)(2,1)S(1)}, bf16[2,48,1536]{2,1,0:T(8,128)(2,1)S(1)}, u32[]{:S(2)}, u32[]{:S(2)}) collective-permute-start(bf16[2,48,1536]{2,1,0:T(8,128)(2,1)S(1)} %pad_maximum_fusion.7), channel_id=1, source_target_pairs={{0,6},{1,7},{2,0},{3,1},{4,2},{5,3},{6,4},{7,5},{8,14},{9,15},{10,... | collective-permute-start | bytes 884744 | tf_op jit(solution)/shard_map/ppermute | solution.py:46
  169.8 3.1 %collective-permute-done.26 = bf16[2,48,1536]{2,1,0:T(8,128)(2,1)S(1)} collective-permute-done((bf16[2,48,1536]{2,1,0:T(8,128)(2,1)S(1)}, bf16[2,48,1536]{2,1,0:T(8,128)(2,1)S(1)}, u32[]{:S(2)}, u32[]{:S(2)}) %collective-permute-start.26) | collective-permute-done | bytes 294944 | tf_op jit(solution)/shard_map/ppermute | solution.py:46
  (143 shorter events, 61.0 us)
Async XLA Ops:
  3.8 62.4 %collective-permute-start.12 = (bf16[1024,512]{1,0:T(8,128)(2,1)}, bf16[1024,512]{1,0:T(8,128)(2,1)S(1)}, u32[]{:S(2)}, u32[]{:S(2)}) collective-permute-start(bf16[1024,512]{1,0:T(8,128)(2,1)} %own_w_ref.1), channel_id=1, source_target_pairs={{0,1},{1,0},{2,3},{3,2},{4,5},{5,4},{6,7},{7,6},{8,9},{9,8},{10,11... | collective-permute-start | bytes 3145736 | tf_op jit(solution)/shard_map/ppermute | solution.py:46
  8.0 17.2 %collective-permute-start.9 = (bf16[2,48,1024]{2,1,0:T(8,128)(2,1)S(1)}, bf16[2,48,1024]{2,1,0:T(8,128)(2,1)S(1)}, u32[]{:S(2)}, u32[]{:S(2)}) collective-permute-start(bf16[2,48,1024]{2,1,0:T(8,128)(2,1)S(1)} %pad_maximum_fusion.8.q_ref), channel_id=1, source_target_pairs={{0,32},{16,48},{32,0},{48,16},{64,96},{80,112},{96,64},{112,80},{1... | collective-permute-start | bytes 589832 | tf_op jit(solution)/shard_map/ppermute | solution.py:42
  12.1 19.7 %collective-permute-start.6 = (bf16[2,48,1024]{2,1,0:T(8,128)(2,1)S(1)}, bf16[2,48,1024]{2,1,0:T(8,128)(2,1)S(1)}, u32[]{:S(2)}, u32[]{:S(2)}) collective-permute-start(bf16[2,48,1024]{2,1,0:T(8,128)(2,1)S(1)} %pad_maximum_fusion.8.q_ref), channel_id=1, source_target_pairs={{0,48},{16,0},{32,16},{48,32},{64,112},{80,64},{96,80},{112,96},{1... | collective-permute-start | bytes 589832 | tf_op jit(solution)/shard_map/ppermute | solution.py:42
  12.9 26.6 %collective-permute-start.3 = (bf16[2,48,1024]{2,1,0:T(8,128)(2,1)S(1)}, bf16[2,48,1024]{2,1,0:T(8,128)(2,1)S(1)}, u32[]{:S(2)}, u32[]{:S(2)}) collective-permute-start(bf16[2,48,1024]{2,1,0:T(8,128)(2,1)S(1)} %pad_maximum_fusion.8.q_ref), channel_id=1, source_target_pairs={{0,16},{16,32},{32,48},{48,0},{64,80},{80,96},{96,112},{112,64},{1... | collective-permute-start | bytes 589832 | tf_op jit(solution)/shard_map/ppermute | solution.py:42
  22.1 24.0 %collective-permute-start.2 = (bf16[432,128]{1,0:T(8,128)(2,1)S(1)}, bf16[432,128]{1,0:T(8,128)(2,1)S(1)}, u32[]{:S(2)}, u32[]{:S(2)}) collective-permute-start(bf16[432,128]{1,0:T(8,128)(2,1)S(1)} %get-tuple-element.26), channel_id=1, source_target_pairs={{0,64},{16,80},{32,96},{48,112},{64,0},{80,16},{96,32},{112,48},{1... | collective-permute-start | bytes 331784 | tf_op jit(solution)/shard_map/ppermute | solution.py:42
  30.6 18.2 %collective-permute-start.10 = (bf16[432,128]{1,0:T(8,128)(2,1)S(1)}, bf16[432,128]{1,0:T(8,128)(2,1)S(1)}, u32[]{:S(2)}, u32[]{:S(2)}) collective-permute-start(bf16[432,128]{1,0:T(8,128)(2,1)S(1)} %get-tuple-element.31), channel_id=1, source_target_pairs={{0,32},{16,48},{32,0},{48,16},{64,96},{80,112},{96,64},{112,80},{1... | collective-permute-start | bytes 331784 | tf_op jit(solution)/shard_map/ppermute | solution.py:42
  31.7 20.1 %collective-permute-start.11 = (bf16[432,128]{1,0:T(8,128)(2,1)S(1)}, bf16[432,128]{1,0:T(8,128)(2,1)S(1)}, u32[]{:S(2)}, u32[]{:S(2)}) collective-permute-start(bf16[432,128]{1,0:T(8,128)(2,1)S(1)} %get-tuple-element.32), channel_id=1, source_target_pairs={{0,96},{16,112},{32,64},{48,80},{64,32},{80,48},{96,0},{112,16},{1... | collective-permute-start | bytes 331784 | tf_op jit(solution)/shard_map/ppermute | solution.py:42
  39.6 16.0 %collective-permute-start.7 = (bf16[432,128]{1,0:T(8,128)(2,1)S(1)}, bf16[432,128]{1,0:T(8,128)(2,1)S(1)}, u32[]{:S(2)}, u32[]{:S(2)}) collective-permute-start(bf16[432,128]{1,0:T(8,128)(2,1)S(1)} %get-tuple-element.29), channel_id=1, source_target_pairs={{0,16},{16,32},{32,48},{48,0},{64,80},{80,96},{96,112},{112,64},{1... | collective-permute-start | bytes 331784 | tf_op jit(solution)/shard_map/ppermute | solution.py:42
  46.0 9.5 %collective-permute-start.8 = (bf16[432,128]{1,0:T(8,128)(2,1)S(1)}, bf16[432,128]{1,0:T(8,128)(2,1)S(1)}, u32[]{:S(2)}, u32[]{:S(2)}) collective-permute-start(bf16[432,128]{1,0:T(8,128)(2,1)S(1)} %get-tuple-element.30), channel_id=1, source_target_pairs={{0,80},{16,96},{32,112},{48,64},{64,16},{80,32},{96,48},{112,0},{1... | collective-permute-start | bytes 331784 | tf_op jit(solution)/shard_map/ppermute | solution.py:42
  61.7 14.0 %all-to-all-start = ((bf16[8,48,1024]{2,1,0:T(8,128)(2,1)}), bf16[8,48,1024]{2,1,0:T(8,128)(2,1)S(1)}, u32[]{:S(2)}, u32[]{:S(2)}) async-start(bf16[8,48,1024]{2,1,0:T(8,128)(2,1)} %broadcast_in_dim.30), calls=%async_computation | async-start | bytes 1572864 | tf_op jit(solution)/shard_map/all_to_all | solution.py:369
  77.4 8.9 %collective-permute-start.14 = (bf16[96,1024]{1,0:T(8,128)(2,1)}, bf16[96,1024]{1,0:T(8,128)(2,1)S(1)}, u32[]{:S(2)}, u32[]{:S(2)}) collective-permute-start(bf16[96,1024]{1,0:T(8,128)(2,1)} %get-tuple-element.37), channel_id=1, source_target_pairs={{0,48},{16,0},{32,16},{48,32},{64,112},{80,64},{96,80},{112,96},{1... | collective-permute-start | bytes 589832 | tf_op jit(solution)/shard_map/ppermute | solution.py:42
  81.0 38.8 %collective-permute-start.22 = (bf16[512,3584]{1,0:T(8,128)(2,1)}, bf16[512,3584]{1,0:T(8,128)(2,1)}, u32[]{:S(2)}, u32[]{:S(2)}) collective-permute-start(bf16[512,3584]{1,0:T(8,128)(2,1)} %g0.3), channel_id=1, source_target_pairs={{0,1},{1,0},{2,3},{3,2},{4,5},{5,4},{6,7},{7,6},{8,9},{9,8},{10,11... | collective-permute-start | bytes 11010056 | tf_op jit(solution)/shard_map/ppermute | solution.py:46
  81.0 38.8 %collective-permute-start.23 = (bf16[512,3584]{1,0:T(8,128)(2,1)}, bf16[512,3584]{1,0:T(8,128)(2,1)}, u32[]{:S(2)}, u32[]{:S(2)}) collective-permute-start(bf16[512,3584]{1,0:T(8,128)(2,1)} %u0.3), channel_id=1, source_target_pairs={{0,1},{1,0},{2,3},{3,2},{4,5},{5,4},{6,7},{7,6},{8,9},{9,8},{10,11... | collective-permute-start | bytes 11010056 | tf_op jit(solution)/shard_map/ppermute | solution.py:46
  95.2 8.9 %collective-permute-start.17 = (bf16[96,1024]{1,0:T(8,128)(2,1)S(1)}, bf16[96,1024]{1,0:T(8,128)(2,1)S(1)}, u32[]{:S(2)}, u32[]{:S(2)}) collective-permute-start(bf16[96,1024]{1,0:T(8,128)(2,1)S(1)} %add_convert_fusion.1.refs_0_), channel_id=1, source_target_pairs={{0,16},{16,32},{32,48},{48,0},{64,80},{80,96},{96,112},{112,64},{1... | collective-permute-start | bytes 589832 | tf_op jit(solution)/shard_map/ppermute | solution.py:42
  95.9 9.0 %collective-permute-start.18 = (bf16[96,1024]{1,0:T(8,128)(2,1)S(1)}, bf16[96,1024]{1,0:T(8,128)(2,1)S(1)}, u32[]{:S(2)}, u32[]{:S(2)}) collective-permute-start(bf16[96,1024]{1,0:T(8,128)(2,1)S(1)} %add_convert_fusion.1.refs_0_), channel_id=1, source_target_pairs={{0,48},{16,0},{32,16},{48,32},{64,112},{80,64},{96,80},{112,96},{1... | collective-permute-start | bytes 589832 | tf_op jit(solution)/shard_map/ppermute | solution.py:42
  108.7 10.6 %collective-permute-start.20 = (bf16[384,512]{1,0:T(8,128)(2,1)S(1)}, bf16[384,512]{1,0:T(8,128)(2,1)S(1)}, u32[]{:S(2)}, u32[]{:S(2)}) collective-permute-start(bf16[384,512]{1,0:T(8,128)(2,1)S(1)} %pad_maximum_fusion.4), channel_id=1, source_target_pairs={{0,1},{1,0},{2,3},{3,2},{4,5},{5,4},{6,7},{7,6},{8,9},{9,8},{10,11... | collective-permute-start | bytes 1179656 | tf_op jit(solution)/shard_map/ppermute | solution.py:46
  127.1 10.4 %collective-permute-start.33 = (bf16[96,2048]{1,0:T(8,128)(2,1)S(1)}, bf16[96,2048]{1,0:T(8,128)(2,1)S(1)}, u32[]{:S(2)}, u32[]{:S(2)}) collective-permute-start(bf16[96,2048]{1,0:T(8,128)(2,1)S(1)} %get-tuple-element.45), channel_id=1, source_target_pairs={{0,2},{1,3},{2,4},{3,5},{4,6},{5,7},{6,0},{7,1},{8,10},{9,11},{10,... | collective-permute-start | bytes 1179656 | tf_op jit(solution)/shard_map/ppermute | solution.py:46
  132.7 24.0 %collective-permute-start.24 = (bf16[4,2,48,1536]{3,2,1,0:T(8,128)(2,1)S(1)}, bf16[4,2,48,1536]{3,2,1,0:T(8,128)(2,1)S(1)}, u32[]{:S(2)}, u32[]{:S(2)}) collective-permute-start(bf16[4,2,48,1536]{3,2,1,0:T(8,128)(2,1)S(1)} %get-tuple-element.41), channel_id=1, source_target_pairs={{0,8},{1,9},{2,10},{3,11},{4,12},{5,13},{6,14},{7,15},{8,0},{9,1},... | collective-permute-start | bytes 3538952 | tf_op jit(solution)/shard_map/ppermute | solution.py:46
  134.0 10.7 %collective-permute-start.35 = (bf16[96,2048]{1,0:T(8,128)(2,1)S(1)}, bf16[96,2048]{1,0:T(8,128)(2,1)S(1)}, u32[]{:S(2)}, u32[]{:S(2)}) collective-permute-start(bf16[96,2048]{1,0:T(8,128)(2,1)S(1)} %get-tuple-element.47), channel_id=1, source_target_pairs={{0,6},{1,7},{2,0},{3,1},{4,2},{5,3},{6,4},{7,5},{8,14},{9,15},{10,... | collective-permute-start | bytes 1179656 | tf_op jit(solution)/shard_map/ppermute | solution.py:46
  137.7 22.5 %collective-permute-start.34 = (bf16[2,96,2048]{2,1,0:T(8,128)(2,1)S(1)}, bf16[2,96,2048]{2,1,0:T(8,128)(2,1)S(1)}, u32[]{:S(2)}, u32[]{:S(2)}) collective-permute-start(bf16[2,96,2048]{2,1,0:T(8,128)(2,1)S(1)} %pad_maximum_fusion.1), channel_id=1, source_target_pairs={{0,2},{1,3},{2,4},{3,5},{4,6},{5,7},{6,0},{7,1},{8,10},{9,11},{10,... | collective-permute-start | bytes 2359304 | tf_op jit(solution)/shard_map/ppermute | solution.py:46
  144.9 16.3 %collective-permute-start.36 = (bf16[2,96,2048]{2,1,0:T(8,128)(2,1)S(1)}, bf16[2,96,2048]{2,1,0:T(8,128)(2,1)S(1)}, u32[]{:S(2)}, u32[]{:S(2)}) collective-permute-start(bf16[2,96,2048]{2,1,0:T(8,128)(2,1)S(1)} %pad_maximum_fusion.2), channel_id=1, source_target_pairs={{0,6},{1,7},{2,0},{3,1},{4,2},{5,3},{6,4},{7,5},{8,14},{9,15},{10,... | collective-permute-start | bytes 2359304 | tf_op jit(solution)/shard_map/ppermute | solution.py:46
  156.9 7.9 %collective-permute-start.25 = (bf16[48,1536]{1,0:T(8,128)(2,1)S(1)}, bf16[48,1536]{1,0:T(8,128)(2,1)S(1)}, u32[]{:S(2)}, u32[]{:S(2)}) collective-permute-start(bf16[48,1536]{1,0:T(8,128)(2,1)S(1)} %get-tuple-element.59), channel_id=1, source_target_pairs={{0,2},{1,3},{2,4},{3,5},{4,6},{5,7},{6,0},{7,1},{8,10},{9,11},{10,... | collective-permute-start | bytes 442376 | tf_op jit(solution)/shard_map/ppermute | solution.py:46
  161.6 7.9 %collective-permute-start.37 = (bf16[2,48,2048]{2,1,0:T(8,128)(2,1)S(1)}, bf16[2,48,2048]{2,1,0:T(8,128)(2,1)S(1)}, u32[]{:S(2)}, u32[]{:S(2)}) collective-permute-start(bf16[2,48,2048]{2,1,0:T(8,128)(2,1)S(1)} %slice.290), channel_id=1, source_target_pairs={{0,8},{1,9},{2,10},{3,11},{4,12},{5,13},{6,14},{7,15},{8,0},{9,1},... | collective-permute-start | bytes 1179656 | tf_op jit(solution)/shard_map/ppermute | solution.py:46
  164.9 8.0 %collective-permute-start.26 = (bf16[2,48,1536]{2,1,0:T(8,128)(2,1)S(1)}, bf16[2,48,1536]{2,1,0:T(8,128)(2,1)S(1)}, u32[]{:S(2)}, u32[]{:S(2)}) collective-permute-start(bf16[2,48,1536]{2,1,0:T(8,128)(2,1)S(1)} %pad_maximum_fusion.6), channel_id=1, source_target_pairs={{0,2},{1,3},{2,4},{3,5},{4,6},{5,7},{6,0},{7,1},{8,10},{9,11},{10,... | collective-permute-start | bytes 884744 | tf_op jit(solution)/shard_map/ppermute | solution.py:46
  (27 other events, 223.1 us)

commit v2 on v1

v2 whole, which is shorter than its diff:
```python
import functools

import jax
import jax.numpy as jnp
from jax import lax
from jax.experimental import pallas as pl
from jax.experimental.pallas import tpu as pltpu
from jax.sharding import PartitionSpec as P

D = 8192
KV = 8
HD = 128
SUF = 128
GROUP = 8
ROWS = 48
QROWS = ROWS * GROUP
META = 16
PAYLOAD = QROWS + QROWS // 128 * META
PRE = 2048
HALF = 512
HIDDEN = 3584
A_COLS = 1280
B_COLS = HIDDEN - A_COLS
A_TILE = 256
B_TILE = 768
SAME_CORE = [list(range(0, 16, 2)), list(range(1, 16, 2))]
BF = jnp.bfloat16
F32 = jnp.float32
VMEM = 16 << 20
Q_TILE = 192
LOG2E = 1.4426950408889634


def ctx_perm(flip, s):
    return [(x * 4 + z, (x ^ flip) * 4 + (z + s) % 4) for x in range(2) for z in range(4)]


def batch_perm(flip_x, s, flip_core):
    return [
        (x * 8 + y * 2 + k, (x ^ flip_x) * 8 + (y + s) % 4 * 2 + (k ^ flip_core))
        for x in range(2)
        for y in range(4)
        for k in range(2)
    ]


def over_ctx(v, flip, s):
    return lax.ppermute(v, "ctx", ctx_perm(flip, s))


def over_batch(v, flip_x, s, flip_core=0):
    return lax.ppermute(v, "batch", batch_perm(flip_x, s, flip_core))


def nt_dot(a, b):
    return lax.dot_general(a, b, (((1,), (1,)), ((), ())), preferred_element_type=F32)


def heads_as_rows(q):
    return jnp.concatenate([q[:, h * HD : (h + 1) * HD] for h in range(GROUP)], axis=0)


def split3(v):
    hi = v.astype(BF).astype(F32)
    rest = v - hi
    mid = rest.astype(BF).astype(F32)
    return hi, mid, rest - mid


def attend_prefix(q, k, v):
    scale = 1.0 / (HD**0.5)
    outs, sums = [], []
    for t in range(QROWS // Q_TILE):
        s = nt_dot(q[t * Q_TILE : (t + 1) * Q_TILE], k)
        top = jnp.max(s, axis=1, keepdims=True)
        w = jnp.exp2((s - top) * (scale * LOG2E))
        total = jnp.sum(w, axis=1, keepdims=True)
        o = jnp.dot(w.astype(BF), v, preferred_element_type=F32)
        outs.append((o / total).astype(BF))
        sums.append(top * scale + jnp.log(total))
    return outs, jnp.concatenate(sums, axis=0)


def put_payload(put, outs, lse):
    column = lax.broadcasted_iota(jnp.int32, (128, 128), 1)
    for t, o in enumerate(outs):
        put(t * Q_TILE, o)
    for t in range(QROWS // 128):
        hi, mid, lo = split3(lse[t * 128 : (t + 1) * 128])
        parts = jnp.where(column == 0, hi, jnp.where(column == 1, mid, jnp.where(column == 2, lo, 0.0)))
        put(QROWS + t * META, parts.T[:META].astype(BF))


def prefix_kernel(which, group_ref, q_ref, k_ref, v_ref, *refs):
    out_ref = refs[-1]
    at = pl.ds(pl.multiple_of(group_ref[0] * HD, HD), HD)
    q = heads_as_rows(q_ref[...] if which is None else q_ref[which])

    def put(row, value):
        out_ref[row : row + value.shape[0], :] = value

    put_payload(put, *attend_prefix(q, k_ref[:, at], v_ref[:, at]))


def prefix_part(group, q, which, keys, values, after):
    vmem = pl.BlockSpec(memory_space=pltpu.VMEM)
    return pl.pallas_call(
        functools.partial(prefix_kernel, which),
        in_specs=[pl.BlockSpec(memory_space=pltpu.SMEM), pl.BlockSpec(), vmem, vmem]
        + [pl.BlockSpec(memory_space=pl.ANY)] * len(after),
        out_shape=jax.ShapeDtypeStruct((PAYLOAD, HD), BF),
        compiler_params=pltpu.CompilerParams(vmem_limit_bytes=VMEM),
        cost_estimate=pl.CostEstimate(
            flops=4 * QROWS * PRE * HD, bytes_accessed=2 * 2 * PRE * HD, transcendentals=QROWS * PRE
        ),
        name="prefix_part",
    )(group.astype(jnp.int32).reshape(1), q, keys, values, *after)


def pair_kernel(mine_ref, across_ref, _, out_ref):
    out_ref[0] = mine_ref[...]
    out_ref[1] = across_ref[...]


def pair_up(mine, across, after):
    return pl.pallas_call(
        pair_kernel,
        in_specs=[pl.BlockSpec(), pl.BlockSpec(), pl.BlockSpec(memory_space=pl.ANY)],
        out_shape=jax.ShapeDtypeStruct((2, *mine.shape), mine.dtype),
        compiler_params=pltpu.CompilerParams(vmem_limit_bytes=VMEM),
        cost_estimate=pl.CostEstimate(flops=0, bytes_accessed=4 * mine.size * 2, transcendentals=0),
        name="pair_up",
    )(mine, across, after)


SUF_LEAVES = 16


def suffix_kernel(q_ref, k_ref, v_ref, nk_ref, nv_ref, len_ref, o_ref, lse_ref):
    scale = 1.0 / (HD**0.5)
    n = SUF_LEAVES * GROUP
    q = heads_as_rows(q_ref[...])
    s = nt_dot(q, k_ref[...]) * scale
    lengths = jnp.concatenate([len_ref[...][:, :1]] * GROUP, axis=0)
    row = lax.broadcasted_iota(jnp.int32, (n, 1), 0) % SUF_LEAVES
    slot = lax.broadcasted_iota(jnp.int32, s.shape, 1) - row * SUF
    s = jnp.where((slot >= 0) & (slot < lengths), s, -1e30)
    fresh_key = jnp.concatenate([nk_ref[...].astype(F32)] * GROUP, axis=0)
    fresh = jnp.sum(q.astype(F32) * fresh_key, axis=1, keepdims=True) * scale
    top = jnp.maximum(jnp.max(s, axis=1, keepdims=True), fresh)
    w = jnp.exp(s - top)
    wn = jnp.exp(fresh - top)
    total = jnp.sum(w, axis=1, keepdims=True) + wn
    o = jnp.dot(w.astype(BF), v_ref[...], preferred_element_type=F32)
    fresh_value = jnp.concatenate([nv_ref[...].astype(F32)] * GROUP, axis=0)
    o = (o + wn.astype(BF).astype(F32) * fresh_value) / total
    lse = jnp.broadcast_to(top + jnp.log(total), o.shape)
    for h in range(GROUP):
        o_ref[h] = o[h * SUF_LEAVES : (h + 1) * SUF_LEAVES]
        lse_ref[h] = lse[h * SUF_LEAVES : (h + 1) * SUF_LEAVES]


def suffix_part(q, keys, values, new_key, new_value, lengths):
    shape = jax.ShapeDtypeStruct((GROUP, ROWS, HD), F32)
    leaf = lambda w: pl.BlockSpec((SUF_LEAVES, w), lambda i: (i, 0))
    cached = pl.BlockSpec((SUF_LEAVES * SUF, HD), lambda i: (i, 0))
    return pl.pallas_call(
        suffix_kernel,
        grid=(ROWS // SUF_LEAVES,),
        in_specs=[leaf(GROUP * HD), cached, cached, leaf(HD), leaf(HD), leaf(HD)],
        out_specs=[pl.BlockSpec((GROUP, SUF_LEAVES, HD), lambda i: (0, i, 0))] * 2,
        out_shape=[shape, shape],
        compiler_params=pltpu.CompilerParams(vmem_limit_bytes=VMEM),
        cost_estimate=pl.CostEstimate(flops=4 * QROWS * 2048 * HD, bytes_accessed=4 << 20, transcendentals=QROWS * 2048),
        name="suffix_part",
    )(
        q,
        keys.reshape(ROWS * SUF, HD),
        values.reshape(ROWS * SUF, HD),
        new_key,
        new_value,
        jnp.broadcast_to(lengths[:, None], (ROWS, HD)),
    )


def merge_kernel(*refs):
    parts, (so_ref, sl_ref, out_ref, token_ref, held) = refs[:KV], refs[KV:]
    token_ref[...] = jnp.zeros_like(token_ref)

    def rows_of(at, n):
        return [p[at : at + n, :].astype(F32) for p in parts]

    for t in range(QROWS // 128):
        rows = [m[0:1] + m[1:2] + m[2:3] for m in rows_of(QROWS + t * META, META)]
        lse = jnp.concatenate(rows, axis=0).T
        suf_lse = sl_ref[t * 128 : (t + 1) * 128, :1]
        top = jnp.maximum(jnp.max(lse, axis=1, keepdims=True), suf_lse)
        w = jnp.exp(lse - top)
        ws = jnp.exp(suf_lse - top)
        total = jnp.sum(w, axis=1, keepdims=True) + ws
        o = so_ref[t * 128 : (t + 1) * 128, :] * ws
        for i, p in enumerate(rows_of(t * 128, 128)):
            o = o + p * w[:, i : i + 1]
        held[t * 128 : (t + 1) * 128, :] = (o / total).astype(BF)
    for n in range(8):
        for h in range(GROUP):
            out_ref[n, :, h * HD : (h + 1) * HD] = held[h * ROWS : (h + 1) * ROWS, :]


def merge_parts(parts, suffix_out, suffix_lse):
    return pl.pallas_call(
        merge_kernel,
        out_shape=[jax.ShapeDtypeStruct((8, ROWS, GROUP * HD), BF), jax.ShapeDtypeStruct((8, HD), F32)],
        scratch_shapes=[pltpu.VMEM((QROWS, HD), BF)],
        compiler_params=pltpu.CompilerParams(vmem_limit_bytes=VMEM),
        cost_estimate=pl.CostEstimate(flops=QROWS * HD * 20, bytes_accessed=2 << 20, transcendentals=QROWS * 10),
        name="merge_parts",
    )(*parts, suffix_out.reshape(QROWS, HD), suffix_lse.reshape(QROWS, HD))


def project_kernel(z_ref, a_ref, own_w_ref, other_w_ref, g0_ref, g1_ref, _, gain_ref, mine_ref, *send_refs):
    gain_ref[:, :HALF] = g0_ref[...].astype(F32)
    gain_ref[:, HALF:] = g1_ref[...].astype(F32)
    z = z_ref[0]
    pieces = [a_ref[pl.ds(pl.multiple_of((z + s) % 4 * 96, 16), 96), :] for s in range(4)]
    a = jnp.concatenate(pieces, axis=0)
    for half, w_ref in enumerate((own_w_ref, other_w_ref)):
        y = jnp.dot(a, w_ref[...], preferred_element_type=F32)
        at = slice(half * HALF, (half + 1) * HALF)
        mine_ref[:, at] = y[:96]
        for s, ref in enumerate(send_refs):
            ref[:, at] = y[(s + 1) * 96 : (s + 2) * 96].astype(BF)


def project(z, attended, own_w, other_w, own_gain, other_gain, token):
    vmem = pl.BlockSpec(memory_space=pltpu.VMEM)
    return pl.pallas_call(
        project_kernel,
        in_specs=[pl.BlockSpec(memory_space=pltpu.SMEM)] + [vmem] * 5 + [pl.BlockSpec(memory_space=pl.ANY)],
        out_specs=[vmem] * 5,
        out_shape=[jax.ShapeDtypeStruct((1, 2 * HALF), F32), jax.ShapeDtypeStruct((96, 2 * HALF), F32)] + [jax.ShapeDtypeStruct((96, 2 * HALF), BF)] * 3,
        compiler_params=pltpu.CompilerParams(vmem_limit_bytes=VMEM),
        cost_estimate=pl.CostEstimate(flops=2 * 384 * 1024 * 1024, bytes_accessed=4 << 20, transcendentals=0),
        name="project",
    )(z, attended, own_w, other_w, own_gain, other_gain, token)


def fill_kernel(place_ref, *refs):
    pieces, (gain_ref, scaled_ref, squares_ref, theirs_ref) = refs[:4], refs[4:]
    for j, piece in enumerate(pieces):
        for e in range(2):
            sent = pl.multiple_of(place_ref[j * 2 + e] * ROWS, 16)
            block = pl.multiple_of(place_ref[8 + j * 2 + e] * ROWS, 16)
            rows = piece[e * ROWS : (e + 1) * ROWS, :]
            wide = rows.astype(F32)
            scaled_ref[pl.ds(sent, ROWS), :] = (wide * gain_ref[...]).astype(BF)
            theirs_ref[pl.ds(block, ROWS), :] = rows[:, HALF:]
            squares = jnp.sum(wide * wide, axis=1, keepdims=True)
            squares_ref[pl.ds(sent, ROWS), :] = jnp.broadcast_to(squares, (ROWS, HD))


def fill(place, pieces, gain):
    vmem = pl.BlockSpec(memory_space=pltpu.VMEM)
    return pl.pallas_call(
        fill_kernel,
        in_specs=[pl.BlockSpec(memory_space=pltpu.SMEM)] + [vmem] * 5,
        out_shape=[
            jax.ShapeDtypeStruct((384, 2 * HALF), BF),
            jax.ShapeDtypeStruct((384, HD), F32),
            jax.ShapeDtypeStruct((384, HALF), BF),
        ],
        compiler_params=pltpu.CompilerParams(vmem_limit_bytes=VMEM),
        cost_estimate=pl.CostEstimate(flops=384 * 4096, bytes_accessed=2 << 20, transcendentals=0),
        name="scale_rows",
    )(place, *pieces, gain)


def assemble_kernel(place_ref, *refs):
    pieces, (theirs_ref, out_ref) = refs[:4], refs[4:]
    core = place_ref[16]
    for j, piece in enumerate(pieces):
        for e in range(2):
            block = place_ref[8 + j * 2 + e]
            ours = pl.multiple_of((block * 2 + core) * ROWS, 16)
            other = pl.multiple_of((block * 2 + 1 - core) * ROWS, 16)
            out_ref[pl.ds(ours, ROWS), :] = piece[e * ROWS : (e + 1) * ROWS, :HALF]
            out_ref[pl.ds(other, ROWS), :] = theirs_ref[pl.ds(pl.multiple_of(block * ROWS, 16), ROWS), :]


def assemble(place, pieces, theirs):
    return pl.pallas_call(
        assemble_kernel,
        in_specs=[pl.BlockSpec(memory_space=pltpu.SMEM)] + [pl.BlockSpec()] * 5,
        out_shape=jax.ShapeDtypeStruct((768, HALF), BF),
        compiler_params=pltpu.CompilerParams(vmem_limit_bytes=VMEM),
        cost_estimate=pl.CostEstimate(flops=0, bytes_accessed=2 << 20, transcendentals=0),
        name="assemble_stream",
    )(place, *pieces, theirs)


def weight_tiles(first, columns, tile, weights, held, sems):
    copies = []
    tiles = columns // tile
    for t in range(tiles):
        at = slice(first + t * tile, first + (t + 1) * tile)
        copies.append([pltpu.make_async_copy(w.at[:, at], held.at[t, i], sems.at[t, i]) for i, w in enumerate(weights)])
        for copy in copies[t]:
            copy.start()
    for t in range(tiles):
        for copy in copies[t]:
            copy.wait()
        yield t, [held[t, i] for i in range(4)]


def hidden_sums(s, own_gate, other_gate, own_up, other_up):
    out = []
    for own, other in ((own_gate, other_gate), (own_up, other_up)):
        y = jnp.dot(s[:, :HALF], own, preferred_element_type=F32)
        out.append(y + jnp.dot(s[:, HALF:], other, preferred_element_type=F32))
    return out


def x_first_kernel(first, columns, s_ref, g0, g1, u0, u1, *refs):
    keep_ref, send_ref, held, sems = refs[-4:]
    for t, blocks in weight_tiles(first, columns, A_TILE, (g0, g1, u0, u1), held, sems):
        to = slice(t * A_TILE, (t + 1) * A_TILE)
        for n, y in enumerate(hidden_sums(s_ref[...], *blocks)):
            for k in range(4):
                keep_ref[k, n, :, to] = y[k * ROWS : (k + 1) * ROWS].astype(BF)
                send_ref[k, n, :, to] = y[(4 + k) * ROWS : (5 + k) * ROWS].astype(BF)


def y_first_kernel(first, columns, s_ref, g0, g1, u0, u1, squares_ref, *refs):
    here_ref, up_add, up_pass, down_add, down_pass, far_gate, far_up, held, sems = refs
    up, down, far = (up_add, up_pass), (down_pass, down_add), (far_gate, far_up)

    def put(n, to, y):
        for x in range(2):
            at = slice(x * ROWS, (x + 1) * ROWS)
            part = [y[(x * 4 + k) * ROWS : (x * 4 + k + 1) * ROWS] for k in range(4)]
            here_ref[at, to.start + n * (columns + HD) : to.stop + n * (columns + HD)] = part[0].astype(BF)
            for ref, value in ((up[n], part[1]), (far[n], part[2]), (down[n], part[3])):
                ref[at, to] = value.astype(BF)

    put(0, slice(columns, columns + HD), squares_ref[...])
    for t, blocks in weight_tiles(first, columns, B_TILE, (g0, g1, u0, u1), held, sems):
        for n, y in enumerate(hidden_sums(s_ref[...], *blocks)):
            put(n, slice(t * B_TILE, (t + 1) * B_TILE), y)


def hidden_call(kernel, first, columns, tile, scaled, weights, shapes, flops, name, more):
    tiles = columns // tile
    return pl.pallas_call(
        functools.partial(kernel, first, columns),
        in_specs=[pl.BlockSpec()] + [pl.BlockSpec(memory_space=pl.ANY)] * 4 + [pl.BlockSpec()] * len(more),
        out_shape=shapes,
        scratch_shapes=[pltpu.VMEM((tiles, 4, HALF, tile), BF), pltpu.SemaphoreType.DMA((tiles, 4))],
        compiler_params=pltpu.CompilerParams(vmem_limit_bytes=48 << 20),
        cost_estimate=pl.CostEstimate(flops=flops, bytes_accessed=flops // 1000, transcendentals=0),
        name=name,
    )(scaled, *weights, *more)


def x_first(first, columns, scaled, weights, *after):
    shapes = [jax.ShapeDtypeStruct((4, 2, ROWS, columns), BF)] * 2
    return hidden_call(
        x_first_kernel, first, columns, A_TILE, scaled, weights, shapes, 10**8, "hidden_x_first", after
    )


def y_first(first, columns, scaled, weights, squares):
    gate, rows = columns + HD, 2 * ROWS
    parts = [gate + columns, gate, columns, columns, gate, gate, columns]
    shapes = [jax.ShapeDtypeStruct((rows, n), BF) for n in parts]
    return hidden_call(
        y_first_kernel, first, columns, B_TILE, scaled, weights, shapes, 10**9, "hidden_y_first", (squares,)
    )


def pass_on_kernel(up_add, up_pass, down_add, down_pass, below, above, to_above, to_below):
    gate = up_add.shape[1]
    to_above[:, :gate] = (up_add[...].astype(F32) + below[...].astype(F32)).astype(BF)
    to_above[:, gate:] = up_pass[...]
    to_below[:, :gate] = down_pass[...]
    to_below[:, gate:] = (down_add[...].astype(F32) + above[...].astype(F32)).astype(BF)


def pass_on(*sums):
    shape = jax.ShapeDtypeStruct((2 * ROWS, sums[0].shape[1] + sums[1].shape[1]), BF)
    return pl.pallas_call(
        pass_on_kernel,
        out_shape=[shape, shape],
        compiler_params=pltpu.CompilerParams(vmem_limit_bytes=VMEM),
        cost_estimate=pl.CostEstimate(flops=10**6, bytes_accessed=5 << 20, transcendentals=0),
        name="pass_on_sums",
    )(*sums)


def add_kernel(keep_ref, got_ref, _, __, mine_ref, *send_refs):
    for k, ref in enumerate((mine_ref, *send_refs)):
        ref[...] = (keep_ref[k].astype(F32) + got_ref[k].astype(F32)).astype(ref.dtype)


def add_got(keep, got, after):
    held = pl.BlockSpec(memory_space=pl.ANY)
    return pl.pallas_call(
        add_kernel,
        in_specs=[pl.BlockSpec(), pl.BlockSpec(), held, held],
        out_shape=[jax.ShapeDtypeStruct(keep.shape[1:], t) for t in (F32, BF, BF, BF)],
        compiler_params=pltpu.CompilerParams(vmem_limit_bytes=VMEM),
        cost_estimate=pl.CostEstimate(flops=10**6, bytes_accessed=5 << 20, transcendentals=0),
        name="add_across_x",
    )(keep, got, *after)


def x_then_y(keep, send, after):
    mine, *sends = add_got(keep, over_batch(send, 1, 0), after)
    return mine + sum(over_batch(sends[s - 1], 0, s).astype(F32) for s in (2, 1, 3))


def y_sums(up_add, up_pass, down_add, down_pass, far_gate, far_up):
    from_below = over_batch(far_gate, 0, 1)
    from_above = over_batch(far_up, 0, -1)
    to_above, to_below = pass_on(up_add, up_pass, down_add, down_pass, from_below, from_above)
    return over_batch(to_above, 0, 1), over_batch(to_below, 0, -1)


def on_device(
    queries,
    new_key,
    new_value,
    prefix_keys,
    prefix_values,
    suffix_keys,
    suffix_values,
    suffix_lengths,
    out_weight,
    residual,
    norm_gain,
    gate_weight,
    up_weight,
):
    c = lax.axis_index("ctx")
    b = lax.axis_index("batch")
    xh, z = c // 4, c % 4
    xl, y, core = b // 8, b // 2 % 4, b % 2

    other_out = over_batch(out_weight, 0, 0, 1)
    own_gain = norm_gain.reshape(1, HALF)
    other_gain = over_batch(own_gain, 0, 0, 1)
    blocks = residual.reshape(4, 2, 2, ROWS, HALF)
    take = lambda k: lax.dynamic_slice(blocks, (z, 0, k, 0, 0), (1, 2, 1, ROWS, HALF)).reshape(96, HALF)
    residual_rows = jnp.concatenate([take(core), over_batch(take(1 - core), 0, 0, 1)], axis=1)

    def prefix(flip, s, q, which=None, after=()):
        return prefix_part((xh + flip) % 2 * 4 + (z - s) % 4, q, which, prefix_keys, prefix_values, after)

    q_across = over_ctx(queries, 1, 0)
    own = prefix(0, 0, queries)
    q2 = pair_up(queries, q_across, own)
    arrived = {0: None} | {s: over_ctx(q2, 0, s) for s in (1, 3, 2)}
    across = prefix(1, 0, q_across, None, (own,))
    suffix_out, suffix_lse = suffix_part(queries, suffix_keys, suffix_values, new_key, new_value, suffix_lengths)
    parts, last = [own, over_ctx(across, 1, 0)], across
    for s in (1, 3, 2):
        for flip in (1, 0):
            after = (last,) if len(parts) < 5 else (last, parts[len(parts) - 4])
            last = prefix(flip, s, arrived[s], flip, after)
            parts.append(over_ctx(last, flip, -s))
    attended, token = merge_parts(parts, suffix_out, suffix_lse)
    token, gate_weight, up_weight = lax.optimization_barrier((token, gate_weight, up_weight))
    everyone = lax.all_to_all(
        attended,
        "batch",
        0,
        0,
        axis_index_groups=SAME_CORE,
        tiled=True,
    ).reshape(384, 1024)
    gain, mine, *send = project(
        z.astype(jnp.int32).reshape(1), everyone, out_weight, other_out, own_gain, other_gain, token
    )
    other_gate, other_up = over_batch(gate_weight, 0, 0, 1), over_batch(up_weight, 0, 0, 1)
    for s in (1, 3, 2):
        mine = mine + over_ctx(send[s - 1], 0, s).astype(F32)
    mine = mine.astype(BF)
    across = over_ctx(mine, 1, 0)
    mixed = mine.astype(F32) + across.astype(F32)
    chunk = (residual_rows.astype(F32) + mixed).astype(BF)
    pieces = [chunk] + [over_ctx(chunk, 0, s) for s in (1, 3, 2)]
    piece_z = [z, (z - 1) % 4, (z - 3) % 4, (z - 2) % 4]

    blocks = [2 * pz + e for pz in piece_z for e in range(2)]
    place = [(block // 4 - xl) % 2 * 4 + (block % 4 - y) % 4 for block in blocks] + blocks + [core]
    place, other_gate, other_up = lax.optimization_barrier((jnp.stack(place).astype(jnp.int32), other_gate, other_up))
    scaled, squares, their_columns = fill(place, pieces, gain)
    weights = (gate_weight, other_gate, up_weight, other_up)
    b_first = y_first(A_COLS, B_COLS, scaled, weights, squares)
    a_first = x_first(0, A_COLS, scaled, weights, b_first[-1])
    received = y_sums(*b_first[1:])
    b_sums = b_first[0].astype(F32) + received[0].astype(F32) + received[1].astype(F32)
    b_sums = b_sums[:ROWS] + over_batch(b_sums[ROWS:].astype(BF), 1, 0).astype(F32)
    a_sums = x_then_y(*a_first, received)
    rms = jnp.sqrt(b_sums[:, B_COLS : B_COLS + 1] / D + 1e-05)

    def activate(gate, up):
        return (jax.nn.silu(gate / rms) * (up / rms)).astype(BF)

    activation = jnp.concatenate(
        [activate(a_sums[0], a_sums[1]), activate(b_sums[:, :B_COLS], b_sums[:, B_COLS + HD :])], axis=1
    )
    stream = assemble(place, pieces, over_batch(their_columns, 0, 0, 1))
    return (stream, activation)


def solution(mesh):
    in_specs = (
        P("batch", "ctx"),
        P("batch", "ctx"),
        P("batch", "ctx"),
        P("ctx", None),
        P("ctx", None),
        P("batch", None, "ctx"),
        P("batch", None, "ctx"),
        P("batch"),
        P("ctx", "batch"),
        P(None, "batch"),
        P("batch"),
        P("batch", "ctx"),
        P("batch", "ctx"),
    )
    out_specs = (P(None, "batch"), P("batch", "ctx"))
    return jax.shard_map(
        on_device, mesh=mesh, in_specs=in_specs, out_specs=out_specs, check_vma=False
    )
```

time: 175 us -> 163 us (0.931)
  Pallas kernels: 41.6 us -> 33.7 us
  starting transfers between devices: 59 us -> 53 us
  local copies, waits for them, and re-layouts: 5.11 us -> 10.9 us
  other arithmetic: 4 us -> 1.97 us
    pallas_call x7 -> x15, Pallas kernels: 36.3 us -> 28.5 us  [the longest x8 13.3 us: prefix_part(): pl.pallas_call(functools.partial(prefix_kernel, which), in_specs=[pl.Bloc...]
    unnamed x24 -> x26, local copies, waits for them, and re-layouts: 2.25 us -> 9.69 us
    ppermute x20 -> x15, starting transfers between devices: 21.5 us -> 15.2 us  [over_batch(): return lax.ppermute(v, 'batch', batch_perm(flip_x, s, flip_core))]
    ppermute x20 -> x15, waiting for transfers between devices: 31 us -> 31.6 us  [over_batch(): return lax.ppermute(v, 'batch', batch_perm(flip_x, s, flip_core))]
  transfers between devices with their start and end apart: 39 -> 34, of which waited for: 21 -> 17; matrix products, arithmetic and copies ran while one was open for 3% -> 1% of each run, Pallas kernels for 19% -> 15%
where the time goes in v2:
time: 163 us; the launch traced here: 162 us
  waiting for transfers between devices  61.9 us (38%)
  starting transfers between devices  53 us (33%)
  Pallas kernels  33.7 us (21%)
  local copies, waits for them, and re-layouts  10.9 us (7%)
  other arithmetic  1.97 us (1%)
    ppermute x18, starting transfers between devices, over_ctx(): return lax.ppermute(v, 'ctx', ctx_perm(flip, s))  32.5 us
    ppermute x15, waiting for transfers between devices, over_batch(): return lax.ppermute(v, 'batch', batch_perm(flip_x, s, flip_core))  31.6 us
    ppermute x18, waiting for transfers between devices, over_ctx(): return lax.ppermute(v, 'ctx', ctx_perm(flip, s))  21.2 us
    ppermute x15, starting transfers between devices, over_batch(): return lax.ppermute(v, 'batch', batch_perm(flip_x, s, flip_core))  15.2 us
    pallas_call x8, Pallas kernels, prefix_part(): pl.pallas_call(functools.partial(prefix_kernel, which), in_specs=[pl.Bloc...  13.3 us
    pallas_call x2, Pallas kernels, hidden_call(): pl.pallas_call(functools.partial(kernel, first, columns), in_specs=[pl.Bl...  10.4 us
    unnamed x26, local copies, waits for them, and re-layouts  9.69 us
    all_to_all x1, waiting for transfers between devices, on_device(): lax.all_to_all(attended, 'batch', 0, 0, axis_index_groups=SAME_CORE, tile...  9.09 us
  transfers between devices with their start and end apart: 34, of which 17 were waited for; matrix products, arithmetic and copies ran while one was open for 1% of the time, Pallas kernels for 15%

profile of v2, /device:TPU:0, one launch (start us, length us, event | category | flops | bytes accessed | tf_op | source)
XLA Modules:
  0.0 162.3 jit_solution(9993474261435063216)
XLA Ops:
  0.6 3.2 %collective-permute-start = (bf16[48,1024]{1,0:T(8,128)(2,1)}, bf16[48,1024]{1,0:T(8,128)(2,1)S(1)}, u32[]{:S(2)}, u32[]{:S(2)}) collective-permute-start(bf16[48,1024]{1,0:T(8,128)(2,1)} %q_ref.3), channel_id=1, source_target_pairs={{0,64},{16,80},{32,96},{48,112},{64,0},{80,16},{96,32},{112,48},{1... | collective-permute-start | bytes 294920 | tf_op jit(solution)/shard_map/ppermute | solution.py:48
  25.0 3.3 %collective-permute-start.3 = (bf16[432,128]{1,0:T(8,128)(2,1)S(1)}, bf16[432,128]{1,0:T(8,128)(2,1)S(1)}, u32[]{:S(2)}, u32[]{:S(2)}) collective-permute-start(bf16[432,128]{1,0:T(8,128)(2,1)S(1)} %prefix_part.10.refs_0_), channel_id=1, source_target_pairs={{0,112},{16,64},{32,80},{48,96},{64,48},{80,0},{96,16},{112,32},{1... | collective-permute-start | bytes 331784 | tf_op jit(solution)/shard_map/ppermute | solution.py:48
  40.2 3.1 %collective-permute-start.10 = (bf16[432,128]{1,0:T(8,128)(2,1)S(1)}, bf16[432,128]{1,0:T(8,128)(2,1)S(1)}, u32[]{:S(2)}, u32[]{:S(2)}) collective-permute-start(bf16[432,128]{1,0:T(8,128)(2,1)S(1)} %prefix_part.15), channel_id=1, source_target_pairs={{0,32},{16,48},{32,0},{48,16},{64,96},{80,112},{96,64},{112,80},{1... | collective-permute-start | bytes 331784 | tf_op jit(solution)/shard_map/ppermute | solution.py:48
  43.4 2.9 %collective-permute-start.9 = (bf16[432,128]{1,0:T(8,128)(2,1)S(1)}, bf16[432,128]{1,0:T(8,128)(2,1)S(1)}, u32[]{:S(2)}, u32[]{:S(2)}) collective-permute-start(bf16[432,128]{1,0:T(8,128)(2,1)S(1)} %prefix_part.14.refs_0_), channel_id=1, source_target_pairs={{0,96},{16,112},{32,64},{48,80},{64,32},{80,48},{96,0},{112,16},{1... | collective-permute-start | bytes 331784 | tf_op jit(solution)/shard_map/ppermute | solution.py:48
  46.4 2.7 %suffix_part.1 = (f32[8,48,128]{2,1,0:T(8,128)S(1)}, f32[8,48,128]{2,1,0:T(8,128)S(1)}) custom-call(bf16[48,1024]{1,0:T(8,128)(2,1)S(1)} %copy-done.7, bf16[6144,128]{1,0:T(8,128)(2,1)S(1)} %bitcast.52, bf16[6144,128]{1,0:T(8,128)(2,1)S(1)} %bitcast.53, bf16[48,128]{1,0:T(8,128)(2,1)S(1)} %copy-done.8, bf16[48,128]{1,0:T(8,128)(2,1)S(1)} %copy-done.9, ...), custom_call_target="tpu_custom_call" | custom-call | flops 402653184 | bytes 4194304 | tf_op jit(solution)/shard_map/suffix_part/pallas_call | solution.py:167
  49.1 2.9 %collective-permute-done.9.refs_6_ = bf16[432,128]{1,0:T(8,128)(2,1)S(1)} collective-permute-done((bf16[432,128]{1,0:T(8,128)(2,1)S(1)}, bf16[432,128]{1,0:T(8,128)(2,1)S(1)}, u32[]{:S(2)}, u32[]{:S(2)}) %collective-permute-start.9) | collective-permute-done | bytes 110624 | tf_op jit(solution)/shard_map/ppermute | solution.py:48
  52.0 2.8 %merge_parts.1 = (bf16[8,48,1024]{2,1,0:T(8,128)(2,1)}, f32[8,128]{1,0:T(8,128)S(1)}) custom-call(bf16[432,128]{1,0:T(8,128)(2,1)S(1)} %prefix_part.8.refs_0_._, bf16[432,128]{1,0:T(8,128)(2,1)S(1)} %collective-permute-done.1.refs_1_, bf16[432,128]{1,0:T(8,128)(2,1)S(1)} %collective-permute-done.3.refs_1_.refs_2_, ...), custom_call_target="tpu_custom_call" | custom-call | flops 983040 | bytes 2097152 | tf_op jit(solution)/shard_map/merge_parts/pallas_call | solution.py:211
  55.3 5.2 %all-to-all-start = ((bf16[8,48,1024]{2,1,0:T(8,128)(2,1)}), bf16[8,48,1024]{2,1,0:T(8,128)(2,1)S(1)}, u32[]{:S(2)}, u32[]{:S(2)}) async-start(bf16[8,48,1024]{2,1,0:T(8,128)(2,1)} %get-tuple-element.41), calls=%async_computation | async-start | bytes 1572864 | tf_op jit(solution)/shard_map/all_to_all | solution.py:472
  60.9 3.2 %collective-permute-done.15.g1_ref = bf16[1,512]{1,0:T(2,128)(2,1)S(1)} collective-permute-done((bf16[1,512]{1,0:T(2,128)(2,1)S(1)}, bf16[1,512]{1,0:T(2,128)(2,1)S(1)}, u32[]{:S(2)}, u32[]{:S(2)}) %collective-permute-start.15) | collective-permute-done | bytes 1056 | tf_op jit(solution)/shard_map/ppermute | solution.py:52
  64.1 9.1 %all-to-all-done = bf16[8,48,1024]{2,1,0:T(8,128)(2,1)S(1)} async-done(((bf16[8,48,1024]{2,1,0:T(8,128)(2,1)}), bf16[8,48,1024]{2,1,0:T(8,128)(2,1)S(1)}, u32[]{:S(2)}, u32[]{:S(2)}) %all-to-all-start) | async-done | bytes 786464 | tf_op jit(solution)/shard_map/all_to_all | solution.py:472
  74.9 3.2 %collective-permute-start.17 = (bf16[96,1024]{1,0:T(8,128)(2,1)}, bf16[96,1024]{1,0:T(8,128)(2,1)S(1)}, u32[]{:S(2)}, u32[]{:S(2)}) collective-permute-start(bf16[96,1024]{1,0:T(8,128)(2,1)} %get-tuple-element.45), channel_id=1, source_target_pairs={{0,48},{16,0},{32,16},{48,32},{64,112},{80,64},{96,80},{112,96},{1... | collective-permute-start | bytes 589832 | tf_op jit(solution)/shard_map/ppermute | solution.py:48
  78.1 9.0 %collective-permute-done.16 = bf16[96,1024]{1,0:T(8,128)(2,1)S(1)} collective-permute-done((bf16[96,1024]{1,0:T(8,128)(2,1)}, bf16[96,1024]{1,0:T(8,128)(2,1)S(1)}, u32[]{:S(2)}, u32[]{:S(2)}) %collective-permute-start.16) | collective-permute-done | bytes 196640 | tf_op jit(solution)/shard_map/ppermute | solution.py:48
  87.2 2.8 %collective-permute-start.19 = (bf16[96,1024]{1,0:T(8,128)(2,1)S(1)}, bf16[96,1024]{1,0:T(8,128)(2,1)S(1)}, u32[]{:S(2)}, u32[]{:S(2)}) collective-permute-start(bf16[96,1024]{1,0:T(8,128)(2,1)S(1)} %add_convert_fusion.1), channel_id=1, source_target_pairs={{0,64},{16,80},{32,96},{48,112},{64,0},{80,16},{96,32},{112,48},{1... | collective-permute-start | bytes 589832 | tf_op jit(solution)/shard_map/ppermute | solution.py:48
  95.5 2.6 %collective-permute-start.21 = (bf16[96,1024]{1,0:T(8,128)(2,1)S(1)}, bf16[96,1024]{1,0:T(8,128)(2,1)S(1)}, u32[]{:S(2)}, u32[]{:S(2)}) collective-permute-start(bf16[96,1024]{1,0:T(8,128)(2,1)S(1)} %add_convert_fusion.refs_0_), channel_id=1, source_target_pairs={{0,48},{16,0},{32,16},{48,32},{64,112},{80,64},{96,80},{112,96},{1... | collective-permute-start | bytes 589832 | tf_op jit(solution)/shard_map/ppermute | solution.py:48
  98.5 4.7 %collective-permute-done.22.refs_3_ = bf16[96,1024]{1,0:T(8,128)(2,1)S(1)} collective-permute-done((bf16[96,1024]{1,0:T(8,128)(2,1)S(1)}, bf16[96,1024]{1,0:T(8,128)(2,1)S(1)}, u32[]{:S(2)}, u32[]{:S(2)}) %collective-permute-start.22) | collective-permute-done | bytes 196640 | tf_op jit(solution)/shard_map/ppermute | solution.py:48
  106.6 6.1 %hidden_y_first.1 = (bf16[96,4736]{1,0:T(8,128)(2,1)S(1)}, bf16[96,2432]{1,0:T(8,128)(2,1)S(1)}, bf16[96,2304]{1,0:T(8,128)(2,1)S(1)}, bf16[96,2304]{1,0:T(8,128...) custom-call(bf16[384,1024]{1,0:T(8,128)(2,1)S(1)} %get-tuple-element.49.s_ref, ...), custom_call_target="tpu_custom_call" | custom-call | flops 1000000000 | bytes 1000000 | tf_op jit(solution)/shard_map/hidden_y_first/pallas_call | solution.py:353
  113.3 2.7 %collective-permute-start.26 = (bf16[96,2304]{1,0:T(8,128)(2,1)S(1)}, bf16[96,2304]{1,0:T(8,128)(2,1)S(1)}, u32[]{:S(2)}, u32[]{:S(2)}) collective-permute-start(bf16[96,2304]{1,0:T(8,128)(2,1)S(1)} %get-tuple-element.53.refs_0_), channel_id=1, source_target_pairs={{0,6},{1,7},{2,0},{3,1},{4,2},{5,3},{6,4},{7,5},{8,14},{9,15},{10,... | collective-permute-start | bytes 1327112 | tf_op jit(solution)/shard_map/ppermute | solution.py:52
  116.1 4.3 %hidden_x_first.1 = (bf16[4,2,48,1280]{3,2,1,0:T(8,128)(2,1)S(1)}, bf16[4,2,48,1280]{3,2,1,0:T(8,128)(2,1)S(1)}) custom-call(bf16[384,1024]{1,0:T(8,128)(2,1)S(1)} %get-tuple-element.49.s_ref, bf16[512,3584]{1,0:T(8,128)(2,1)} %g0.1, bf16[512,3584]{1,0:T(8,128)(2,1)} %collective-permute-done.11.g1, bf16[512,3584]{1,0:T(8,128)(2,1)} %u0.1, ...), custom_call_target="tpu_custom_call" | custom-call | flops 100000000 | bytes 100000 | tf_op jit(solution)/shard_map/hidden_x_first/pallas_call | solution.py:353
  125.4 3.2 %collective-permute-start.28 = (bf16[96,4736]{1,0:T(8,128)(2,1)S(1)}, bf16[96,4736]{1,0:T(8,128)(2,1)S(1)}, u32[]{:S(2)}, u32[]{:S(2)}) collective-permute-start(bf16[96,4736]{1,0:T(8,128)(2,1)S(1)} %get-tuple-element.62), channel_id=1, source_target_pairs={{0,6},{1,7},{2,0},{3,1},{4,2},{5,3},{6,4},{7,5},{8,14},{9,15},{10,... | collective-permute-start | bytes 2727944 | tf_op jit(solution)/shard_map/ppermute | solution.py:52
  131.8 10.1 %collective-permute-done.24.got_ref = bf16[4,2,48,1280]{3,2,1,0:T(8,128)(2,1)S(1)} collective-permute-done((bf16[4,2,48,1280]{3,2,1,0:T(8,128)(2,1)S(1)}, bf16[4,2,48,1280]{3,2,1,0:T(8,128)(2,1)S(1)}, u32[]{:S(2)}, u32[]{:S(2)}) %collective-permute-start.24) | collective-permute-done | bytes 983072 | tf_op jit(solution)/shard_map/ppermute | solution.py:52
  141.9 4.2 %collective-permute-done.27._ = bf16[96,4736]{1,0:T(8,128)(2,1)S(1)} collective-permute-done((bf16[96,4736]{1,0:T(8,128)(2,1)S(1)}, bf16[96,4736]{1,0:T(8,128)(2,1)S(1)}, u32[]{:S(2)}, u32[]{:S(2)}) %collective-permute-start.27) | collective-permute-done | bytes 909344 | tf_op jit(solution)/shard_map/ppermute | solution.py:52
  146.4 2.4 %collective-permute-start.29 = (bf16[2,48,1280]{2,1,0:T(8,128)(2,1)S(1)}, bf16[2,48,1280]{2,1,0:T(8,128)(2,1)S(1)}, u32[]{:S(2)}, u32[]{:S(2)}) collective-permute-start(bf16[2,48,1280]{2,1,0:T(8,128)(2,1)S(1)} %get-tuple-element.64), channel_id=1, source_target_pairs={{0,4},{1,5},{2,6},{3,7},{4,0},{5,1},{6,2},{7,3},{8,12},{9,13},{10,... | collective-permute-start | bytes 737288 | tf_op jit(solution)/shard_map/ppermute | solution.py:52
  155.2 2.5 %collective-permute-done.30 = bf16[2,48,1280]{2,1,0:T(8,128)(2,1)S(1)} collective-permute-done((bf16[2,48,1280]{2,1,0:T(8,128)(2,1)S(1)}, bf16[2,48,1280]{2,1,0:T(8,128)(2,1)S(1)}, u32[]{:S(2)}, u32[]{:S(2)}) %collective-permute-start.30) | collective-permute-done | bytes 245792 | tf_op jit(solution)/shard_map/ppermute | solution.py:52
  157.8 3.2 %collective-permute-done.32 = bf16[48,4736]{1,0:T(8,128)(2,1)S(1)} collective-permute-done((bf16[48,4736]{1,0:T(8,128)(2,1)S(1)}, bf16[48,4736]{1,0:T(8,128)(2,1)S(1)}, u32[]{:S(2)}, u32[]{:S(2)}) %collective-permute-start.32) | collective-permute-done | bytes 454688 | tf_op jit(solution)/shard_map/ppermute | solution.py:52
  (102 shorter events, 62.0 us)
Async XLA Ops:
  0.6 10.1 %collective-permute-start = (bf16[48,1024]{1,0:T(8,128)(2,1)}, bf16[48,1024]{1,0:T(8,128)(2,1)S(1)}, u32[]{:S(2)}, u32[]{:S(2)}) collective-permute-start(bf16[48,1024]{1,0:T(8,128)(2,1)} %q_ref.3), channel_id=1, source_target_pairs={{0,64},{16,80},{32,96},{48,112},{64,0},{80,16},{96,32},{112,48},{1... | collective-permute-start | bytes 294920 | tf_op jit(solution)/shard_map/ppermute | solution.py:48
  10.8 12.5 %collective-permute-start.2 = (bf16[2,48,1024]{2,1,0:T(8,128)(2,1)S(1)}, bf16[2,48,1024]{2,1,0:T(8,128)(2,1)S(1)}, u32[]{:S(2)}, u32[]{:S(2)}) collective-permute-start(bf16[2,48,1024]{2,1,0:T(8,128)(2,1)S(1)} %pair_up.1), channel_id=1, source_target_pairs={{0,16},{16,32},{32,48},{48,0},{64,80},{80,96},{96,112},{112,64},{1... | collective-permute-start | bytes 589832 | tf_op jit(solution)/shard_map/ppermute | solution.py:48
  12.8 18.8 %collective-permute-start.5 = (bf16[2,48,1024]{2,1,0:T(8,128)(2,1)S(1)}, bf16[2,48,1024]{2,1,0:T(8,128)(2,1)S(1)}, u32[]{:S(2)}, u32[]{:S(2)}) collective-permute-start(bf16[2,48,1024]{2,1,0:T(8,128)(2,1)S(1)} %pair_up.1), channel_id=1, source_target_pairs={{0,48},{16,0},{32,16},{48,32},{64,112},{80,64},{96,80},{112,96},{1... | collective-permute-start | bytes 589832 | tf_op jit(solution)/shard_map/ppermute | solution.py:48
  15.0 21.9 %collective-permute-start.8 = (bf16[2,48,1024]{2,1,0:T(8,128)(2,1)S(1)}, bf16[2,48,1024]{2,1,0:T(8,128)(2,1)S(1)}, u32[]{:S(2)}, u32[]{:S(2)}) collective-permute-start(bf16[2,48,1024]{2,1,0:T(8,128)(2,1)S(1)} %pair_up.1), channel_id=1, source_target_pairs={{0,32},{16,48},{32,0},{48,16},{64,96},{80,112},{96,64},{112,80},{1... | collective-permute-start | bytes 589832 | tf_op jit(solution)/shard_map/ppermute | solution.py:48
  22.8 11.0 %collective-permute-start.1 = (bf16[432,128]{1,0:T(8,128)(2,1)S(1)}, bf16[432,128]{1,0:T(8,128)(2,1)S(1)}, u32[]{:S(2)}, u32[]{:S(2)}) collective-permute-start(bf16[432,128]{1,0:T(8,128)(2,1)S(1)} %prefix_part.9.refs_0_), channel_id=1, source_target_pairs={{0,64},{16,80},{32,96},{48,112},{64,0},{80,16},{96,32},{112,48},{1... | collective-permute-start | bytes 331784 | tf_op jit(solution)/shard_map/ppermute | solution.py:48
  25.0 11.8 %collective-permute-start.3 = (bf16[432,128]{1,0:T(8,128)(2,1)S(1)}, bf16[432,128]{1,0:T(8,128)(2,1)S(1)}, u32[]{:S(2)}, u32[]{:S(2)}) collective-permute-start(bf16[432,128]{1,0:T(8,128)(2,1)S(1)} %prefix_part.10.refs_0_), channel_id=1, source_target_pairs={{0,112},{16,64},{32,80},{48,96},{64,48},{80,0},{96,16},{112,32},{1... | collective-permute-start | bytes 331784 | tf_op jit(solution)/shard_map/ppermute | solution.py:48
  33.2 15.9 %collective-permute-start.6 = (bf16[432,128]{1,0:T(8,128)(2,1)S(1)}, bf16[432,128]{1,0:T(8,128)(2,1)S(1)}, u32[]{:S(2)}, u32[]{:S(2)}) collective-permute-start(bf16[432,128]{1,0:T(8,128)(2,1)S(1)} %prefix_part.12.refs_0_), channel_id=1, source_target_pairs={{0,80},{16,96},{32,112},{48,64},{64,16},{80,32},{96,48},{112,0},{1... | collective-permute-start | bytes 331784 | tf_op jit(solution)/shard_map/ppermute | solution.py:48
  35.5 13.6 %collective-permute-start.7 = (bf16[432,128]{1,0:T(8,128)(2,1)S(1)}, bf16[432,128]{1,0:T(8,128)(2,1)S(1)}, u32[]{:S(2)}, u32[]{:S(2)}) collective-permute-start(bf16[432,128]{1,0:T(8,128)(2,1)S(1)} %prefix_part.13.refs_0_), channel_id=1, source_target_pairs={{0,16},{16,32},{32,48},{48,0},{64,80},{80,96},{96,112},{112,64},{1... | collective-permute-start | bytes 331784 | tf_op jit(solution)/shard_map/ppermute | solution.py:48
  40.2 8.9 %collective-permute-start.10 = (bf16[432,128]{1,0:T(8,128)(2,1)S(1)}, bf16[432,128]{1,0:T(8,128)(2,1)S(1)}, u32[]{:S(2)}, u32[]{:S(2)}) collective-permute-start(bf16[432,128]{1,0:T(8,128)(2,1)S(1)} %prefix_part.15), channel_id=1, source_target_pairs={{0,32},{16,48},{32,0},{48,16},{64,96},{80,112},{96,64},{112,80},{1... | collective-permute-start | bytes 331784 | tf_op jit(solution)/shard_map/ppermute | solution.py:48
  54.8 43.7 %collective-permute-start.11 = (bf16[512,3584]{1,0:T(8,128)(2,1)}, bf16[512,3584]{1,0:T(8,128)(2,1)}, u32[]{:S(2)}, u32[]{:S(2)}) collective-permute-start(bf16[512,3584]{1,0:T(8,128)(2,1)} %g0.1), channel_id=1, source_target_pairs={{0,1},{1,0},{2,3},{3,2},{4,5},{5,4},{6,7},{7,6},{8,9},{9,8},{10,11... | collective-permute-start | bytes 11010056 | tf_op jit(solution)/shard_map/ppermute | solution.py:52
  54.8 43.7 %collective-permute-start.12 = (bf16[512,3584]{1,0:T(8,128)(2,1)}, bf16[512,3584]{1,0:T(8,128)(2,1)}, u32[]{:S(2)}, u32[]{:S(2)}) collective-permute-start(bf16[512,3584]{1,0:T(8,128)(2,1)} %u0.1), channel_id=1, source_target_pairs={{0,1},{1,0},{2,3},{3,2},{4,5},{5,4},{6,7},{7,6},{8,9},{9,8},{10,11... | collective-permute-start | bytes 11010056 | tf_op jit(solution)/shard_map/ppermute | solution.py:52
  55.3 8.8 %collective-permute-start.14 = (bf16[1024,512]{1,0:T(8,128)(2,1)S(1)}, bf16[1024,512]{1,0:T(8,128)(2,1)S(1)}, u32[]{:S(2)}, u32[]{:S(2)}) collective-permute-start(bf16[1024,512]{1,0:T(8,128)(2,1)S(1)} %copy-done.10), channel_id=1, source_target_pairs={{0,1},{1,0},{2,3},{3,2},{4,5},{5,4},{6,7},{7,6},{8,9},{9,8},{10,11... | collective-permute-start | bytes 3145736 | tf_op jit(solution)/shard_map/ppermute | solution.py:52
  55.3 17.9 %all-to-all-start = ((bf16[8,48,1024]{2,1,0:T(8,128)(2,1)}), bf16[8,48,1024]{2,1,0:T(8,128)(2,1)S(1)}, u32[]{:S(2)}, u32[]{:S(2)}) async-start(bf16[8,48,1024]{2,1,0:T(8,128)(2,1)} %get-tuple-element.41), calls=%async_computation | async-start | bytes 1572864 | tf_op jit(solution)/shard_map/all_to_all | solution.py:472
  74.9 12.2 %collective-permute-start.16 = (bf16[96,1024]{1,0:T(8,128)(2,1)}, bf16[96,1024]{1,0:T(8,128)(2,1)S(1)}, u32[]{:S(2)}, u32[]{:S(2)}) collective-permute-start(bf16[96,1024]{1,0:T(8,128)(2,1)} %get-tuple-element.44), channel_id=1, source_target_pairs={{0,16},{16,32},{32,48},{48,0},{64,80},{80,96},{96,112},{112,64},{1... | collective-permute-start | bytes 589832 | tf_op jit(solution)/shard_map/ppermute | solution.py:48
  74.9 12.2 %collective-permute-start.17 = (bf16[96,1024]{1,0:T(8,128)(2,1)}, bf16[96,1024]{1,0:T(8,128)(2,1)S(1)}, u32[]{:S(2)}, u32[]{:S(2)}) collective-permute-start(bf16[96,1024]{1,0:T(8,128)(2,1)} %get-tuple-element.45), channel_id=1, source_target_pairs={{0,48},{16,0},{32,16},{48,32},{64,112},{80,64},{96,80},{112,96},{1... | collective-permute-start | bytes 589832 | tf_op jit(solution)/shard_map/ppermute | solution.py:48
  78.1 9.0 %collective-permute-start.18 = (bf16[96,1024]{1,0:T(8,128)(2,1)S(1)}, bf16[96,1024]{1,0:T(8,128)(2,1)S(1)}, u32[]{:S(2)}, u32[]{:S(2)}) collective-permute-start(bf16[96,1024]{1,0:T(8,128)(2,1)S(1)} %get-tuple-element.46), channel_id=1, source_target_pairs={{0,32},{16,48},{32,0},{48,16},{64,96},{80,112},{96,64},{112,80},{1... | collective-permute-start | bytes 589832 | tf_op jit(solution)/shard_map/ppermute | solution.py:48
  95.5 10.0 %collective-permute-start.21 = (bf16[96,1024]{1,0:T(8,128)(2,1)S(1)}, bf16[96,1024]{1,0:T(8,128)(2,1)S(1)}, u32[]{:S(2)}, u32[]{:S(2)}) collective-permute-start(bf16[96,1024]{1,0:T(8,128)(2,1)S(1)} %add_convert_fusion.refs_0_), channel_id=1, source_target_pairs={{0,48},{16,0},{32,16},{48,32},{64,112},{80,64},{96,80},{112,96},{1... | collective-permute-start | bytes 589832 | tf_op jit(solution)/shard_map/ppermute | solution.py:48
  112.8 12.3 %collective-permute-start.25 = (bf16[96,2432]{1,0:T(8,128)(2,1)S(1)}, bf16[96,2432]{1,0:T(8,128)(2,1)S(1)}, u32[]{:S(2)}, u32[]{:S(2)}) collective-permute-start(bf16[96,2432]{1,0:T(8,128)(2,1)S(1)} %get-tuple-element.60), channel_id=1, source_target_pairs={{0,2},{1,3},{2,4},{3,5},{4,6},{5,7},{6,0},{7,1},{8,10},{9,11},{10,... | collective-permute-start | bytes 1400840 | tf_op jit(solution)/shard_map/ppermute | solution.py:52
  113.3 10.5 %collective-permute-start.26 = (bf16[96,2304]{1,0:T(8,128)(2,1)S(1)}, bf16[96,2304]{1,0:T(8,128)(2,1)S(1)}, u32[]{:S(2)}, u32[]{:S(2)}) collective-permute-start(bf16[96,2304]{1,0:T(8,128)(2,1)S(1)} %get-tuple-element.53.refs_0_), channel_id=1, source_target_pairs={{0,6},{1,7},{2,0},{3,1},{4,2},{5,3},{6,4},{7,5},{8,14},{9,15},{10,... | collective-permute-start | bytes 1327112 | tf_op jit(solution)/shard_map/ppermute | solution.py:52
  120.3 21.6 %collective-permute-start.24 = (bf16[4,2,48,1280]{3,2,1,0:T(8,128)(2,1)S(1)}, bf16[4,2,48,1280]{3,2,1,0:T(8,128)(2,1)S(1)}, u32[]{:S(2)}, u32[]{:S(2)}) collective-permute-start(bf16[4,2,48,1280]{3,2,1,0:T(8,128)(2,1)S(1)} %get-tuple-element.55), channel_id=1, source_target_pairs={{0,8},{1,9},{2,10},{3,11},{4,12},{5,13},{6,14},{7,15},{8,0},{9,1},... | collective-permute-start | bytes 2949128 | tf_op jit(solution)/shard_map/ppermute | solution.py:52
  125.3 20.9 %collective-permute-start.27 = (bf16[96,4736]{1,0:T(8,128)(2,1)S(1)}, bf16[96,4736]{1,0:T(8,128)(2,1)S(1)}, u32[]{:S(2)}, u32[]{:S(2)}) collective-permute-start(bf16[96,4736]{1,0:T(8,128)(2,1)S(1)} %get-tuple-element.61), channel_id=1, source_target_pairs={{0,2},{1,3},{2,4},{3,5},{4,6},{5,7},{6,0},{7,1},{8,10},{9,11},{10,... | collective-permute-start | bytes 2727944 | tf_op jit(solution)/shard_map/ppermute | solution.py:52
  125.4 20.8 %collective-permute-start.28 = (bf16[96,4736]{1,0:T(8,128)(2,1)S(1)}, bf16[96,4736]{1,0:T(8,128)(2,1)S(1)}, u32[]{:S(2)}, u32[]{:S(2)}) collective-permute-start(bf16[96,4736]{1,0:T(8,128)(2,1)S(1)} %get-tuple-element.62), channel_id=1, source_target_pairs={{0,6},{1,7},{2,0},{3,1},{4,2},{5,3},{6,4},{7,5},{8,14},{9,15},{10,... | collective-permute-start | bytes 2727944 | tf_op jit(solution)/shard_map/ppermute | solution.py:52
  146.4 8.8 %collective-permute-start.29 = (bf16[2,48,1280]{2,1,0:T(8,128)(2,1)S(1)}, bf16[2,48,1280]{2,1,0:T(8,128)(2,1)S(1)}, u32[]{:S(2)}, u32[]{:S(2)}) collective-permute-start(bf16[2,48,1280]{2,1,0:T(8,128)(2,1)S(1)} %get-tuple-element.64), channel_id=1, source_target_pairs={{0,4},{1,5},{2,6},{3,7},{4,0},{5,1},{6,2},{7,3},{8,12},{9,13},{10,... | collective-permute-start | bytes 737288 | tf_op jit(solution)/shard_map/ppermute | solution.py:52
  148.8 8.9 %collective-permute-start.30 = (bf16[2,48,1280]{2,1,0:T(8,128)(2,1)S(1)}, bf16[2,48,1280]{2,1,0:T(8,128)(2,1)S(1)}, u32[]{:S(2)}, u32[]{:S(2)}) collective-permute-start(bf16[2,48,1280]{2,1,0:T(8,128)(2,1)S(1)} %get-tuple-element.65), channel_id=1, source_target_pairs={{0,2},{1,3},{2,4},{3,5},{4,6},{5,7},{6,0},{7,1},{8,10},{9,11},{10,... | collective-permute-start | bytes 737288 | tf_op jit(solution)/shard_map/ppermute | solution.py:52
  (23 other events, 140.3 us)

commit v3 on v2

--- a/solution.py
+++ b/solution.py
@@ -19,15 +19,16 @@
 PRE = 2048
 HALF = 512
 HIDDEN = 3584
-A_COLS = 1280
+A_COLS = 1536
 B_COLS = HIDDEN - A_COLS
-A_TILE = 256
-B_TILE = 768
+A_TILE = 512
+B_TILE = 512
 SAME_CORE = [list(range(0, 16, 2)), list(range(1, 16, 2))]
 BF = jnp.bfloat16
 F32 = jnp.float32
 VMEM = 16 << 20
 Q_TILE = 192
+OWN_COPIES = 4
 LOG2E = 1.4426950408889634
 
 
@@ -102,6 +103,40 @@
     put_payload(put, *attend_prefix(q, k_ref[:, at], v_ref[:, at]))
 
 
+def own_prefix_kernel(group_ref, q_ref, k_ref, v_ref, out_ref, token_ref, k_held, v_held, sems):
+    token_ref[...] = jnp.zeros_like(token_ref)
+    at = pl.ds(pl.multiple_of(group_ref[0] * HD, HD), HD)
+    copies = []
+    for n, (source, held) in enumerate(((k_ref, k_held), (v_ref, v_held))):
+        for m in range(OWN_COPIES):
+            rows = pl.ds(m * (PRE // OWN_COPIES), PRE // OWN_COPIES)
+            copies.append(pltpu.make_async_copy(source.at[rows, at], held.at[rows], sems.at[n, m]))
+    for copy in copies:
+        copy.start()
+    for copy in copies:
+        copy.wait()
+
+    def put(row, value):
+        out_ref[row : row + value.shape[0], :] = value
+
+    put_payload(put, *attend_prefix(heads_as_rows(q_ref[...]), k_held[...], v_held[...]))
+
+
+def own_prefix(group, q, keys, values):
+    held = pl.BlockSpec(memory_space=pl.ANY)
+    return pl.pallas_call(
+        own_prefix_kernel,
+        in_specs=[pl.BlockSpec(memory_space=pltpu.SMEM), pl.BlockSpec(), held, held],
+        out_shape=[jax.ShapeDtypeStruct((PAYLOAD, HD), BF), jax.ShapeDtypeStruct((8, HD), F32)],
+        scratch_shapes=[pltpu.VMEM((PRE, HD), BF), pltpu.VMEM((PRE, HD), BF), pltpu.SemaphoreType.DMA((2, OWN_COPIES))],
+        compiler_params=pltpu.CompilerParams(vmem_limit_bytes=59 << 20),
+        cost_estimate=pl.CostEstimate(
+            flops=4 * QROWS * PRE * HD, bytes_accessed=2 * 2 * PRE * HD, transcendentals=QROWS * PRE
+        ),
+        name="own_prefix",
+    )(group, q, keys, values)
+
+
 def prefix_part(group, q, which, keys, values, after):
     vmem = pl.BlockSpec(memory_space=pltpu.VMEM)
     return pl.pallas_call(
@@ -114,7 +149,7 @@
             flops=4 * QROWS * PRE * HD, bytes_accessed=2 * 2 * PRE * HD, transcendentals=QROWS * PRE
         ),
         name="prefix_part",
-    )(group.astype(jnp.int32).reshape(1), q, keys, values, *after)
+    )(group, q, keys, values, *after)
 
 
 def pair_kernel(mine_ref, across_ref, _, out_ref):
@@ -125,7 +160,6 @@
 def pair_up(mine, across, after):
     return pl.pallas_call(
         pair_kernel,
-        in_specs=[pl.BlockSpec(), pl.BlockSpec(), pl.BlockSpec(memory_space=pl.ANY)],
         out_shape=jax.ShapeDtypeStruct((2, *mine.shape), mine.dtype),
         compiler_params=pltpu.CompilerParams(vmem_limit_bytes=VMEM),
         cost_estimate=pl.CostEstimate(flops=0, bytes_accessed=4 * mine.size * 2, transcendentals=0),
@@ -184,8 +218,7 @@
 
 
 def merge_kernel(*refs):
-    parts, (so_ref, sl_ref, out_ref, token_ref, held) = refs[:KV], refs[KV:]
-    token_ref[...] = jnp.zeros_like(token_ref)
+    parts, (so_ref, sl_ref, out_ref, held) = refs[:KV], refs[KV:]
 
     def rows_of(at, n):
         return [p[at : at + n, :].astype(F32) for p in parts]
@@ -210,7 +243,7 @@
 def merge_parts(parts, suffix_out, suffix_lse):
     return pl.pallas_call(
         merge_kernel,
-        out_shape=[jax.ShapeDtypeStruct((8, ROWS, GROUP * HD), BF), jax.ShapeDtypeStruct((8, HD), F32)],
+        out_shape=jax.ShapeDtypeStruct((8, ROWS, GROUP * HD), BF),
         scratch_shapes=[pltpu.VMEM((QROWS, HD), BF)],
         compiler_params=pltpu.CompilerParams(vmem_limit_bytes=VMEM),
         cost_estimate=pl.CostEstimate(flops=QROWS * HD * 20, bytes_accessed=2 << 20, transcendentals=QROWS * 10),
@@ -218,7 +251,7 @@
     )(*parts, suffix_out.reshape(QROWS, HD), suffix_lse.reshape(QROWS, HD))
 
 
-def project_kernel(z_ref, a_ref, own_w_ref, other_w_ref, g0_ref, g1_ref, _, gain_ref, mine_ref, *send_refs):
+def project_kernel(z_ref, a_ref, own_w_ref, other_w_ref, g0_ref, g1_ref, gain_ref, mine_ref, *send_refs):
     gain_ref[:, :HALF] = g0_ref[...].astype(F32)
     gain_ref[:, HALF:] = g1_ref[...].astype(F32)
     z = z_ref[0]
@@ -232,17 +265,17 @@
             ref[:, at] = y[(s + 1) * 96 : (s + 2) * 96].astype(BF)
 
 
-def project(z, attended, own_w, other_w, own_gain, other_gain, token):
+def project(z, attended, own_w, other_w, own_gain, other_gain):
     vmem = pl.BlockSpec(memory_space=pltpu.VMEM)
     return pl.pallas_call(
         project_kernel,
-        in_specs=[pl.BlockSpec(memory_space=pltpu.SMEM)] + [vmem] * 5 + [pl.BlockSpec(memory_space=pl.ANY)],
+        in_specs=[pl.BlockSpec(memory_space=pltpu.SMEM)] + [vmem] * 5,
         out_specs=[vmem] * 5,
         out_shape=[jax.ShapeDtypeStruct((1, 2 * HALF), F32), jax.ShapeDtypeStruct((96, 2 * HALF), F32)] + [jax.ShapeDtypeStruct((96, 2 * HALF), BF)] * 3,
         compiler_params=pltpu.CompilerParams(vmem_limit_bytes=VMEM),
         cost_estimate=pl.CostEstimate(flops=2 * 384 * 1024 * 1024, bytes_accessed=4 << 20, transcendentals=0),
         name="project",
-    )(z, attended, own_w, other_w, own_gain, other_gain, token)
+    )(z, attended, own_w, other_w, own_gain, other_gain)
 
 
 def fill_kernel(place_ref, *refs):
@@ -276,7 +309,8 @@
 
 
 def assemble_kernel(place_ref, *refs):
-    pieces, (theirs_ref, out_ref) = refs[:4], refs[4:]
+    pieces, (theirs_ref, out_ref, token_ref) = refs[:4], refs[4:]
+    token_ref[...] = jnp.zeros_like(token_ref)
     core = place_ref[16]
     for j, piece in enumerate(pieces):
         for e in range(2):
@@ -291,9 +325,9 @@
     return pl.pallas_call(
         assemble_kernel,
         in_specs=[pl.BlockSpec(memory_space=pltpu.SMEM)] + [pl.BlockSpec()] * 5,
-        out_shape=jax.ShapeDtypeStruct((768, HALF), BF),
-        compiler_params=pltpu.CompilerParams(vmem_limit_bytes=VMEM),
-        cost_estimate=pl.CostEstimate(flops=0, bytes_accessed=2 << 20, transcendentals=0),
+        out_shape=[jax.ShapeDtypeStruct((768, HALF), BF), jax.ShapeDtypeStruct((8, HD), F32)],
+        compiler_params=pltpu.CompilerParams(vmem_limit_bytes=VMEM),
+        cost_estimate=pl.CostEstimate(flops=1000, bytes_accessed=1000, transcendentals=0),
         name="assemble_stream",
     )(place, *pieces, theirs)
 
@@ -321,7 +355,8 @@
 
 
 def x_first_kernel(first, columns, s_ref, g0, g1, u0, u1, *refs):
-    keep_ref, send_ref, held, sems = refs[-4:]
+    keep_ref, send_ref, token_ref, held, sems = refs[-5:]
+    token_ref[...] = jnp.zeros_like(token_ref)
     for t, blocks in weight_tiles(first, columns, A_TILE, (g0, g1, u0, u1), held, sems):
         to = slice(t * A_TILE, (t + 1) * A_TILE)
         for n, y in enumerate(hidden_sums(s_ref[...], *blocks)):
@@ -362,7 +397,7 @@
 
 
 def x_first(first, columns, scaled, weights, *after):
-    shapes = [jax.ShapeDtypeStruct((4, 2, ROWS, columns), BF)] * 2
+    shapes = [jax.ShapeDtypeStruct((4, 2, ROWS, columns), BF)] * 2 + [jax.ShapeDtypeStruct((8, HD), F32)]
     return hidden_call(
         x_first_kernel, first, columns, A_TILE, scaled, weights, shapes, 10**8, "hidden_x_first", after
     )
@@ -377,7 +412,7 @@
     )
 
 
-def pass_on_kernel(up_add, up_pass, down_add, down_pass, below, above, to_above, to_below):
+def pass_on_kernel(up_add, up_pass, down_add, down_pass, below, above, _, to_above, to_below):
     gate = up_add.shape[1]
     to_above[:, :gate] = (up_add[...].astype(F32) + below[...].astype(F32)).astype(BF)
     to_above[:, gate:] = up_pass[...]
@@ -391,12 +426,30 @@
         pass_on_kernel,
         out_shape=[shape, shape],
         compiler_params=pltpu.CompilerParams(vmem_limit_bytes=VMEM),
-        cost_estimate=pl.CostEstimate(flops=10**6, bytes_accessed=5 << 20, transcendentals=0),
+        cost_estimate=pl.CostEstimate(flops=1000, bytes_accessed=1000, transcendentals=0),
         name="pass_on_sums",
     )(*sums)
 
 
-def add_kernel(keep_ref, got_ref, _, __, mine_ref, *send_refs):
+def finish_kernel(here_ref, below_ref, above_ref, _, keep_ref, send_ref):
+    sums = here_ref[...].astype(F32) + below_ref[...].astype(F32) + above_ref[...].astype(F32)
+    keep_ref[...] = sums[:ROWS]
+    send_ref[...] = sums[ROWS:].astype(BF)
+
+
+def finish_y(here, below, above, after):
+    shape = lambda t: jax.ShapeDtypeStruct((ROWS, here.shape[1]), t)
+    return pl.pallas_call(
+        finish_kernel,
+        in_specs=[pl.BlockSpec()] * 4,
+        out_shape=[shape(F32), shape(BF)],
+        compiler_params=pltpu.CompilerParams(vmem_limit_bytes=VMEM),
+        cost_estimate=pl.CostEstimate(flops=1000, bytes_accessed=1000, transcendentals=0),
+        name="finish_y",
+    )(here, below, above, after)
+
+
+def add_kernel(keep_ref, got_ref, _, mine_ref, *send_refs):
     for k, ref in enumerate((mine_ref, *send_refs)):
         ref[...] = (keep_ref[k].astype(F32) + got_ref[k].astype(F32)).astype(ref.dtype)
 
@@ -405,23 +458,57 @@
     held = pl.BlockSpec(memory_space=pl.ANY)
     return pl.pallas_call(
         add_kernel,
-        in_specs=[pl.BlockSpec(), pl.BlockSpec(), held, held],
+        in_specs=[pl.BlockSpec(), pl.BlockSpec(), held],
         out_shape=[jax.ShapeDtypeStruct(keep.shape[1:], t) for t in (F32, BF, BF, BF)],
         compiler_params=pltpu.CompilerParams(vmem_limit_bytes=VMEM),
-        cost_estimate=pl.CostEstimate(flops=10**6, bytes_accessed=5 << 20, transcendentals=0),
+        cost_estimate=pl.CostEstimate(flops=1000, bytes_accessed=1000, transcendentals=0),
         name="add_across_x",
-    )(keep, got, *after)
-
-
-def x_then_y(keep, send, after):
-    mine, *sends = add_got(keep, over_batch(send, 1, 0), after)
-    return mine + sum(over_batch(sends[s - 1], 0, s).astype(F32) for s in (2, 1, 3))
-
-
-def y_sums(up_add, up_pass, down_add, down_pass, far_gate, far_up):
+    )(keep, got, after)
+
+
+def activate(gate, up, rms):
+    return (jax.nn.silu(gate / rms) * (up / rms)).astype(BF)
+
+
+def finish_b_kernel(keep_ref, got_ref, out_ref, rms_ref):
+    columns = out_ref.shape[1]
+    sums = keep_ref[...] + got_ref[...].astype(F32)
+    rms = jnp.sqrt(sums[:, columns : columns + HD] / D + 1e-05)
+    rms_ref[...] = rms
+    out_ref[...] = activate(sums[:, :columns], sums[:, columns + HD :], rms[:, :1])
+
+
+def finish_b(keep, got):
+    return pl.pallas_call(
+        finish_b_kernel,
+        out_shape=[jax.ShapeDtypeStruct((ROWS, B_COLS), BF), jax.ShapeDtypeStruct((ROWS, HD), F32)],
+        compiler_params=pltpu.CompilerParams(vmem_limit_bytes=VMEM),
+        cost_estimate=pl.CostEstimate(flops=10**6, bytes_accessed=1 << 20, transcendentals=10**5),
+        name="finish_b",
+    )(keep, got)
+
+
+def finish_a_kernel(mine_ref, *refs):
+    got, (b_ref, rms_ref, out_ref) = refs[:3], refs[3:]
+    gate, up = (mine_ref[n] + sum(g[n].astype(F32) for g in got) for n in range(2))
+    out_ref[:, :A_COLS] = activate(gate, up, rms_ref[:, :1])
+    out_ref[:, A_COLS:] = b_ref[...]
+
+
+def finish_a(mine, got, b_part, rms):
+    return pl.pallas_call(
+        finish_a_kernel,
+        out_shape=jax.ShapeDtypeStruct((ROWS, HIDDEN), BF),
+        compiler_params=pltpu.CompilerParams(vmem_limit_bytes=VMEM),
+        cost_estimate=pl.CostEstimate(flops=10**6, bytes_accessed=1 << 20, transcendentals=10**5),
+        name="finish_a",
+    )(mine, *got, b_part, rms)
+
+
+def y_sums(up_add, up_pass, down_add, down_pass, far_gate, far_up, token):
     from_below = over_batch(far_gate, 0, 1)
     from_above = over_batch(far_up, 0, -1)
-    to_above, to_below = pass_on(up_add, up_pass, down_add, down_pass, from_below, from_above)
+    to_above, to_below = pass_on(up_add, up_pass, down_add, down_pass, from_below, from_above, token)
     return over_batch(to_above, 0, 1), over_batch(to_below, 0, -1)
 
 
@@ -445,6 +532,7 @@
     xh, z = c // 4, c % 4
     xl, y, core = b // 8, b // 2 % 4, b % 2
 
+    other_gate, other_up = over_batch(gate_weight, 0, 0, 1), over_batch(up_weight, 0, 0, 1)
     other_out = over_batch(out_weight, 0, 0, 1)
     own_gain = norm_gain.reshape(1, HALF)
     other_gain = over_batch(own_gain, 0, 0, 1)
@@ -452,23 +540,25 @@
     take = lambda k: lax.dynamic_slice(blocks, (z, 0, k, 0, 0), (1, 2, 1, ROWS, HALF)).reshape(96, HALF)
     residual_rows = jnp.concatenate([take(core), over_batch(take(1 - core), 0, 0, 1)], axis=1)
 
-    def prefix(flip, s, q, which=None, after=()):
-        return prefix_part((xh + flip) % 2 * 4 + (z - s) % 4, q, which, prefix_keys, prefix_values, after)
+    def group_of(flip, s):
+        return ((xh + flip) % 2 * 4 + (z - s) % 4).astype(jnp.int32).reshape(1)
 
     q_across = over_ctx(queries, 1, 0)
-    own = prefix(0, 0, queries)
-    q2 = pair_up(queries, q_across, own)
+    own, token = own_prefix(group_of(0, 0), queries, prefix_keys, prefix_values)
+    q2 = pair_up(queries, q_across, token)
     arrived = {0: None} | {s: over_ctx(q2, 0, s) for s in (1, 3, 2)}
-    across = prefix(1, 0, q_across, None, (own,))
+    across = prefix_part(group_of(1, 0), q_across, None, prefix_keys, prefix_values, ())
     suffix_out, suffix_lse = suffix_part(queries, suffix_keys, suffix_values, new_key, new_value, suffix_lengths)
     parts, last = [own, over_ctx(across, 1, 0)], across
     for s in (1, 3, 2):
         for flip in (1, 0):
             after = (last,) if len(parts) < 5 else (last, parts[len(parts) - 4])
-            last = prefix(flip, s, arrived[s], flip, after)
+            group = group_of(flip, s)
+            if len(parts) == 2:
+                group, other_gate, other_up = lax.optimization_barrier((group, other_gate, other_up))
+            last = prefix_part(group, arrived[s], flip, prefix_keys, prefix_values, after)
             parts.append(over_ctx(last, flip, -s))
-    attended, token = merge_parts(parts, suffix_out, suffix_lse)
-    token, gate_weight, up_weight = lax.optimization_barrier((token, gate_weight, up_weight))
+    attended = merge_parts(parts, suffix_out, suffix_lse)
     everyone = lax.all_to_all(
         attended,
         "batch",
@@ -478,9 +568,8 @@
         tiled=True,
     ).reshape(384, 1024)
     gain, mine, *send = project(
-        z.astype(jnp.int32).reshape(1), everyone, out_weight, other_out, own_gain, other_gain, token
+        z.astype(jnp.int32).reshape(1), everyone, out_weight, other_out, own_gain, other_gain
     )
-    other_gate, other_up = over_batch(gate_weight, 0, 0, 1), over_batch(up_weight, 0, 0, 1)
     for s in (1, 3, 2):
         mine = mine + over_ctx(send[s - 1], 0, s).astype(F32)
     mine = mine.astype(BF)
@@ -492,24 +581,17 @@
 
     blocks = [2 * pz + e for pz in piece_z for e in range(2)]
     place = [(block // 4 - xl) % 2 * 4 + (block % 4 - y) % 4 for block in blocks] + blocks + [core]
-    place, other_gate, other_up = lax.optimization_barrier((jnp.stack(place).astype(jnp.int32), other_gate, other_up))
+    place = jnp.stack(place).astype(jnp.int32)
     scaled, squares, their_columns = fill(place, pieces, gain)
     weights = (gate_weight, other_gate, up_weight, other_up)
     b_first = y_first(A_COLS, B_COLS, scaled, weights, squares)
     a_first = x_first(0, A_COLS, scaled, weights, b_first[-1])
-    received = y_sums(*b_first[1:])
-    b_sums = b_first[0].astype(F32) + received[0].astype(F32) + received[1].astype(F32)
-    b_sums = b_sums[:ROWS] + over_batch(b_sums[ROWS:].astype(BF), 1, 0).astype(F32)
-    a_sums = x_then_y(*a_first, received)
-    rms = jnp.sqrt(b_sums[:, B_COLS : B_COLS + 1] / D + 1e-05)
-
-    def activate(gate, up):
-        return (jax.nn.silu(gate / rms) * (up / rms)).astype(BF)
-
-    activation = jnp.concatenate(
-        [activate(a_sums[0], a_sums[1]), activate(b_sums[:, :B_COLS], b_sums[:, B_COLS + HD :])], axis=1
-    )
-    stream = assemble(place, pieces, over_batch(their_columns, 0, 0, 1))
+    received = y_sums(*b_first[1:], a_first[2])
+    stream, token = assemble(place, pieces, over_batch(their_columns, 0, 0, 1))
+    b_keep, b_send = finish_y(b_first[0], *received, token)
+    b_part, rms = finish_b(b_keep, over_batch(b_send, 1, 0))
+    mine, *sends = add_got(a_first[0], over_batch(a_first[1], 1, 0), b_send)
+    activation = finish_a(mine, [over_batch(sends[s - 1], 0, s) for s in (2, 1, 3)], b_part, rms)
     return (stream, activation)
 
 

time: 163 us -> 157 us (0.963)
  local copies, waits for them, and re-layouts: 10.9 us -> 6.22 us
  Pallas kernels: 33.7 us -> 38 us
  waiting for transfers between devices: 61.9 us -> 58.5 us
  other arithmetic: 1.97 us -> 0.17 us
    pallas_call x2 -> x6, Pallas kernels: 2.79 us -> 8.92 us  [the longest x1 4.63 us: own_prefix(): pl.pallas_call(own_prefix_kernel, in_specs=[pl.BlockSpec(memory_space=plt...]
    unnamed x26 -> x24, local copies, waits for them, and re-layouts: 9.69 us -> 5.1 us
    ppermute x15, waiting for transfers between devices: 31.6 us -> 28.6 us  [over_batch(): return lax.ppermute(v, 'batch', batch_perm(flip_x, s, flip_core))]
    ppermute x15, starting transfers between devices: 15.2 us -> 17.1 us  [over_batch(): return lax.ppermute(v, 'batch', batch_perm(flip_x, s, flip_core))]
    pallas_call x8 -> x7, Pallas kernels: 13.3 us -> 11.7 us  [prefix_part(): pl.pallas_call(functools.partial(prefix_kernel, which), in_specs=[pl.Bloc...]
  transfers between devices with their start and end apart: 34 -> 34, of which waited for: 17 -> 17; matrix products, arithmetic and copies ran while one was open for 1% -> 1% of each run, Pallas kernels for 15% -> 18%
where the time goes in v3:
time: 157 us; the launch traced here: 156 us
  waiting for transfers between devices  58.5 us (37%)
  starting transfers between devices  52.7 us (34%)
  Pallas kernels  38 us (24%)
  local copies, waits for them, and re-layouts  6.22 us (4%)
    ppermute x18, starting transfers between devices, over_ctx(): return lax.ppermute(v, 'ctx', ctx_perm(flip, s))  31.1 us
    ppermute x15, waiting for transfers between devices, over_batch(): return lax.ppermute(v, 'batch', batch_perm(flip_x, s, flip_core))  28.6 us
    ppermute x18, waiting for transfers between devices, over_ctx(): return lax.ppermute(v, 'ctx', ctx_perm(flip, s))  21 us
    ppermute x15, starting transfers between devices, over_batch(): return lax.ppermute(v, 'batch', batch_perm(flip_x, s, flip_core))  17.1 us
    pallas_call x7, Pallas kernels, prefix_part(): pl.pallas_call(functools.partial(prefix_kernel, which), in_specs=[pl.Bloc...  11.7 us
    pallas_call x2, Pallas kernels, hidden_call(): pl.pallas_call(functools.partial(kernel, first, columns), in_specs=[pl.Bl...  10.2 us
    all_to_all x1, waiting for transfers between devices, on_device(): lax.all_to_all(attended, 'batch', 0, 0, axis_index_groups=SAME_CORE, tile...  8.9 us
    unnamed x24, local copies, waits for them, and re-layouts  5.1 us
  transfers between devices with their start and end apart: 34, of which 17 were waited for; matrix products, arithmetic and copies ran while one was open for 1% of the time, Pallas kernels for 18%

profile of v3, /device:TPU:0, one launch (start us, length us, event | category | flops | bytes accessed | tf_op | source)
XLA Modules:
  0.0 156.5 jit_solution(4765762517094109056)
XLA Ops:
  1.2 3.1 %collective-permute-start.1 = (bf16[48,1024]{1,0:T(8,128)(2,1)}, bf16[48,1024]{1,0:T(8,128)(2,1)S(1)}, u32[]{:S(2)}, u32[]{:S(2)}) collective-permute-start(bf16[48,1024]{1,0:T(8,128)(2,1)} %q_ref.3), channel_id=1, source_target_pairs={{0,64},{16,80},{32,96},{48,112},{64,0},{80,16},{96,32},{112,48},{1... | collective-permute-start | bytes 294920 | tf_op jit(solution)/shard_map/ppermute | solution.py:49
  4.3 4.6 %own_prefix.1 = (bf16[432,128]{1,0:T(8,128)(2,1)}, f32[8,128]{1,0:T(8,128)}) custom-call(s32[1]{0:T(128)} %bitcast.21.group_ref, bf16[48,1024]{1,0:T(8,128)(2,1)} %q_ref.3, bf16[2048,1024]{1,0:T(8,128)(2,1)} %k_ref.15, bf16[2048,1024]{1,0:T(8,128)(2,1)} %v_ref.15), custom_call_target="tpu_custom_call" | custom-call | flops 402653184 | bytes 1048576 | tf_op jit(solution)/shard_map/own_prefix/pallas_call | solution.py:127
  40.6 3.0 %collective-permute-start.13 = (bf16[432,128]{1,0:T(8,128)(2,1)S(1)}, bf16[432,128]{1,0:T(8,128)(2,1)S(1)}, u32[]{:S(2)}, u32[]{:S(2)}) collective-permute-start(bf16[432,128]{1,0:T(8,128)(2,1)S(1)} %prefix_part.13), channel_id=1, source_target_pairs={{0,32},{16,48},{32,0},{48,16},{64,96},{80,112},{96,64},{112,80},{1... | collective-permute-start | bytes 331784 | tf_op jit(solution)/shard_map/ppermute | solution.py:49
  45.4 2.7 %suffix_part.1 = (f32[8,48,128]{2,1,0:T(8,128)S(1)}, f32[8,48,128]{2,1,0:T(8,128)S(1)}) custom-call(bf16[48,1024]{1,0:T(8,128)(2,1)S(1)} %copy-done.4, bf16[6144,128]{1,0:T(8,128)(2,1)S(1)} %bitcast.38, bf16[6144,128]{1,0:T(8,128)(2,1)S(1)} %bitcast.39, bf16[48,128]{1,0:T(8,128)(2,1)S(1)} %copy-done.6, bf16[48,128]{1,0:T(8,128)(2,1)S(1)} %copy-done.7, ...), custom_call_target="tpu_custom_call" | custom-call | flops 402653184 | bytes 4194304 | tf_op jit(solution)/shard_map/suffix_part/pallas_call | solution.py:201
  48.1 4.1 %collective-permute-done.12.refs_6_ = bf16[432,128]{1,0:T(8,128)(2,1)S(1)} collective-permute-done((bf16[432,128]{1,0:T(8,128)(2,1)S(1)}, bf16[432,128]{1,0:T(8,128)(2,1)S(1)}, u32[]{:S(2)}, u32[]{:S(2)}) %collective-permute-start.12) | collective-permute-done | bytes 110624 | tf_op jit(solution)/shard_map/ppermute | solution.py:49
  52.2 2.8 %merge_parts.1 = bf16[8,48,1024]{2,1,0:T(8,128)(2,1)} custom-call(bf16[432,128]{1,0:T(8,128)(2,1)S(1)} %copy-done.5, bf16[432,128]{1,0:T(8,128)(2,1)S(1)} %collective-permute-done.2.refs_1_, bf16[432,128]{1,0:T(8,128)(2,1)S(1)} %collective-permute-done.6.refs_1_.refs_2_, bf16[432,128]{1,0:T(8,128)(2,1)S(1)} %collective-permute-done.7.refs_1_.refs_3_, ...), custom_call_target="tpu_custom_call" | custom-call | flops 983040 | bytes 2097152 | tf_op jit(solution)/shard_map/merge_parts/pallas_call | solution.py:244
  54.9 4.5 %all-to-all-start = ((bf16[8,48,1024]{2,1,0:T(8,128)(2,1)}), bf16[8,48,1024]{2,1,0:T(8,128)(2,1)S(1)}, u32[]{:S(2)}, u32[]{:S(2)}) async-start(bf16[8,48,1024]{2,1,0:T(8,128)(2,1)} %merge_parts.1), calls=%async_computation | async-start | bytes 1572864 | tf_op jit(solution)/shard_map/all_to_all | solution.py:562
  60.7 8.9 %all-to-all-done = bf16[8,48,1024]{2,1,0:T(8,128)(2,1)S(1)} async-done(((bf16[8,48,1024]{2,1,0:T(8,128)(2,1)}), bf16[8,48,1024]{2,1,0:T(8,128)(2,1)S(1)}, u32[]{:S(2)}, u32[]{:S(2)}) %all-to-all-start) | async-done | bytes 786464 | tf_op jit(solution)/shard_map/all_to_all | solution.py:562
  71.3 3.2 %collective-permute-start.17 = (bf16[96,1024]{1,0:T(8,128)(2,1)}, bf16[96,1024]{1,0:T(8,128)(2,1)S(1)}, u32[]{:S(2)}, u32[]{:S(2)}) collective-permute-start(bf16[96,1024]{1,0:T(8,128)(2,1)} %get-tuple-element.46), channel_id=1, source_target_pairs={{0,48},{16,0},{32,16},{48,32},{64,112},{80,64},{96,80},{112,96},{1... | collective-permute-start | bytes 589832 | tf_op jit(solution)/shard_map/ppermute | solution.py:49
  74.5 3.9 %collective-permute-done.16 = bf16[96,1024]{1,0:T(8,128)(2,1)S(1)} collective-permute-done((bf16[96,1024]{1,0:T(8,128)(2,1)}, bf16[96,1024]{1,0:T(8,128)(2,1)S(1)}, u32[]{:S(2)}, u32[]{:S(2)}) %collective-permute-start.16) | collective-permute-done | bytes 196640 | tf_op jit(solution)/shard_map/ppermute | solution.py:49
  81.8 2.4 %collective-permute-start.19 = (bf16[96,1024]{1,0:T(8,128)(2,1)S(1)}, bf16[96,1024]{1,0:T(8,128)(2,1)S(1)}, u32[]{:S(2)}, u32[]{:S(2)}) collective-permute-start(bf16[96,1024]{1,0:T(8,128)(2,1)S(1)} %add_convert_fusion.1), channel_id=1, source_target_pairs={{0,64},{16,80},{32,96},{48,112},{64,0},{80,16},{96,32},{112,48},{1... | collective-permute-start | bytes 589832 | tf_op jit(solution)/shard_map/ppermute | solution.py:49
  86.5 2.5 %collective-permute-done.19 = bf16[96,1024]{1,0:T(8,128)(2,1)S(1)} collective-permute-done((bf16[96,1024]{1,0:T(8,128)(2,1)S(1)}, bf16[96,1024]{1,0:T(8,128)(2,1)S(1)}, u32[]{:S(2)}, u32[]{:S(2)}) %collective-permute-start.19) | collective-permute-done | bytes 196640 | tf_op jit(solution)/shard_map/ppermute | solution.py:49
  92.2 5.2 %collective-permute-done.22.refs_3_ = bf16[96,1024]{1,0:T(8,128)(2,1)S(1)} collective-permute-done((bf16[96,1024]{1,0:T(8,128)(2,1)S(1)}, bf16[96,1024]{1,0:T(8,128)(2,1)S(1)}, u32[]{:S(2)}, u32[]{:S(2)}) %collective-permute-start.22) | collective-permute-done | bytes 196640 | tf_op jit(solution)/shard_map/ppermute | solution.py:49
  100.2 5.6 %hidden_y_first.1 = (bf16[96,4224]{1,0:T(8,128)(2,1)S(1)}, bf16[96,2176]{1,0:T(8,128)(2,1)S(1)}, bf16[96,2048]{1,0:T(8,128)(2,1)S(1)}, bf16[96,2048]{1,0:T(8,128...) custom-call(bf16[384,1024]{1,0:T(8,128)(2,1)S(1)} %get-tuple-element.51.s_ref, ...), custom_call_target="tpu_custom_call" | custom-call | flops 1000000000 | bytes 1000000 | tf_op jit(solution)/shard_map/hidden_y_first/pallas_call | solution.py:388
  106.4 2.7 %collective-permute-start.26 = (bf16[96,2048]{1,0:T(8,128)(2,1)S(1)}, bf16[96,2048]{1,0:T(8,128)(2,1)S(1)}, u32[]{:S(2)}, u32[]{:S(2)}) collective-permute-start(bf16[96,2048]{1,0:T(8,128)(2,1)S(1)} %get-tuple-element.55.refs_0_), channel_id=1, source_target_pairs={{0,6},{1,7},{2,0},{3,1},{4,2},{5,3},{6,4},{7,5},{8,14},{9,15},{10,... | collective-permute-start | bytes 1179656 | tf_op jit(solution)/shard_map/ppermute | solution.py:53
  109.1 4.6 %hidden_x_first.1 = (bf16[4,2,48,1536]{3,2,1,0:T(8,128)(2,1)S(1)}, bf16[4,2,48,1536]{3,2,1,0:T(8,128)(2,1)S(1)}, f32[8,128]{1,0:T(8,128)S(1)}) custom-call(bf16[384,1024]{1,0:T(8,128)(2,1)S(1)} %get-tuple-element.51.s_ref, bf16[512,3584]{1,0:T(8,128)(2,1)} %g0.3, bf16[512,3584]{1,0:T(8,128)(2,1)} %collective-permute-done.3.g1, bf16[512,3584]{1,0:T(8,128)(2,1)} %u0.3, ...), custom_call_target="tpu_custom_call" | custom-call | flops 100000000 | bytes 100000 | tf_op jit(solution)/shard_map/hidden_x_first/pallas_call | solution.py:388
  113.7 3.4 %collective-permute-start.24 = (bf16[4,2,48,1536]{3,2,1,0:T(8,128)(2,1)S(1)}, bf16[4,2,48,1536]{3,2,1,0:T(8,128)(2,1)S(1)}, u32[]{:S(2)}, u32[]{:S(2)}) collective-permute-start(bf16[4,2,48,1536]{3,2,1,0:T(8,128)(2,1)S(1)} %get-tuple-element.57), channel_id=1, source_target_pairs={{0,8},{1,9},{2,10},{3,11},{4,12},{5,13},{6,14},{7,15},{8,0},{9,1},... | collective-permute-start | bytes 3538952 | tf_op jit(solution)/shard_map/ppermute | solution.py:53
  117.4 3.2 %collective-permute-start.28 = (bf16[96,4224]{1,0:T(8,128)(2,1)S(1)}, bf16[96,4224]{1,0:T(8,128)(2,1)S(1)}, u32[]{:S(2)}, u32[]{:S(2)}) collective-permute-start(bf16[96,4224]{1,0:T(8,128)(2,1)S(1)} %get-tuple-element.66), channel_id=1, source_target_pairs={{0,6},{1,7},{2,0},{3,1},{4,2},{5,3},{6,4},{7,5},{8,14},{9,15},{10,... | collective-permute-start | bytes 2433032 | tf_op jit(solution)/shard_map/ppermute | solution.py:53
  123.8 12.1 %collective-permute-done.27.below_ref = bf16[96,4224]{1,0:T(8,128)(2,1)S(1)} collective-permute-done((bf16[96,4224]{1,0:T(8,128)(2,1)S(1)}, bf16[96,4224]{1,0:T(8,128)(2,1)S(1)}, u32[]{:S(2)}, u32[]{:S(2)}) %collective-permute-start.27) | collective-permute-done | bytes 811040 | tf_op jit(solution)/shard_map/ppermute | solution.py:53
  136.2 3.0 %collective-permute-start.32 = (bf16[48,4224]{1,0:T(8,128)(2,1)S(1)}, bf16[48,4224]{1,0:T(8,128)(2,1)S(1)}, u32[]{:S(2)}, u32[]{:S(2)}) collective-permute-start(bf16[48,4224]{1,0:T(8,128)(2,1)S(1)} %get-tuple-element.68._), channel_id=1, source_target_pairs={{0,8},{1,9},{2,10},{3,11},{4,12},{5,13},{6,14},{7,15},{8,0},{9,1},... | collective-permute-start | bytes 1216520 | tf_op jit(solution)/shard_map/ppermute | solution.py:53
  139.2 4.7 %collective-permute-done.24.got_ref = bf16[4,2,48,1536]{3,2,1,0:T(8,128)(2,1)S(1)} collective-permute-done((bf16[4,2,48,1536]{3,2,1,0:T(8,128)(2,1)S(1)}, bf16[4,2,48,1536]{3,2,1,0:T(8,128)(2,1)S(1)}, u32[]{:S(2)}, u32[]{:S(2)}) %collective-permute-start.24) | collective-permute-done | bytes 1179680 | tf_op jit(solution)/shard_map/ppermute | solution.py:53
  144.4 3.2 %collective-permute-start.31 = (bf16[2,48,1536]{2,1,0:T(8,128)(2,1)S(1)}, bf16[2,48,1536]{2,1,0:T(8,128)(2,1)S(1)}, u32[]{:S(2)}, u32[]{:S(2)}) collective-permute-start(bf16[2,48,1536]{2,1,0:T(8,128)(2,1)S(1)} %get-tuple-element.72), channel_id=1, source_target_pairs={{0,6},{1,7},{2,0},{3,1},{4,2},{5,3},{6,4},{7,5},{8,14},{9,15},{10,... | collective-permute-start | bytes 884744 | tf_op jit(solution)/shard_map/ppermute | solution.py:53
  149.7 2.9 %collective-permute-done.29.refs_0_ = bf16[2,48,1536]{2,1,0:T(8,128)(2,1)S(1)} collective-permute-done((bf16[2,48,1536]{2,1,0:T(8,128)(2,1)S(1)}, bf16[2,48,1536]{2,1,0:T(8,128)(2,1)S(1)}, u32[]{:S(2)}, u32[]{:S(2)}) %collective-permute-start.29) | collective-permute-done | bytes 294944 | tf_op jit(solution)/shard_map/ppermute | solution.py:53
  152.6 2.8 %collective-permute-done.30.refs_1_ = bf16[2,48,1536]{2,1,0:T(8,128)(2,1)S(1)} collective-permute-done((bf16[2,48,1536]{2,1,0:T(8,128)(2,1)S(1)}, bf16[2,48,1536]{2,1,0:T(8,128)(2,1)S(1)}, u32[]{:S(2)}, u32[]{:S(2)}) %collective-permute-start.30) | collective-permute-done | bytes 294944 | tf_op jit(solution)/shard_map/ppermute | solution.py:53
  (95 shorter events, 56.5 us)
Async XLA Ops:
  0.6 15.1 %collective-permute-start.3 = (bf16[512,3584]{1,0:T(8,128)(2,1)}, bf16[512,3584]{1,0:T(8,128)(2,1)}, u32[]{:S(2)}, u32[]{:S(2)}) collective-permute-start(bf16[512,3584]{1,0:T(8,128)(2,1)} %g0.3), channel_id=1, source_target_pairs={{0,1},{1,0},{2,3},{3,2},{4,5},{5,4},{6,7},{7,6},{8,9},{9,8},{10,11... | collective-permute-start | bytes 11010056 | tf_op jit(solution)/shard_map/ppermute | solution.py:53
  0.7 21.0 %collective-permute-start.4 = (bf16[512,3584]{1,0:T(8,128)(2,1)}, bf16[512,3584]{1,0:T(8,128)(2,1)}, u32[]{:S(2)}, u32[]{:S(2)}) collective-permute-start(bf16[512,3584]{1,0:T(8,128)(2,1)} %u0.3), channel_id=1, source_target_pairs={{0,1},{1,0},{2,3},{3,2},{4,5},{5,4},{6,7},{7,6},{8,9},{9,8},{10,11... | collective-permute-start | bytes 11010056 | tf_op jit(solution)/shard_map/ppermute | solution.py:53
  9.7 13.9 %collective-permute-start.5 = (bf16[2,48,1024]{2,1,0:T(8,128)(2,1)S(1)}, bf16[2,48,1024]{2,1,0:T(8,128)(2,1)S(1)}, u32[]{:S(2)}, u32[]{:S(2)}) collective-permute-start(bf16[2,48,1024]{2,1,0:T(8,128)(2,1)S(1)} %pair_up.1), channel_id=1, source_target_pairs={{0,16},{16,32},{32,48},{48,0},{64,80},{80,96},{96,112},{112,64},{1... | collective-permute-start | bytes 589832 | tf_op jit(solution)/shard_map/ppermute | solution.py:49
  11.7 17.2 %collective-permute-start.8 = (bf16[2,48,1024]{2,1,0:T(8,128)(2,1)S(1)}, bf16[2,48,1024]{2,1,0:T(8,128)(2,1)S(1)}, u32[]{:S(2)}, u32[]{:S(2)}) collective-permute-start(bf16[2,48,1024]{2,1,0:T(8,128)(2,1)S(1)} %pair_up.1), channel_id=1, source_target_pairs={{0,48},{16,0},{32,16},{48,32},{64,112},{80,64},{96,80},{112,96},{1... | collective-permute-start | bytes 589832 | tf_op jit(solution)/shard_map/ppermute | solution.py:49
  13.9 21.9 %collective-permute-start.11 = (bf16[2,48,1024]{2,1,0:T(8,128)(2,1)S(1)}, bf16[2,48,1024]{2,1,0:T(8,128)(2,1)S(1)}, u32[]{:S(2)}, u32[]{:S(2)}) collective-permute-start(bf16[2,48,1024]{2,1,0:T(8,128)(2,1)S(1)} %pair_up.1), channel_id=1, source_target_pairs={{0,32},{16,48},{32,0},{48,16},{64,96},{80,112},{96,64},{112,80},{1... | collective-permute-start | bytes 589832 | tf_op jit(solution)/shard_map/ppermute | solution.py:49
  15.7 45.0 %collective-permute-start.14 = (bf16[1024,512]{1,0:T(8,128)(2,1)S(1)}, bf16[1024,512]{1,0:T(8,128)(2,1)S(1)}, u32[]{:S(2)}, u32[]{:S(2)}) collective-permute-start(bf16[1024,512]{1,0:T(8,128)(2,1)S(1)} %copy-done.9), channel_id=1, source_target_pairs={{0,1},{1,0},{2,3},{3,2},{4,5},{5,4},{6,7},{7,6},{8,9},{9,8},{10,11... | collective-permute-start | bytes 3145736 | tf_op jit(solution)/shard_map/ppermute | solution.py:53
  21.7 10.4 %collective-permute-start.2 = (bf16[432,128]{1,0:T(8,128)(2,1)S(1)}, bf16[432,128]{1,0:T(8,128)(2,1)S(1)}, u32[]{:S(2)}, u32[]{:S(2)}) collective-permute-start(bf16[432,128]{1,0:T(8,128)(2,1)S(1)} %prefix_part.7.refs_0_), channel_id=1, source_target_pairs={{0,64},{16,80},{32,96},{48,112},{64,0},{80,16},{96,32},{112,48},{1... | collective-permute-start | bytes 331784 | tf_op jit(solution)/shard_map/ppermute | solution.py:49
  25.3 11.8 %collective-permute-start.6 = (bf16[432,128]{1,0:T(8,128)(2,1)S(1)}, bf16[432,128]{1,0:T(8,128)(2,1)S(1)}, u32[]{:S(2)}, u32[]{:S(2)}) collective-permute-start(bf16[432,128]{1,0:T(8,128)(2,1)S(1)} %prefix_part.8.refs_0_), channel_id=1, source_target_pairs={{0,112},{16,64},{32,80},{48,96},{64,48},{80,0},{96,16},{112,32},{1... | collective-permute-start | bytes 331784 | tf_op jit(solution)/shard_map/ppermute | solution.py:49
  28.9 9.9 %collective-permute-start.7 = (bf16[432,128]{1,0:T(8,128)(2,1)S(1)}, bf16[432,128]{1,0:T(8,128)(2,1)S(1)}, u32[]{:S(2)}, u32[]{:S(2)}) collective-permute-start(bf16[432,128]{1,0:T(8,128)(2,1)S(1)} %prefix_part.9.refs_0_), channel_id=1, source_target_pairs={{0,48},{16,0},{32,16},{48,32},{64,112},{80,64},{96,80},{112,96},{1... | collective-permute-start | bytes 331784 | tf_op jit(solution)/shard_map/ppermute | solution.py:49
  32.2 15.9 %collective-permute-start.9 = (bf16[432,128]{1,0:T(8,128)(2,1)S(1)}, bf16[432,128]{1,0:T(8,128)(2,1)S(1)}, u32[]{:S(2)}, u32[]{:S(2)}) collective-permute-start(bf16[432,128]{1,0:T(8,128)(2,1)S(1)} %prefix_part.10.refs_0_), channel_id=1, source_target_pairs={{0,80},{16,96},{32,112},{48,64},{64,16},{80,32},{96,48},{112,0},{1... | collective-permute-start | bytes 331784 | tf_op jit(solution)/shard_map/ppermute | solution.py:49
  35.8 12.3 %collective-permute-start.10 = (bf16[432,128]{1,0:T(8,128)(2,1)S(1)}, bf16[432,128]{1,0:T(8,128)(2,1)S(1)}, u32[]{:S(2)}, u32[]{:S(2)}) collective-permute-start(bf16[432,128]{1,0:T(8,128)(2,1)S(1)} %prefix_part.11.refs_0_), channel_id=1, source_target_pairs={{0,16},{16,32},{32,48},{48,0},{64,80},{80,96},{96,112},{112,64},{1... | collective-permute-start | bytes 331784 | tf_op jit(solution)/shard_map/ppermute | solution.py:49
  43.5 8.7 %collective-permute-start.12 = (bf16[432,128]{1,0:T(8,128)(2,1)S(1)}, bf16[432,128]{1,0:T(8,128)(2,1)S(1)}, u32[]{:S(2)}, u32[]{:S(2)}) collective-permute-start(bf16[432,128]{1,0:T(8,128)(2,1)S(1)} %prefix_part.12.refs_0_), channel_id=1, source_target_pairs={{0,96},{16,112},{32,64},{48,80},{64,32},{80,48},{96,0},{112,16},{1... | collective-permute-start | bytes 331784 | tf_op jit(solution)/shard_map/ppermute | solution.py:49
  54.9 14.7 %all-to-all-start = ((bf16[8,48,1024]{2,1,0:T(8,128)(2,1)}), bf16[8,48,1024]{2,1,0:T(8,128)(2,1)S(1)}, u32[]{:S(2)}, u32[]{:S(2)}) async-start(bf16[8,48,1024]{2,1,0:T(8,128)(2,1)} %merge_parts.1), calls=%async_computation | async-start | bytes 1572864 | tf_op jit(solution)/shard_map/all_to_all | solution.py:562
  71.3 8.8 %collective-permute-start.17 = (bf16[96,1024]{1,0:T(8,128)(2,1)}, bf16[96,1024]{1,0:T(8,128)(2,1)S(1)}, u32[]{:S(2)}, u32[]{:S(2)}) collective-permute-start(bf16[96,1024]{1,0:T(8,128)(2,1)} %get-tuple-element.46), channel_id=1, source_target_pairs={{0,48},{16,0},{32,16},{48,32},{64,112},{80,64},{96,80},{112,96},{1... | collective-permute-start | bytes 589832 | tf_op jit(solution)/shard_map/ppermute | solution.py:49
  89.2 9.6 %collective-permute-start.21 = (bf16[96,1024]{1,0:T(8,128)(2,1)S(1)}, bf16[96,1024]{1,0:T(8,128)(2,1)S(1)}, u32[]{:S(2)}, u32[]{:S(2)}) collective-permute-start(bf16[96,1024]{1,0:T(8,128)(2,1)S(1)} %add_convert_fusion.refs_0_), channel_id=1, source_target_pairs={{0,48},{16,0},{32,16},{48,32},{64,112},{80,64},{96,80},{112,96},{1... | collective-permute-start | bytes 589832 | tf_op jit(solution)/shard_map/ppermute | solution.py:49
  105.8 11.3 %collective-permute-start.25 = (bf16[96,2176]{1,0:T(8,128)(2,1)S(1)}, bf16[96,2176]{1,0:T(8,128)(2,1)S(1)}, u32[]{:S(2)}, u32[]{:S(2)}) collective-permute-start(bf16[96,2176]{1,0:T(8,128)(2,1)S(1)} %get-tuple-element.63), channel_id=1, source_target_pairs={{0,2},{1,3},{2,4},{3,5},{4,6},{5,7},{6,0},{7,1},{8,10},{9,11},{10,... | collective-permute-start | bytes 1253384 | tf_op jit(solution)/shard_map/ppermute | solution.py:53
  106.4 10.7 %collective-permute-start.26 = (bf16[96,2048]{1,0:T(8,128)(2,1)S(1)}, bf16[96,2048]{1,0:T(8,128)(2,1)S(1)}, u32[]{:S(2)}, u32[]{:S(2)}) collective-permute-start(bf16[96,2048]{1,0:T(8,128)(2,1)S(1)} %get-tuple-element.55.refs_0_), channel_id=1, source_target_pairs={{0,6},{1,7},{2,0},{3,1},{4,2},{5,3},{6,4},{7,5},{8,14},{9,15},{10,... | collective-permute-start | bytes 1179656 | tf_op jit(solution)/shard_map/ppermute | solution.py:53
  113.7 30.2 %collective-permute-start.24 = (bf16[4,2,48,1536]{3,2,1,0:T(8,128)(2,1)S(1)}, bf16[4,2,48,1536]{3,2,1,0:T(8,128)(2,1)S(1)}, u32[]{:S(2)}, u32[]{:S(2)}) collective-permute-start(bf16[4,2,48,1536]{3,2,1,0:T(8,128)(2,1)S(1)} %get-tuple-element.57), channel_id=1, source_target_pairs={{0,8},{1,9},{2,10},{3,11},{4,12},{5,13},{6,14},{7,15},{8,0},{9,1},... | collective-permute-start | bytes 3538952 | tf_op jit(solution)/shard_map/ppermute | solution.py:53
  117.3 18.6 %collective-permute-start.27 = (bf16[96,4224]{1,0:T(8,128)(2,1)S(1)}, bf16[96,4224]{1,0:T(8,128)(2,1)S(1)}, u32[]{:S(2)}, u32[]{:S(2)}) collective-permute-start(bf16[96,4224]{1,0:T(8,128)(2,1)S(1)} %get-tuple-element.65), channel_id=1, source_target_pairs={{0,2},{1,3},{2,4},{3,5},{4,6},{5,7},{6,0},{7,1},{8,10},{9,11},{10,... | collective-permute-start | bytes 2433032 | tf_op jit(solution)/shard_map/ppermute | solution.py:53
  117.4 18.5 %collective-permute-start.28 = (bf16[96,4224]{1,0:T(8,128)(2,1)S(1)}, bf16[96,4224]{1,0:T(8,128)(2,1)S(1)}, u32[]{:S(2)}, u32[]{:S(2)}) collective-permute-start(bf16[96,4224]{1,0:T(8,128)(2,1)S(1)} %get-tuple-element.66), channel_id=1, source_target_pairs={{0,6},{1,7},{2,0},{3,1},{4,2},{5,3},{6,4},{7,5},{8,14},{9,15},{10,... | collective-permute-start | bytes 2433032 | tf_op jit(solution)/shard_map/ppermute | solution.py:53
  136.2 13.3 %collective-permute-start.32 = (bf16[48,4224]{1,0:T(8,128)(2,1)S(1)}, bf16[48,4224]{1,0:T(8,128)(2,1)S(1)}, u32[]{:S(2)}, u32[]{:S(2)}) collective-permute-start(bf16[48,4224]{1,0:T(8,128)(2,1)S(1)} %get-tuple-element.68._), channel_id=1, source_target_pairs={{0,8},{1,9},{2,10},{3,11},{4,12},{5,13},{6,14},{7,15},{8,0},{9,1},... | collective-permute-start | bytes 1216520 | tf_op jit(solution)/shard_map/ppermute | solution.py:53
  144.2 8.4 %collective-permute-start.29 = (bf16[2,48,1536]{2,1,0:T(8,128)(2,1)S(1)}, bf16[2,48,1536]{2,1,0:T(8,128)(2,1)S(1)}, u32[]{:S(2)}, u32[]{:S(2)}) collective-permute-start(bf16[2,48,1536]{2,1,0:T(8,128)(2,1)S(1)} %get-tuple-element.70), channel_id=1, source_target_pairs={{0,4},{1,5},{2,6},{3,7},{4,0},{5,1},{6,2},{7,3},{8,12},{9,13},{10,... | collective-permute-start | bytes 884744 | tf_op jit(solution)/shard_map/ppermute | solution.py:53
  144.3 11.2 %collective-permute-start.30 = (bf16[2,48,1536]{2,1,0:T(8,128)(2,1)S(1)}, bf16[2,48,1536]{2,1,0:T(8,128)(2,1)S(1)}, u32[]{:S(2)}, u32[]{:S(2)}) collective-permute-start(bf16[2,48,1536]{2,1,0:T(8,128)(2,1)S(1)} %get-tuple-element.71), channel_id=1, source_target_pairs={{0,2},{1,3},{2,4},{3,5},{4,6},{5,7},{6,0},{7,1},{8,10},{9,11},{10,... | collective-permute-start | bytes 884744 | tf_op jit(solution)/shard_map/ppermute | solution.py:53
  144.4 11.1 %collective-permute-start.31 = (bf16[2,48,1536]{2,1,0:T(8,128)(2,1)S(1)}, bf16[2,48,1536]{2,1,0:T(8,128)(2,1)S(1)}, u32[]{:S(2)}, u32[]{:S(2)}) collective-permute-start(bf16[2,48,1536]{2,1,0:T(8,128)(2,1)S(1)} %get-tuple-element.72), channel_id=1, source_target_pairs={{0,6},{1,7},{2,0},{3,1},{4,2},{5,3},{6,4},{7,5},{8,14},{9,15},{10,... | collective-permute-start | bytes 884744 | tf_op jit(solution)/shard_map/ppermute | solution.py:53
  (22 other events, 143.0 us)

commit v4 on v3

--- a/solution.py
+++ b/solution.py
@@ -19,10 +19,9 @@
 PRE = 2048
 HALF = 512
 HIDDEN = 3584
-A_COLS = 1536
+A_COLS = 1408
 B_COLS = HIDDEN - A_COLS
-A_TILE = 512
-B_TILE = 512
+TILE = 512
 SAME_CORE = [list(range(0, 16, 2)), list(range(1, 16, 2))]
 BF = jnp.bfloat16
 F32 = jnp.float32
@@ -332,18 +331,33 @@
     )(place, *pieces, theirs)
 
 
-def weight_tiles(first, columns, tile, weights, held, sems):
-    copies = []
-    tiles = columns // tile
-    for t in range(tiles):
-        at = slice(first + t * tile, first + (t + 1) * tile)
-        copies.append([pltpu.make_async_copy(w.at[:, at], held.at[t, i], sems.at[t, i]) for i, w in enumerate(weights)])
-        for copy in copies[t]:
-            copy.start()
-    for t in range(tiles):
-        for copy in copies[t]:
-            copy.wait()
-        yield t, [held[t, i] for i in range(4)]
+def hold_kernel(_, *refs):
+    sources, places, sems = refs[:4], refs[4:8], refs[8]
+    copies = [pltpu.make_async_copy(a, b, sems.at[i]) for i, (a, b) in enumerate(zip(sources, places))]
+    for copy in copies:
+        copy.start()
+    for copy in copies:
+        copy.wait()
+
+
+def hold(after, *arrays):
+    return pl.pallas_call(
+        hold_kernel,
+        in_specs=[pl.BlockSpec()] + [pl.BlockSpec(memory_space=pl.ANY)] * 4,
+        out_specs=[pl.BlockSpec(memory_space=pltpu.VMEM)] * 4,
+        out_shape=[jax.ShapeDtypeStruct(a.shape, a.dtype) for a in arrays],
+        scratch_shapes=[pltpu.SemaphoreType.DMA((4,))],
+        compiler_params=pltpu.CompilerParams(vmem_limit_bytes=24 << 20),
+        cost_estimate=pl.CostEstimate(flops=0, bytes_accessed=sum(a.size * 4 for a in arrays), transcendentals=0),
+        name="hold_weights",
+    )(after, *arrays)
+
+
+def weight_tiles(first, columns, weights):
+    ends = range(columns % TILE or TILE, columns + 1, TILE)
+    for end in ends:
+        at = slice(max(end - TILE, 0), end)
+        yield at, [w[:, first + at.start : first + at.stop] for w in weights]
 
 
 def hidden_sums(s, own_gate, other_gate, own_up, other_up):
@@ -355,10 +369,9 @@
 
 
 def x_first_kernel(first, columns, s_ref, g0, g1, u0, u1, *refs):
-    keep_ref, send_ref, token_ref, held, sems = refs[-5:]
+    keep_ref, send_ref, token_ref = refs[-3:]
     token_ref[...] = jnp.zeros_like(token_ref)
-    for t, blocks in weight_tiles(first, columns, A_TILE, (g0, g1, u0, u1), held, sems):
-        to = slice(t * A_TILE, (t + 1) * A_TILE)
+    for to, blocks in weight_tiles(first, columns, (g0, g1, u0, u1)):
         for n, y in enumerate(hidden_sums(s_ref[...], *blocks)):
             for k in range(4):
                 keep_ref[k, n, :, to] = y[k * ROWS : (k + 1) * ROWS].astype(BF)
@@ -366,7 +379,7 @@
 
 
 def y_first_kernel(first, columns, s_ref, g0, g1, u0, u1, squares_ref, *refs):
-    here_ref, up_add, up_pass, down_add, down_pass, far_gate, far_up, held, sems = refs
+    here_ref, up_add, up_pass, down_add, down_pass, far_gate, far_up = refs
     up, down, far = (up_add, up_pass), (down_pass, down_add), (far_gate, far_up)
 
     def put(n, to, y):
@@ -378,19 +391,17 @@
                 ref[at, to] = value.astype(BF)
 
     put(0, slice(columns, columns + HD), squares_ref[...])
-    for t, blocks in weight_tiles(first, columns, B_TILE, (g0, g1, u0, u1), held, sems):
+    for to, blocks in weight_tiles(first, columns, (g0, g1, u0, u1)):
         for n, y in enumerate(hidden_sums(s_ref[...], *blocks)):
-            put(n, slice(t * B_TILE, (t + 1) * B_TILE), y)
-
-
-def hidden_call(kernel, first, columns, tile, scaled, weights, shapes, flops, name, more):
-    tiles = columns // tile
+            put(n, to, y)
+
+
+def hidden_call(kernel, first, columns, scaled, weights, shapes, flops, name, more):
     return pl.pallas_call(
         functools.partial(kernel, first, columns),
-        in_specs=[pl.BlockSpec()] + [pl.BlockSpec(memory_space=pl.ANY)] * 4 + [pl.BlockSpec()] * len(more),
+        in_specs=[pl.BlockSpec()] + [pl.BlockSpec(memory_space=pltpu.VMEM)] * 4 + [pl.BlockSpec()] * len(more),
         out_shape=shapes,
-        scratch_shapes=[pltpu.VMEM((tiles, 4, HALF, tile), BF), pltpu.SemaphoreType.DMA((tiles, 4))],
-        compiler_params=pltpu.CompilerParams(vmem_limit_bytes=48 << 20),
+        compiler_params=pltpu.CompilerParams(vmem_limit_bytes=12 << 20),
         cost_estimate=pl.CostEstimate(flops=flops, bytes_accessed=flops // 1000, transcendentals=0),
         name=name,
     )(scaled, *weights, *more)
@@ -399,7 +410,7 @@
 def x_first(first, columns, scaled, weights, *after):
     shapes = [jax.ShapeDtypeStruct((4, 2, ROWS, columns), BF)] * 2 + [jax.ShapeDtypeStruct((8, HD), F32)]
     return hidden_call(
-        x_first_kernel, first, columns, A_TILE, scaled, weights, shapes, 10**8, "hidden_x_first", after
+        x_first_kernel, first, columns, scaled, weights, shapes, 10**8, "hidden_x_first", after
     )
 
 
@@ -408,7 +419,7 @@
     parts = [gate + columns, gate, columns, columns, gate, gate, columns]
     shapes = [jax.ShapeDtypeStruct((rows, n), BF) for n in parts]
     return hidden_call(
-        y_first_kernel, first, columns, B_TILE, scaled, weights, shapes, 10**9, "hidden_y_first", (squares,)
+        y_first_kernel, first, columns, scaled, weights, shapes, 10**9, "hidden_y_first", (squares,)
     )
 
 
@@ -583,7 +594,7 @@
     place = [(block // 4 - xl) % 2 * 4 + (block % 4 - y) % 4 for block in blocks] + blocks + [core]
     place = jnp.stack(place).astype(jnp.int32)
     scaled, squares, their_columns = fill(place, pieces, gain)
-    weights = (gate_weight, other_gate, up_weight, other_up)
+    weights = hold(chunk, gate_weight, other_gate, up_weight, other_up)
     b_first = y_first(A_COLS, B_COLS, scaled, weights, squares)
     a_first = x_first(0, A_COLS, scaled, weights, b_first[-1])
     received = y_sums(*b_first[1:], a_first[2])

time: 157 us -> 154 us (0.981)
  waiting for transfers between devices: 58.5 us -> 46.7 us
  starting transfers between devices: 52.7 us -> 57.6 us
  local copies, waits for them, and re-layouts: 6.22 us -> 10.3 us
    ppermute x18, waiting for transfers between devices: 21 us -> 13.8 us  [over_ctx(): return lax.ppermute(v, 'ctx', ctx_perm(flip, s))]
    ppermute x15, waiting for transfers between devices: 28.6 us -> 23.9 us  [over_batch(): return lax.ppermute(v, 'batch', batch_perm(flip_x, s, flip_core))]
    ppermute x15, starting transfers between devices: 17.1 us -> 21.4 us  [over_batch(): return lax.ppermute(v, 'batch', batch_perm(flip_x, s, flip_core))]
    unnamed x24 -> x28, local copies, waits for them, and re-layouts: 5.1 us -> 9.17 us
    pallas_call x2, Pallas kernels: 10.2 us -> 6.42 us  [hidden_call(): pl.pallas_call(functools.partial(kernel, first, columns), in_specs=[pl.Bl...]
    pallas_call x0 -> x1, Pallas kernels: none -> 3.5 us  [hold(): pl.pallas_call(hold_kernel, in_specs=[pl.BlockSpec()] + [pl.BlockSpec(mem...]
  transfers between devices with their start and end apart: 34 -> 34, of which waited for: 17 -> 15; matrix products, arithmetic and copies ran while one was open for 1% -> 1% of each run, Pallas kernels for 18% -> 20%
where the time goes in v4:
time: 154 us; the launch traced here: 153 us
  starting transfers between devices  57.6 us (37%)
  waiting for transfers between devices  46.7 us (30%)
  Pallas kernels  37.8 us (25%)
  local copies, waits for them, and re-layouts  10.3 us (7%)
    ppermute x18, starting transfers between devices, over_ctx(): return lax.ppermute(v, 'ctx', ctx_perm(flip, s))  31.7 us
    ppermute x15, waiting for transfers between devices, over_batch(): return lax.ppermute(v, 'batch', batch_perm(flip_x, s, flip_core))  23.9 us
    ppermute x15, starting transfers between devices, over_batch(): return lax.ppermute(v, 'batch', batch_perm(flip_x, s, flip_core))  21.4 us
    ppermute x18, waiting for transfers between devices, over_ctx(): return lax.ppermute(v, 'ctx', ctx_perm(flip, s))  13.8 us
    pallas_call x7, Pallas kernels, prefix_part(): pl.pallas_call(functools.partial(prefix_kernel, which), in_specs=[pl.Bloc...  11.7 us
    unnamed x28, local copies, waits for them, and re-layouts  9.17 us
    all_to_all x1, waiting for transfers between devices, on_device(): lax.all_to_all(attended, 'batch', 0, 0, axis_index_groups=SAME_CORE, tile...  8.9 us
    pallas_call x2, Pallas kernels, hidden_call(): pl.pallas_call(functools.partial(kernel, first, columns), in_specs=[pl.Bl...  6.42 us
  transfers between devices with their start and end apart: 34, of which 15 were waited for; matrix products, arithmetic and copies ran while one was open for 1% of the time, Pallas kernels for 20%

profile of v4, /device:TPU:0, one launch (start us, length us, event | category | flops | bytes accessed | tf_op | source)
XLA Modules:
  0.0 153.4 jit_solution(16124520063007406271)
XLA Ops:
  1.2 3.1 %collective-permute-start.1 = (bf16[48,1024]{1,0:T(8,128)(2,1)}, bf16[48,1024]{1,0:T(8,128)(2,1)S(1)}, u32[]{:S(2)}, u32[]{:S(2)}) collective-permute-start(bf16[48,1024]{1,0:T(8,128)(2,1)} %q_ref.3), channel_id=1, source_target_pairs={{0,64},{16,80},{32,96},{48,112},{64,0},{80,16},{96,32},{112,48},{1... | collective-permute-start | bytes 294920 | tf_op jit(solution)/shard_map/ppermute | solution.py:48
  4.3 4.6 %own_prefix.1 = (bf16[432,128]{1,0:T(8,128)(2,1)}, f32[8,128]{1,0:T(8,128)}) custom-call(s32[1]{0:T(128)} %bitcast.21.group_ref, bf16[48,1024]{1,0:T(8,128)(2,1)} %q_ref.3, bf16[2048,1024]{1,0:T(8,128)(2,1)} %k_ref.15, bf16[2048,1024]{1,0:T(8,128)(2,1)} %v_ref.15), custom_call_target="tpu_custom_call" | custom-call | flops 402653184 | bytes 1048576 | tf_op jit(solution)/shard_map/own_prefix/pallas_call | solution.py:126
  11.7 2.2 %collective-permute-start.8 = (bf16[2,48,1024]{2,1,0:T(8,128)(2,1)S(1)}, bf16[2,48,1024]{2,1,0:T(8,128)(2,1)S(1)}, u32[]{:S(2)}, u32[]{:S(2)}) collective-permute-start(bf16[2,48,1024]{2,1,0:T(8,128)(2,1)S(1)} %pair_up.1), channel_id=1, source_target_pairs={{0,48},{16,0},{32,16},{48,32},{64,112},{80,64},{96,80},{112,96},{1... | collective-permute-start | bytes 589832 | tf_op jit(solution)/shard_map/ppermute | solution.py:48
  40.6 3.0 %collective-permute-start.13 = (bf16[432,128]{1,0:T(8,128)(2,1)S(1)}, bf16[432,128]{1,0:T(8,128)(2,1)S(1)}, u32[]{:S(2)}, u32[]{:S(2)}) collective-permute-start(bf16[432,128]{1,0:T(8,128)(2,1)S(1)} %prefix_part.13), channel_id=1, source_target_pairs={{0,32},{16,48},{32,0},{48,16},{64,96},{80,112},{96,64},{112,80},{1... | collective-permute-start | bytes 331784 | tf_op jit(solution)/shard_map/ppermute | solution.py:48
  45.4 2.7 %suffix_part.1 = (f32[8,48,128]{2,1,0:T(8,128)S(1)}, f32[8,48,128]{2,1,0:T(8,128)S(1)}) custom-call(bf16[48,1024]{1,0:T(8,128)(2,1)S(1)} %copy-done.6, bf16[6144,128]{1,0:T(8,128)(2,1)S(1)} %bitcast.38, bf16[6144,128]{1,0:T(8,128)(2,1)S(1)} %bitcast.39, bf16[48,128]{1,0:T(8,128)(2,1)S(1)} %copy-done.8, bf16[48,128]{1,0:T(8,128)(2,1)S(1)} %copy-done.9, ...), custom_call_target="tpu_custom_call" | custom-call | flops 402653184 | bytes 4194304 | tf_op jit(solution)/shard_map/suffix_part/pallas_call | solution.py:200
  48.1 4.1 %collective-permute-done.12.refs_6_ = bf16[432,128]{1,0:T(8,128)(2,1)S(1)} collective-permute-done((bf16[432,128]{1,0:T(8,128)(2,1)S(1)}, bf16[432,128]{1,0:T(8,128)(2,1)S(1)}, u32[]{:S(2)}, u32[]{:S(2)}) %collective-permute-start.12) | collective-permute-done | bytes 110624 | tf_op jit(solution)/shard_map/ppermute | solution.py:48
  52.2 2.8 %merge_parts.1 = bf16[8,48,1024]{2,1,0:T(8,128)(2,1)} custom-call(bf16[432,128]{1,0:T(8,128)(2,1)S(1)} %copy-done.7, bf16[432,128]{1,0:T(8,128)(2,1)S(1)} %collective-permute-done.2.refs_1_, bf16[432,128]{1,0:T(8,128)(2,1)S(1)} %collective-permute-done.6.refs_1_.refs_2_, bf16[432,128]{1,0:T(8,128)(2,1)S(1)} %collective-permute-done.7.refs_1_.refs_3_, ...), custom_call_target="tpu_custom_call" | custom-call | flops 983040 | bytes 2097152 | tf_op jit(solution)/shard_map/merge_parts/pallas_call | solution.py:243
  54.9 4.5 %all-to-all-start = ((bf16[8,48,1024]{2,1,0:T(8,128)(2,1)}), bf16[8,48,1024]{2,1,0:T(8,128)(2,1)S(1)}, u32[]{:S(2)}, u32[]{:S(2)}) async-start(bf16[8,48,1024]{2,1,0:T(8,128)(2,1)} %merge_parts.1), calls=%async_computation | async-start | bytes 1572864 | tf_op jit(solution)/shard_map/all_to_all | solution.py:573
  60.7 8.9 %all-to-all-done = bf16[8,48,1024]{2,1,0:T(8,128)(2,1)S(1)} async-done(((bf16[8,48,1024]{2,1,0:T(8,128)(2,1)}), bf16[8,48,1024]{2,1,0:T(8,128)(2,1)S(1)}, u32[]{:S(2)}, u32[]{:S(2)}) %all-to-all-start) | async-done | bytes 786464 | tf_op jit(solution)/shard_map/all_to_all | solution.py:573
  71.3 3.2 %collective-permute-start.17 = (bf16[96,1024]{1,0:T(8,128)(2,1)}, bf16[96,1024]{1,0:T(8,128)(2,1)S(1)}, u32[]{:S(2)}, u32[]{:S(2)}) collective-permute-start(bf16[96,1024]{1,0:T(8,128)(2,1)} %get-tuple-element.50), channel_id=1, source_target_pairs={{0,48},{16,0},{32,16},{48,32},{64,112},{80,64},{96,80},{112,96},{1... | collective-permute-start | bytes 589832 | tf_op jit(solution)/shard_map/ppermute | solution.py:48
  74.5 3.9 %collective-permute-done.16 = bf16[96,1024]{1,0:T(8,128)(2,1)S(1)} collective-permute-done((bf16[96,1024]{1,0:T(8,128)(2,1)}, bf16[96,1024]{1,0:T(8,128)(2,1)S(1)}, u32[]{:S(2)}, u32[]{:S(2)}) %collective-permute-start.16) | collective-permute-done | bytes 196640 | tf_op jit(solution)/shard_map/ppermute | solution.py:48
  81.8 2.4 %collective-permute-start.19 = (bf16[96,1024]{1,0:T(8,128)(2,1)S(1)}, bf16[96,1024]{1,0:T(8,128)(2,1)S(1)}, u32[]{:S(2)}, u32[]{:S(2)}) collective-permute-start(bf16[96,1024]{1,0:T(8,128)(2,1)S(1)} %add_convert_fusion.1), channel_id=1, source_target_pairs={{0,64},{16,80},{32,96},{48,112},{64,0},{80,16},{96,32},{112,48},{1... | collective-permute-start | bytes 589832 | tf_op jit(solution)/shard_map/ppermute | solution.py:48
  86.5 2.5 %collective-permute-done.19 = bf16[96,1024]{1,0:T(8,128)(2,1)S(1)} collective-permute-done((bf16[96,1024]{1,0:T(8,128)(2,1)S(1)}, bf16[96,1024]{1,0:T(8,128)(2,1)S(1)}, u32[]{:S(2)}, u32[]{:S(2)}) %collective-permute-start.19) | collective-permute-done | bytes 196640 | tf_op jit(solution)/shard_map/ppermute | solution.py:48
  89.2 3.2 %collective-permute-start.21 = (bf16[96,1024]{1,0:T(8,128)(2,1)S(1)}, bf16[96,1024]{1,0:T(8,128)(2,1)S(1)}, u32[]{:S(2)}, u32[]{:S(2)}) collective-permute-start(bf16[96,1024]{1,0:T(8,128)(2,1)S(1)} %add_convert_fusion.refs_0_._), channel_id=1, source_target_pairs={{0,48},{16,0},{32,16},{48,32},{64,112},{80,64},{96,80},{112,96},{1... | collective-permute-start | bytes 589832 | tf_op jit(solution)/shard_map/ppermute | solution.py:48
  96.9 3.5 %hold_weights.1 = (bf16[512,3584]{1,0:T(8,128)(2,1)S(1)}, bf16[512,3584]{1,0:T(8,128)(2,1)S(1)}, bf16[512,3584]{1,0:T(8,128)(2,1)S(1)}, bf16[512,3584]{1,0:T(8,128)(2,1)S(1)}) custom-call(bf16[96,1024]{1,0:T(8,128)(2,1)S(1)} %add_convert_fusion.refs_0_._, bf16[512,3584]{1,0:T(8,128)(2,1)S(1)} %copy-done.2, bf16[512,3584]{1,0:T(8,128)(2,1)} %collective-permute-done.3.refs_1_, ...), custom_call_target="tpu_custom_call" | custom-call | bytes 29360128 | tf_op jit(solution)/shard_map/hold_weights/pallas_call | solution.py:344
  101.3 3.8 %hidden_y_first.1 = (bf16[96,4480]{1,0:T(8,128)(2,1)S(1)}, bf16[96,2304]{1,0:T(8,128)(2,1)S(1)}, bf16[96,2176]{1,0:T(8,128)(2,1)S(1)}, bf16[96,2176]{1,0:T(8,128...) custom-call(bf16[384,1024]{1,0:T(8,128)(2,1)S(1)} %get-tuple-element.55.s_ref, ...), custom_call_target="tpu_custom_call" | custom-call | flops 1000000000 | bytes 1000000 | tf_op jit(solution)/shard_map/hidden_y_first/pallas_call | solution.py:400
  105.7 2.7 %collective-permute-start.26 = (bf16[96,2176]{1,0:T(8,128)(2,1)S(1)}, bf16[96,2176]{1,0:T(8,128)(2,1)S(1)}, u32[]{:S(2)}, u32[]{:S(2)}) collective-permute-start(bf16[96,2176]{1,0:T(8,128)(2,1)S(1)} %get-tuple-element.63.refs_0_), channel_id=1, source_target_pairs={{0,6},{1,7},{2,0},{3,1},{4,2},{5,3},{6,4},{7,5},{8,14},{9,15},{10,... | collective-permute-start | bytes 1253384 | tf_op jit(solution)/shard_map/ppermute | solution.py:52
  108.4 2.6 %hidden_x_first.1 = (bf16[4,2,48,1408]{3,2,1,0:T(8,128)(2,1)S(1)}, bf16[4,2,48,1408]{3,2,1,0:T(8,128)(2,1)S(1)}, f32[8,128]{1,0:T(8,128)S(1)}) custom-call(bf16[384,1024]{1,0:T(8,128)(2,1)S(1)} %get-tuple-element.55.s_ref, bf16[512,3584]{1,0:T(8,128)(2,1)S(1)} %get-tuple-element.58.g0, bf16[512,3584]{1,0:T(8,128)(2,1)S(1)} %get-tuple-element.59.g1, ...), custom_call_target="tpu_custom_call" | custom-call | flops 100000000 | bytes 100000 | tf_op jit(solution)/shard_map/hidden_x_first/pallas_call | solution.py:400
  111.0 3.8 %collective-permute-start.24 = (bf16[4,2,48,1408]{3,2,1,0:T(8,128)(2,1)S(1)}, bf16[4,2,48,1408]{3,2,1,0:T(8,128)(2,1)S(1)}, u32[]{:S(2)}, u32[]{:S(2)}) collective-permute-start(bf16[4,2,48,1408]{3,2,1,0:T(8,128)(2,1)S(1)} %get-tuple-element.65), channel_id=1, source_target_pairs={{0,8},{1,9},{2,10},{3,11},{4,12},{5,13},{6,14},{7,15},{8,0},{9,1},... | collective-permute-start | bytes 3244040 | tf_op jit(solution)/shard_map/ppermute | solution.py:52
  115.8 3.2 %collective-permute-start.28 = (bf16[96,4480]{1,0:T(8,128)(2,1)S(1)}, bf16[96,4480]{1,0:T(8,128)(2,1)S(1)}, u32[]{:S(2)}, u32[]{:S(2)}) collective-permute-start(bf16[96,4480]{1,0:T(8,128)(2,1)S(1)} %get-tuple-element.74), channel_id=1, source_target_pairs={{0,6},{1,7},{2,0},{3,1},{4,2},{5,3},{6,4},{7,5},{8,14},{9,15},{10,... | collective-permute-start | bytes 2580488 | tf_op jit(solution)/shard_map/ppermute | solution.py:52
  122.3 11.9 %collective-permute-done.27.below_ref = bf16[96,4480]{1,0:T(8,128)(2,1)S(1)} collective-permute-done((bf16[96,4480]{1,0:T(8,128)(2,1)S(1)}, bf16[96,4480]{1,0:T(8,128)(2,1)S(1)}, u32[]{:S(2)}, u32[]{:S(2)}) %collective-permute-start.27) | collective-permute-done | bytes 860192 | tf_op jit(solution)/shard_map/ppermute | solution.py:52
  134.5 5.6 %collective-permute-start.32 = (bf16[48,4480]{1,0:T(8,128)(2,1)S(1)}, bf16[48,4480]{1,0:T(8,128)(2,1)S(1)}, u32[]{:S(2)}, u32[]{:S(2)}) collective-permute-start(bf16[48,4480]{1,0:T(8,128)(2,1)S(1)} %get-tuple-element.76._), channel_id=1, source_target_pairs={{0,8},{1,9},{2,10},{3,11},{4,12},{5,13},{6,14},{7,15},{8,0},{9,1},... | collective-permute-start | bytes 1290248 | tf_op jit(solution)/shard_map/ppermute | solution.py:52
  141.4 3.6 %collective-permute-start.30 = (bf16[2,48,1408]{2,1,0:T(8,128)(2,1)S(1)}, bf16[2,48,1408]{2,1,0:T(8,128)(2,1)S(1)}, u32[]{:S(2)}, u32[]{:S(2)}) collective-permute-start(bf16[2,48,1408]{2,1,0:T(8,128)(2,1)S(1)} %get-tuple-element.79), channel_id=1, source_target_pairs={{0,2},{1,3},{2,4},{3,5},{4,6},{5,7},{6,0},{7,1},{8,10},{9,11},{10,... | collective-permute-start | bytes 811016 | tf_op jit(solution)/shard_map/ppermute | solution.py:52
  148.6 2.8 %collective-permute-done.30.refs_1_ = bf16[2,48,1408]{2,1,0:T(8,128)(2,1)S(1)} collective-permute-done((bf16[2,48,1408]{2,1,0:T(8,128)(2,1)S(1)}, bf16[2,48,1408]{2,1,0:T(8,128)(2,1)S(1)}, u32[]{:S(2)}, u32[]{:S(2)}) %collective-permute-start.30) | collective-permute-done | bytes 270368 | tf_op jit(solution)/shard_map/ppermute | solution.py:52
  (100 shorter events, 57.8 us)
Async XLA Ops:
  0.6 15.1 %collective-permute-start.3 = (bf16[512,3584]{1,0:T(8,128)(2,1)}, bf16[512,3584]{1,0:T(8,128)(2,1)}, u32[]{:S(2)}, u32[]{:S(2)}) collective-permute-start(bf16[512,3584]{1,0:T(8,128)(2,1)} %refs_0_.1), channel_id=1, source_target_pairs={{0,1},{1,0},{2,3},{3,2},{4,5},{5,4},{6,7},{7,6},{8,9},{9,8},{10,11... | collective-permute-start | bytes 11010056 | tf_op jit(solution)/shard_map/ppermute | solution.py:52
  0.7 21.0 %collective-permute-start.4 = (bf16[512,3584]{1,0:T(8,128)(2,1)}, bf16[512,3584]{1,0:T(8,128)(2,1)}, u32[]{:S(2)}, u32[]{:S(2)}) collective-permute-start(bf16[512,3584]{1,0:T(8,128)(2,1)} %refs_2_.1), channel_id=1, source_target_pairs={{0,1},{1,0},{2,3},{3,2},{4,5},{5,4},{6,7},{7,6},{8,9},{9,8},{10,11... | collective-permute-start | bytes 11010056 | tf_op jit(solution)/shard_map/ppermute | solution.py:52
  9.7 13.9 %collective-permute-start.5 = (bf16[2,48,1024]{2,1,0:T(8,128)(2,1)S(1)}, bf16[2,48,1024]{2,1,0:T(8,128)(2,1)S(1)}, u32[]{:S(2)}, u32[]{:S(2)}) collective-permute-start(bf16[2,48,1024]{2,1,0:T(8,128)(2,1)S(1)} %pair_up.1), channel_id=1, source_target_pairs={{0,16},{16,32},{32,48},{48,0},{64,80},{80,96},{96,112},{112,64},{1... | collective-permute-start | bytes 589832 | tf_op jit(solution)/shard_map/ppermute | solution.py:48
  11.7 17.2 %collective-permute-start.8 = (bf16[2,48,1024]{2,1,0:T(8,128)(2,1)S(1)}, bf16[2,48,1024]{2,1,0:T(8,128)(2,1)S(1)}, u32[]{:S(2)}, u32[]{:S(2)}) collective-permute-start(bf16[2,48,1024]{2,1,0:T(8,128)(2,1)S(1)} %pair_up.1), channel_id=1, source_target_pairs={{0,48},{16,0},{32,16},{48,32},{64,112},{80,64},{96,80},{112,96},{1... | collective-permute-start | bytes 589832 | tf_op jit(solution)/shard_map/ppermute | solution.py:48
  13.9 21.9 %collective-permute-start.11 = (bf16[2,48,1024]{2,1,0:T(8,128)(2,1)S(1)}, bf16[2,48,1024]{2,1,0:T(8,128)(2,1)S(1)}, u32[]{:S(2)}, u32[]{:S(2)}) collective-permute-start(bf16[2,48,1024]{2,1,0:T(8,128)(2,1)S(1)} %pair_up.1), channel_id=1, source_target_pairs={{0,32},{16,48},{32,0},{48,16},{64,96},{80,112},{96,64},{112,80},{1... | collective-permute-start | bytes 589832 | tf_op jit(solution)/shard_map/ppermute | solution.py:48
  15.7 45.0 %collective-permute-start.14 = (bf16[1024,512]{1,0:T(8,128)(2,1)S(1)}, bf16[1024,512]{1,0:T(8,128)(2,1)S(1)}, u32[]{:S(2)}, u32[]{:S(2)}) collective-permute-start(bf16[1024,512]{1,0:T(8,128)(2,1)S(1)} %copy-done.11), channel_id=1, source_target_pairs={{0,1},{1,0},{2,3},{3,2},{4,5},{5,4},{6,7},{7,6},{8,9},{9,8},{10,11... | collective-permute-start | bytes 3145736 | tf_op jit(solution)/shard_map/ppermute | solution.py:52
  21.7 10.4 %collective-permute-start.2 = (bf16[432,128]{1,0:T(8,128)(2,1)S(1)}, bf16[432,128]{1,0:T(8,128)(2,1)S(1)}, u32[]{:S(2)}, u32[]{:S(2)}) collective-permute-start(bf16[432,128]{1,0:T(8,128)(2,1)S(1)} %prefix_part.7.refs_0_), channel_id=1, source_target_pairs={{0,64},{16,80},{32,96},{48,112},{64,0},{80,16},{96,32},{112,48},{1... | collective-permute-start | bytes 331784 | tf_op jit(solution)/shard_map/ppermute | solution.py:48
  25.3 11.8 %collective-permute-start.6 = (bf16[432,128]{1,0:T(8,128)(2,1)S(1)}, bf16[432,128]{1,0:T(8,128)(2,1)S(1)}, u32[]{:S(2)}, u32[]{:S(2)}) collective-permute-start(bf16[432,128]{1,0:T(8,128)(2,1)S(1)} %prefix_part.8.refs_0_), channel_id=1, source_target_pairs={{0,112},{16,64},{32,80},{48,96},{64,48},{80,0},{96,16},{112,32},{1... | collective-permute-start | bytes 331784 | tf_op jit(solution)/shard_map/ppermute | solution.py:48
  28.9 9.9 %collective-permute-start.7 = (bf16[432,128]{1,0:T(8,128)(2,1)S(1)}, bf16[432,128]{1,0:T(8,128)(2,1)S(1)}, u32[]{:S(2)}, u32[]{:S(2)}) collective-permute-start(bf16[432,128]{1,0:T(8,128)(2,1)S(1)} %prefix_part.9.refs_0_), channel_id=1, source_target_pairs={{0,48},{16,0},{32,16},{48,32},{64,112},{80,64},{96,80},{112,96},{1... | collective-permute-start | bytes 331784 | tf_op jit(solution)/shard_map/ppermute | solution.py:48
  32.2 15.9 %collective-permute-start.9 = (bf16[432,128]{1,0:T(8,128)(2,1)S(1)}, bf16[432,128]{1,0:T(8,128)(2,1)S(1)}, u32[]{:S(2)}, u32[]{:S(2)}) collective-permute-start(bf16[432,128]{1,0:T(8,128)(2,1)S(1)} %prefix_part.10.refs_0_), channel_id=1, source_target_pairs={{0,80},{16,96},{32,112},{48,64},{64,16},{80,32},{96,48},{112,0},{1... | collective-permute-start | bytes 331784 | tf_op jit(solution)/shard_map/ppermute | solution.py:48
  35.8 12.3 %collective-permute-start.10 = (bf16[432,128]{1,0:T(8,128)(2,1)S(1)}, bf16[432,128]{1,0:T(8,128)(2,1)S(1)}, u32[]{:S(2)}, u32[]{:S(2)}) collective-permute-start(bf16[432,128]{1,0:T(8,128)(2,1)S(1)} %prefix_part.11.refs_0_), channel_id=1, source_target_pairs={{0,16},{16,32},{32,48},{48,0},{64,80},{80,96},{96,112},{112,64},{1... | collective-permute-start | bytes 331784 | tf_op jit(solution)/shard_map/ppermute | solution.py:48
  43.5 8.7 %collective-permute-start.12 = (bf16[432,128]{1,0:T(8,128)(2,1)S(1)}, bf16[432,128]{1,0:T(8,128)(2,1)S(1)}, u32[]{:S(2)}, u32[]{:S(2)}) collective-permute-start(bf16[432,128]{1,0:T(8,128)(2,1)S(1)} %prefix_part.12.refs_0_), channel_id=1, source_target_pairs={{0,96},{16,112},{32,64},{48,80},{64,32},{80,48},{96,0},{112,16},{1... | collective-permute-start | bytes 331784 | tf_op jit(solution)/shard_map/ppermute | solution.py:48
  54.9 14.7 %all-to-all-start = ((bf16[8,48,1024]{2,1,0:T(8,128)(2,1)}), bf16[8,48,1024]{2,1,0:T(8,128)(2,1)S(1)}, u32[]{:S(2)}, u32[]{:S(2)}) async-start(bf16[8,48,1024]{2,1,0:T(8,128)(2,1)} %merge_parts.1), calls=%async_computation | async-start | bytes 1572864 | tf_op jit(solution)/shard_map/all_to_all | solution.py:573
  71.3 8.8 %collective-permute-start.17 = (bf16[96,1024]{1,0:T(8,128)(2,1)}, bf16[96,1024]{1,0:T(8,128)(2,1)S(1)}, u32[]{:S(2)}, u32[]{:S(2)}) collective-permute-start(bf16[96,1024]{1,0:T(8,128)(2,1)} %get-tuple-element.50), channel_id=1, source_target_pairs={{0,48},{16,0},{32,16},{48,32},{64,112},{80,64},{96,80},{112,96},{1... | collective-permute-start | bytes 589832 | tf_op jit(solution)/shard_map/ppermute | solution.py:48
  89.1 11.2 %collective-permute-start.20 = (bf16[96,1024]{1,0:T(8,128)(2,1)S(1)}, bf16[96,1024]{1,0:T(8,128)(2,1)S(1)}, u32[]{:S(2)}, u32[]{:S(2)}) collective-permute-start(bf16[96,1024]{1,0:T(8,128)(2,1)S(1)} %add_convert_fusion.refs_0_._), channel_id=1, source_target_pairs={{0,16},{16,32},{32,48},{48,0},{64,80},{80,96},{96,112},{112,64},{1... | collective-permute-start | bytes 589832 | tf_op jit(solution)/shard_map/ppermute | solution.py:48
  89.2 11.2 %collective-permute-start.21 = (bf16[96,1024]{1,0:T(8,128)(2,1)S(1)}, bf16[96,1024]{1,0:T(8,128)(2,1)S(1)}, u32[]{:S(2)}, u32[]{:S(2)}) collective-permute-start(bf16[96,1024]{1,0:T(8,128)(2,1)S(1)} %add_convert_fusion.refs_0_._), channel_id=1, source_target_pairs={{0,48},{16,0},{32,16},{48,32},{64,112},{80,64},{96,80},{112,96},{1... | collective-permute-start | bytes 589832 | tf_op jit(solution)/shard_map/ppermute | solution.py:48
  105.1 10.4 %collective-permute-start.25 = (bf16[96,2304]{1,0:T(8,128)(2,1)S(1)}, bf16[96,2304]{1,0:T(8,128)(2,1)S(1)}, u32[]{:S(2)}, u32[]{:S(2)}) collective-permute-start(bf16[96,2304]{1,0:T(8,128)(2,1)S(1)} %get-tuple-element.71), channel_id=1, source_target_pairs={{0,2},{1,3},{2,4},{3,5},{4,6},{5,7},{6,0},{7,1},{8,10},{9,11},{10,... | collective-permute-start | bytes 1327112 | tf_op jit(solution)/shard_map/ppermute | solution.py:52
  105.7 9.1 %collective-permute-start.26 = (bf16[96,2176]{1,0:T(8,128)(2,1)S(1)}, bf16[96,2176]{1,0:T(8,128)(2,1)S(1)}, u32[]{:S(2)}, u32[]{:S(2)}) collective-permute-start(bf16[96,2176]{1,0:T(8,128)(2,1)S(1)} %get-tuple-element.63.refs_0_), channel_id=1, source_target_pairs={{0,6},{1,7},{2,0},{3,1},{4,2},{5,3},{6,4},{7,5},{8,14},{9,15},{10,... | collective-permute-start | bytes 1253384 | tf_op jit(solution)/shard_map/ppermute | solution.py:52
  111.0 29.1 %collective-permute-start.24 = (bf16[4,2,48,1408]{3,2,1,0:T(8,128)(2,1)S(1)}, bf16[4,2,48,1408]{3,2,1,0:T(8,128)(2,1)S(1)}, u32[]{:S(2)}, u32[]{:S(2)}) collective-permute-start(bf16[4,2,48,1408]{3,2,1,0:T(8,128)(2,1)S(1)} %get-tuple-element.65), channel_id=1, source_target_pairs={{0,8},{1,9},{2,10},{3,11},{4,12},{5,13},{6,14},{7,15},{8,0},{9,1},... | collective-permute-start | bytes 3244040 | tf_op jit(solution)/shard_map/ppermute | solution.py:52
  115.7 18.5 %collective-permute-start.27 = (bf16[96,4480]{1,0:T(8,128)(2,1)S(1)}, bf16[96,4480]{1,0:T(8,128)(2,1)S(1)}, u32[]{:S(2)}, u32[]{:S(2)}) collective-permute-start(bf16[96,4480]{1,0:T(8,128)(2,1)S(1)} %get-tuple-element.73), channel_id=1, source_target_pairs={{0,2},{1,3},{2,4},{3,5},{4,6},{5,7},{6,0},{7,1},{8,10},{9,11},{10,... | collective-permute-start | bytes 2580488 | tf_op jit(solution)/shard_map/ppermute | solution.py:52
  115.8 18.4 %collective-permute-start.28 = (bf16[96,4480]{1,0:T(8,128)(2,1)S(1)}, bf16[96,4480]{1,0:T(8,128)(2,1)S(1)}, u32[]{:S(2)}, u32[]{:S(2)}) collective-permute-start(bf16[96,4480]{1,0:T(8,128)(2,1)S(1)} %get-tuple-element.74), channel_id=1, source_target_pairs={{0,6},{1,7},{2,0},{3,1},{4,2},{5,3},{6,4},{7,5},{8,14},{9,15},{10,... | collective-permute-start | bytes 2580488 | tf_op jit(solution)/shard_map/ppermute | solution.py:52
  134.5 11.8 %collective-permute-start.32 = (bf16[48,4480]{1,0:T(8,128)(2,1)S(1)}, bf16[48,4480]{1,0:T(8,128)(2,1)S(1)}, u32[]{:S(2)}, u32[]{:S(2)}) collective-permute-start(bf16[48,4480]{1,0:T(8,128)(2,1)S(1)} %get-tuple-element.76._), channel_id=1, source_target_pairs={{0,8},{1,9},{2,10},{3,11},{4,12},{5,13},{6,14},{7,15},{8,0},{9,1},... | collective-permute-start | bytes 1290248 | tf_op jit(solution)/shard_map/ppermute | solution.py:52
  140.4 8.1 %collective-permute-start.29 = (bf16[2,48,1408]{2,1,0:T(8,128)(2,1)S(1)}, bf16[2,48,1408]{2,1,0:T(8,128)(2,1)S(1)}, u32[]{:S(2)}, u32[]{:S(2)}) collective-permute-start(bf16[2,48,1408]{2,1,0:T(8,128)(2,1)S(1)} %get-tuple-element.78), channel_id=1, source_target_pairs={{0,4},{1,5},{2,6},{3,7},{4,0},{5,1},{6,2},{7,3},{8,12},{9,13},{10,... | collective-permute-start | bytes 811016 | tf_op jit(solution)/shard_map/ppermute | solution.py:52
  141.4 9.9 %collective-permute-start.30 = (bf16[2,48,1408]{2,1,0:T(8,128)(2,1)S(1)}, bf16[2,48,1408]{2,1,0:T(8,128)(2,1)S(1)}, u32[]{:S(2)}, u32[]{:S(2)}) collective-permute-start(bf16[2,48,1408]{2,1,0:T(8,128)(2,1)S(1)} %get-tuple-element.79), channel_id=1, source_target_pairs={{0,2},{1,3},{2,4},{3,5},{4,6},{5,7},{6,0},{7,1},{8,10},{9,11},{10,... | collective-permute-start | bytes 811016 | tf_op jit(solution)/shard_map/ppermute | solution.py:52
  (24 other events, 146.3 us)

commit v5 on v4

--- a/solution.py
+++ b/solution.py
@@ -19,7 +19,7 @@
 PRE = 2048
 HALF = 512
 HIDDEN = 3584
-A_COLS = 1408
+A_COLS = 1536
 B_COLS = HIDDEN - A_COLS
 TILE = 512
 SAME_CORE = [list(range(0, 16, 2)), list(range(1, 16, 2))]
@@ -423,41 +423,39 @@
     )
 
 
-def pass_on_kernel(up_add, up_pass, down_add, down_pass, below, above, _, to_above, to_below):
-    gate = up_add.shape[1]
-    to_above[:, :gate] = (up_add[...].astype(F32) + below[...].astype(F32)).astype(BF)
-    to_above[:, gate:] = up_pass[...]
-    to_below[:, :gate] = down_pass[...]
-    to_below[:, gate:] = (down_add[...].astype(F32) + above[...].astype(F32)).astype(BF)
+def pass_on_kernel(up_add, down_add, below, above, _, to_above, to_below):
+    to_above[...] = (up_add[...].astype(F32) + below[...].astype(F32)).astype(BF)
+    to_below[...] = (down_add[...].astype(F32) + above[...].astype(F32)).astype(BF)
 
 
 def pass_on(*sums):
-    shape = jax.ShapeDtypeStruct((2 * ROWS, sums[0].shape[1] + sums[1].shape[1]), BF)
+    shapes = [jax.ShapeDtypeStruct(v.shape, BF) for v in sums[:2]]
     return pl.pallas_call(
         pass_on_kernel,
-        out_shape=[shape, shape],
+        out_shape=shapes,
         compiler_params=pltpu.CompilerParams(vmem_limit_bytes=VMEM),
         cost_estimate=pl.CostEstimate(flops=1000, bytes_accessed=1000, transcendentals=0),
         name="pass_on_sums",
     )(*sums)
 
 
-def finish_kernel(here_ref, below_ref, above_ref, _, keep_ref, send_ref):
-    sums = here_ref[...].astype(F32) + below_ref[...].astype(F32) + above_ref[...].astype(F32)
-    keep_ref[...] = sums[:ROWS]
-    send_ref[...] = sums[ROWS:].astype(BF)
-
-
-def finish_y(here, below, above, after):
+def finish_kernel(here_ref, below_gate, below_up, above_gate, above_up, _, keep_ref, send_ref):
+    gate = below_gate.shape[1]
+    for at, below, above in ((slice(0, gate), below_gate, above_gate), (slice(gate, None), below_up, above_up)):
+        sums = here_ref[:, at].astype(F32) + below[...].astype(F32) + above[...].astype(F32)
+        keep_ref[:, at] = sums[:ROWS]
+        send_ref[:, at] = sums[ROWS:].astype(BF)
+
+
+def finish_y(here, received, after):
     shape = lambda t: jax.ShapeDtypeStruct((ROWS, here.shape[1]), t)
     return pl.pallas_call(
         finish_kernel,
-        in_specs=[pl.BlockSpec()] * 4,
         out_shape=[shape(F32), shape(BF)],
         compiler_params=pltpu.CompilerParams(vmem_limit_bytes=VMEM),
         cost_estimate=pl.CostEstimate(flops=1000, bytes_accessed=1000, transcendentals=0),
         name="finish_y",
-    )(here, below, above, after)
+    )(here, *received, after)
 
 
 def add_kernel(keep_ref, got_ref, _, mine_ref, *send_refs):
@@ -519,8 +517,10 @@
 def y_sums(up_add, up_pass, down_add, down_pass, far_gate, far_up, token):
     from_below = over_batch(far_gate, 0, 1)
     from_above = over_batch(far_up, 0, -1)
-    to_above, to_below = pass_on(up_add, up_pass, down_add, down_pass, from_below, from_above, token)
-    return over_batch(to_above, 0, 1), over_batch(to_below, 0, -1)
+    gate_above, up_below = pass_on(up_add, down_add, from_below, from_above, token)
+    above = over_batch(gate_above, 0, 1), over_batch(up_pass, 0, 1)
+    below = over_batch(down_pass, 0, -1), over_batch(up_below, 0, -1)
+    return (*above, *below)
 
 
 def on_device(
@@ -599,7 +599,7 @@
     a_first = x_first(0, A_COLS, scaled, weights, b_first[-1])
     received = y_sums(*b_first[1:], a_first[2])
     stream, token = assemble(place, pieces, over_batch(their_columns, 0, 0, 1))
-    b_keep, b_send = finish_y(b_first[0], *received, token)
+    b_keep, b_send = finish_y(b_first[0], received, token)
     b_part, rms = finish_b(b_keep, over_batch(b_send, 1, 0))
     mine, *sends = add_got(a_first[0], over_batch(a_first[1], 1, 0), b_send)
     activation = finish_a(mine, [over_batch(sends[s - 1], 0, s) for s in (2, 1, 3)], b_part, rms)

time: 154 us -> 153 us (level)
  starting transfers between devices: 57.6 us -> 53.5 us
  waiting for transfers between devices: 46.7 us -> 50 us
    ppermute x15 -> x17, starting transfers between devices: 21.4 us -> 17.3 us  [over_batch(): return lax.ppermute(v, 'batch', batch_perm(flip_x, s, flip_core))]
    ppermute x15 -> x17, waiting for transfers between devices: 23.9 us -> 27.2 us  [over_batch(): return lax.ppermute(v, 'batch', batch_perm(flip_x, s, flip_core))]
  transfers between devices with their start and end apart: 34 -> 36, of which waited for: 15 -> 13; matrix products, arithmetic and copies ran while one was open for 1% -> 1% of each run, Pallas kernels for 20% -> 18%
where the time goes in v5:
time: 153 us; the launch traced here: 152 us
  starting transfers between devices  53.5 us (35%)
  waiting for transfers between devices  50 us (33%)
  Pallas kernels  37.3 us (24%)
  local copies, waits for them, and re-layouts  10.3 us (7%)
    ppermute x18, starting transfers between devices, over_ctx(): return lax.ppermute(v, 'ctx', ctx_perm(flip, s))  31.7 us
    ppermute x17, waiting for transfers between devices, over_batch(): return lax.ppermute(v, 'batch', batch_perm(flip_x, s, flip_core))  27.2 us
    ppermute x17, starting transfers between devices, over_batch(): return lax.ppermute(v, 'batch', batch_perm(flip_x, s, flip_core))  17.3 us
    ppermute x18, waiting for transfers between devices, over_ctx(): return lax.ppermute(v, 'ctx', ctx_perm(flip, s))  13.8 us
    pallas_call x7, Pallas kernels, prefix_part(): pl.pallas_call(functools.partial(prefix_kernel, which), in_specs=[pl.Bloc...  11.7 us
    unnamed x28, local copies, waits for them, and re-layouts  9.17 us
    all_to_all x1, waiting for transfers between devices, on_device(): lax.all_to_all(attended, 'batch', 0, 0, axis_index_groups=SAME_CORE, tile...  8.9 us
    pallas_call x2, Pallas kernels, hidden_call(): pl.pallas_call(functools.partial(kernel, first, columns), in_specs=[pl.Bl...  6 us
  transfers between devices with their start and end apart: 36, of which 13 were waited for; matrix products, arithmetic and copies ran while one was open for 1% of the time, Pallas kernels for 18%

profile of v5, /device:TPU:0, one launch (start us, length us, event | category | flops | bytes accessed | tf_op | source)
XLA Modules:
  0.0 152.2 jit_solution(15183336196035928386)
XLA Ops:
  1.2 3.1 %collective-permute-start.1 = (bf16[48,1024]{1,0:T(8,128)(2,1)}, bf16[48,1024]{1,0:T(8,128)(2,1)S(1)}, u32[]{:S(2)}, u32[]{:S(2)}) collective-permute-start(bf16[48,1024]{1,0:T(8,128)(2,1)} %q_ref.3), channel_id=1, source_target_pairs={{0,64},{16,80},{32,96},{48,112},{64,0},{80,16},{96,32},{112,48},{1... | collective-permute-start | bytes 294920 | tf_op jit(solution)/shard_map/ppermute | solution.py:48
  4.3 4.6 %own_prefix.1 = (bf16[432,128]{1,0:T(8,128)(2,1)}, f32[8,128]{1,0:T(8,128)}) custom-call(s32[1]{0:T(128)} %bitcast.21.group_ref, bf16[48,1024]{1,0:T(8,128)(2,1)} %q_ref.3, bf16[2048,1024]{1,0:T(8,128)(2,1)} %k_ref.15, bf16[2048,1024]{1,0:T(8,128)(2,1)} %v_ref.15), custom_call_target="tpu_custom_call" | custom-call | flops 402653184 | bytes 1048576 | tf_op jit(solution)/shard_map/own_prefix/pallas_call | solution.py:126
  11.7 2.2 %collective-permute-start.8 = (bf16[2,48,1024]{2,1,0:T(8,128)(2,1)S(1)}, bf16[2,48,1024]{2,1,0:T(8,128)(2,1)S(1)}, u32[]{:S(2)}, u32[]{:S(2)}) collective-permute-start(bf16[2,48,1024]{2,1,0:T(8,128)(2,1)S(1)} %pair_up.1), channel_id=1, source_target_pairs={{0,48},{16,0},{32,16},{48,32},{64,112},{80,64},{96,80},{112,96},{1... | collective-permute-start | bytes 589832 | tf_op jit(solution)/shard_map/ppermute | solution.py:48
  17.9 2.2 %copy-done.1 = bf16[2048,1024]{1,0:T(8,128)(2,1)S(1)} copy-done((bf16[2048,1024]{1,0:T(8,128)(2,1)S(1)}, bf16[2048,1024]{1,0:T(8,128)(2,1)}, u32[]{:S(2)}) %copy-start.1) | copy-done | bytes 4194328
  40.6 3.0 %collective-permute-start.13 = (bf16[432,128]{1,0:T(8,128)(2,1)S(1)}, bf16[432,128]{1,0:T(8,128)(2,1)S(1)}, u32[]{:S(2)}, u32[]{:S(2)}) collective-permute-start(bf16[432,128]{1,0:T(8,128)(2,1)S(1)} %prefix_part.13), channel_id=1, source_target_pairs={{0,32},{16,48},{32,0},{48,16},{64,96},{80,112},{96,64},{112,80},{1... | collective-permute-start | bytes 331784 | tf_op jit(solution)/shard_map/ppermute | solution.py:48
  45.4 2.7 %suffix_part.1 = (f32[8,48,128]{2,1,0:T(8,128)S(1)}, f32[8,48,128]{2,1,0:T(8,128)S(1)}) custom-call(bf16[48,1024]{1,0:T(8,128)(2,1)S(1)} %copy-done.6, bf16[6144,128]{1,0:T(8,128)(2,1)S(1)} %bitcast.38, bf16[6144,128]{1,0:T(8,128)(2,1)S(1)} %bitcast.39, bf16[48,128]{1,0:T(8,128)(2,1)S(1)} %copy-done.8, bf16[48,128]{1,0:T(8,128)(2,1)S(1)} %copy-done.9, ...), custom_call_target="tpu_custom_call" | custom-call | flops 402653184 | bytes 4194304 | tf_op jit(solution)/shard_map/suffix_part/pallas_call | solution.py:200
  48.1 4.1 %collective-permute-done.12.refs_6_ = bf16[432,128]{1,0:T(8,128)(2,1)S(1)} collective-permute-done((bf16[432,128]{1,0:T(8,128)(2,1)S(1)}, bf16[432,128]{1,0:T(8,128)(2,1)S(1)}, u32[]{:S(2)}, u32[]{:S(2)}) %collective-permute-start.12) | collective-permute-done | bytes 110624 | tf_op jit(solution)/shard_map/ppermute | solution.py:48
  52.2 2.8 %merge_parts.1 = bf16[8,48,1024]{2,1,0:T(8,128)(2,1)} custom-call(bf16[432,128]{1,0:T(8,128)(2,1)S(1)} %copy-done.7, bf16[432,128]{1,0:T(8,128)(2,1)S(1)} %collective-permute-done.2.refs_1_, bf16[432,128]{1,0:T(8,128)(2,1)S(1)} %collective-permute-done.6.refs_1_.refs_2_, bf16[432,128]{1,0:T(8,128)(2,1)S(1)} %collective-permute-done.7.refs_1_.refs_3_, ...), custom_call_target="tpu_custom_call" | custom-call | flops 983040 | bytes 2097152 | tf_op jit(solution)/shard_map/merge_parts/pallas_call | solution.py:243
  54.9 4.5 %all-to-all-start = ((bf16[8,48,1024]{2,1,0:T(8,128)(2,1)}), bf16[8,48,1024]{2,1,0:T(8,128)(2,1)S(1)}, u32[]{:S(2)}, u32[]{:S(2)}) async-start(bf16[8,48,1024]{2,1,0:T(8,128)(2,1)} %merge_parts.1), calls=%async_computation | async-start | bytes 1572864 | tf_op jit(solution)/shard_map/all_to_all | solution.py:573
  60.7 8.9 %all-to-all-done = bf16[8,48,1024]{2,1,0:T(8,128)(2,1)S(1)} async-done(((bf16[8,48,1024]{2,1,0:T(8,128)(2,1)}), bf16[8,48,1024]{2,1,0:T(8,128)(2,1)S(1)}, u32[]{:S(2)}, u32[]{:S(2)}) %all-to-all-start) | async-done | bytes 786464 | tf_op jit(solution)/shard_map/all_to_all | solution.py:573
  71.3 3.2 %collective-permute-start.17 = (bf16[96,1024]{1,0:T(8,128)(2,1)}, bf16[96,1024]{1,0:T(8,128)(2,1)S(1)}, u32[]{:S(2)}, u32[]{:S(2)}) collective-permute-start(bf16[96,1024]{1,0:T(8,128)(2,1)} %get-tuple-element.50), channel_id=1, source_target_pairs={{0,48},{16,0},{32,16},{48,32},{64,112},{80,64},{96,80},{112,96},{1... | collective-permute-start | bytes 589832 | tf_op jit(solution)/shard_map/ppermute | solution.py:48
  74.5 3.9 %collective-permute-done.16 = bf16[96,1024]{1,0:T(8,128)(2,1)S(1)} collective-permute-done((bf16[96,1024]{1,0:T(8,128)(2,1)}, bf16[96,1024]{1,0:T(8,128)(2,1)S(1)}, u32[]{:S(2)}, u32[]{:S(2)}) %collective-permute-start.16) | collective-permute-done | bytes 196640 | tf_op jit(solution)/shard_map/ppermute | solution.py:48
  81.8 2.4 %collective-permute-start.19 = (bf16[96,1024]{1,0:T(8,128)(2,1)S(1)}, bf16[96,1024]{1,0:T(8,128)(2,1)S(1)}, u32[]{:S(2)}, u32[]{:S(2)}) collective-permute-start(bf16[96,1024]{1,0:T(8,128)(2,1)S(1)} %add_convert_fusion.1), channel_id=1, source_target_pairs={{0,64},{16,80},{32,96},{48,112},{64,0},{80,16},{96,32},{112,48},{1... | collective-permute-start | bytes 589832 | tf_op jit(solution)/shard_map/ppermute | solution.py:48
  86.5 2.5 %collective-permute-done.19 = bf16[96,1024]{1,0:T(8,128)(2,1)S(1)} collective-permute-done((bf16[96,1024]{1,0:T(8,128)(2,1)S(1)}, bf16[96,1024]{1,0:T(8,128)(2,1)S(1)}, u32[]{:S(2)}, u32[]{:S(2)}) %collective-permute-start.19) | collective-permute-done | bytes 196640 | tf_op jit(solution)/shard_map/ppermute | solution.py:48
  89.2 3.2 %collective-permute-start.21 = (bf16[96,1024]{1,0:T(8,128)(2,1)S(1)}, bf16[96,1024]{1,0:T(8,128)(2,1)S(1)}, u32[]{:S(2)}, u32[]{:S(2)}) collective-permute-start(bf16[96,1024]{1,0:T(8,128)(2,1)S(1)} %add_convert_fusion.refs_0_._), channel_id=1, source_target_pairs={{0,48},{16,0},{32,16},{48,32},{64,112},{80,64},{96,80},{112,96},{1... | collective-permute-start | bytes 589832 | tf_op jit(solution)/shard_map/ppermute | solution.py:48
  96.9 3.5 %hold_weights.1 = (bf16[512,3584]{1,0:T(8,128)(2,1)S(1)}, bf16[512,3584]{1,0:T(8,128)(2,1)S(1)}, bf16[512,3584]{1,0:T(8,128)(2,1)S(1)}, bf16[512,3584]{1,0:T(8,128)(2,1)S(1)}) custom-call(bf16[96,1024]{1,0:T(8,128)(2,1)S(1)} %add_convert_fusion.refs_0_._, bf16[512,3584]{1,0:T(8,128)(2,1)S(1)} %copy-done.2, bf16[512,3584]{1,0:T(8,128)(2,1)} %collective-permute-done.3.refs_1_, ...), custom_call_target="tpu_custom_call" | custom-call | bytes 29360128 | tf_op jit(solution)/shard_map/hold_weights/pallas_call | solution.py:344
  101.3 3.4 %hidden_y_first.1 = (bf16[96,4224]{1,0:T(8,128)(2,1)S(1)}, bf16[96,2176]{1,0:T(8,128)(2,1)S(1)}, bf16[96,2048]{1,0:T(8,128)(2,1)S(1)}, bf16[96,2048]{1,0:T(8,128...) custom-call(bf16[384,1024]{1,0:T(8,128)(2,1)S(1)} %get-tuple-element.55.s_ref, ...), custom_call_target="tpu_custom_call" | custom-call | flops 1000000000 | bytes 1000000 | tf_op jit(solution)/shard_map/hidden_y_first/pallas_call | solution.py:400
  104.7 2.6 %hidden_x_first.1 = (bf16[4,2,48,1536]{3,2,1,0:T(8,128)(2,1)S(1)}, bf16[4,2,48,1536]{3,2,1,0:T(8,128)(2,1)S(1)}, f32[8,128]{1,0:T(8,128)S(1)}) custom-call(bf16[384,1024]{1,0:T(8,128)(2,1)S(1)} %get-tuple-element.55.s_ref, bf16[512,3584]{1,0:T(8,128)(2,1)S(1)} %get-tuple-element.58.g0, bf16[512,3584]{1,0:T(8,128)(2,1)S(1)} %get-tuple-element.59.g1, ...), custom_call_target="tpu_custom_call" | custom-call | flops 100000000 | bytes 100000 | tf_op jit(solution)/shard_map/hidden_x_first/pallas_call | solution.py:400
  107.3 3.8 %collective-permute-start.24 = (bf16[4,2,48,1536]{3,2,1,0:T(8,128)(2,1)S(1)}, bf16[4,2,48,1536]{3,2,1,0:T(8,128)(2,1)S(1)}, u32[]{:S(2)}, u32[]{:S(2)}) collective-permute-start(bf16[4,2,48,1536]{3,2,1,0:T(8,128)(2,1)S(1)} %get-tuple-element.65), channel_id=1, source_target_pairs={{0,8},{1,9},{2,10},{3,11},{4,12},{5,13},{6,14},{7,15},{8,0},{9,1},... | collective-permute-start | bytes 3538952 | tf_op jit(solution)/shard_map/ppermute | solution.py:52
  111.1 3.2 %collective-permute-start.26 = (bf16[96,2048]{1,0:T(8,128)(2,1)S(1)}, bf16[96,2048]{1,0:T(8,128)(2,1)S(1)}, u32[]{:S(2)}, u32[]{:S(2)}) collective-permute-start(bf16[96,2048]{1,0:T(8,128)(2,1)S(1)} %get-tuple-element.63.refs_0_), channel_id=1, source_target_pairs={{0,6},{1,7},{2,0},{3,1},{4,2},{5,3},{6,4},{7,5},{8,14},{9,15},{10,... | collective-permute-start | bytes 1179656 | tf_op jit(solution)/shard_map/ppermute | solution.py:52
  114.3 9.5 %collective-permute-done.26.above = bf16[96,2048]{1,0:T(8,128)(2,1)S(1)} collective-permute-done((bf16[96,2048]{1,0:T(8,128)(2,1)S(1)}, bf16[96,2048]{1,0:T(8,128)(2,1)S(1)}, u32[]{:S(2)}, u32[]{:S(2)}) %collective-permute-start.26) | collective-permute-done | bytes 393248 | tf_op jit(solution)/shard_map/ppermute | solution.py:52
  129.4 8.6 %collective-permute-done.28.below_up = bf16[96,2048]{1,0:T(8,128)(2,1)S(1)} collective-permute-done((bf16[96,2048]{1,0:T(8,128)(2,1)S(1)}, bf16[96,2048]{1,0:T(8,128)(2,1)S(1)}, u32[]{:S(2)}, u32[]{:S(2)}) %collective-permute-start.28) | collective-permute-done | bytes 393248 | tf_op jit(solution)/shard_map/ppermute | solution.py:52
  138.8 2.2 %collective-permute-start.31 = (bf16[2,48,1536]{2,1,0:T(8,128)(2,1)S(1)}, bf16[2,48,1536]{2,1,0:T(8,128)(2,1)S(1)}, u32[]{:S(2)}, u32[]{:S(2)}) collective-permute-start(bf16[2,48,1536]{2,1,0:T(8,128)(2,1)S(1)} %get-tuple-element.78), channel_id=1, source_target_pairs={{0,4},{1,5},{2,6},{3,7},{4,0},{5,1},{6,2},{7,3},{8,12},{9,13},{10,... | collective-permute-start | bytes 884744 | tf_op jit(solution)/shard_map/ppermute | solution.py:52
  146.6 2.5 %collective-permute-done.31.refs_0_ = bf16[2,48,1536]{2,1,0:T(8,128)(2,1)S(1)} collective-permute-done((bf16[2,48,1536]{2,1,0:T(8,128)(2,1)S(1)}, bf16[2,48,1536]{2,1,0:T(8,128)(2,1)S(1)}, u32[]{:S(2)}, u32[]{:S(2)}) %collective-permute-start.31) | collective-permute-done | bytes 294944 | tf_op jit(solution)/shard_map/ppermute | solution.py:52
  (104 shorter events, 58.7 us)
Async XLA Ops:
  0.6 15.1 %collective-permute-start.3 = (bf16[512,3584]{1,0:T(8,128)(2,1)}, bf16[512,3584]{1,0:T(8,128)(2,1)}, u32[]{:S(2)}, u32[]{:S(2)}) collective-permute-start(bf16[512,3584]{1,0:T(8,128)(2,1)} %refs_0_.1), channel_id=1, source_target_pairs={{0,1},{1,0},{2,3},{3,2},{4,5},{5,4},{6,7},{7,6},{8,9},{9,8},{10,11... | collective-permute-start | bytes 11010056 | tf_op jit(solution)/shard_map/ppermute | solution.py:52
  0.7 21.0 %collective-permute-start.4 = (bf16[512,3584]{1,0:T(8,128)(2,1)}, bf16[512,3584]{1,0:T(8,128)(2,1)}, u32[]{:S(2)}, u32[]{:S(2)}) collective-permute-start(bf16[512,3584]{1,0:T(8,128)(2,1)} %refs_2_.1), channel_id=1, source_target_pairs={{0,1},{1,0},{2,3},{3,2},{4,5},{5,4},{6,7},{7,6},{8,9},{9,8},{10,11... | collective-permute-start | bytes 11010056 | tf_op jit(solution)/shard_map/ppermute | solution.py:52
  9.7 13.9 %collective-permute-start.5 = (bf16[2,48,1024]{2,1,0:T(8,128)(2,1)S(1)}, bf16[2,48,1024]{2,1,0:T(8,128)(2,1)S(1)}, u32[]{:S(2)}, u32[]{:S(2)}) collective-permute-start(bf16[2,48,1024]{2,1,0:T(8,128)(2,1)S(1)} %pair_up.1), channel_id=1, source_target_pairs={{0,16},{16,32},{32,48},{48,0},{64,80},{80,96},{96,112},{112,64},{1... | collective-permute-start | bytes 589832 | tf_op jit(solution)/shard_map/ppermute | solution.py:48
  11.7 17.2 %collective-permute-start.8 = (bf16[2,48,1024]{2,1,0:T(8,128)(2,1)S(1)}, bf16[2,48,1024]{2,1,0:T(8,128)(2,1)S(1)}, u32[]{:S(2)}, u32[]{:S(2)}) collective-permute-start(bf16[2,48,1024]{2,1,0:T(8,128)(2,1)S(1)} %pair_up.1), channel_id=1, source_target_pairs={{0,48},{16,0},{32,16},{48,32},{64,112},{80,64},{96,80},{112,96},{1... | collective-permute-start | bytes 589832 | tf_op jit(solution)/shard_map/ppermute | solution.py:48
  13.9 21.9 %collective-permute-start.11 = (bf16[2,48,1024]{2,1,0:T(8,128)(2,1)S(1)}, bf16[2,48,1024]{2,1,0:T(8,128)(2,1)S(1)}, u32[]{:S(2)}, u32[]{:S(2)}) collective-permute-start(bf16[2,48,1024]{2,1,0:T(8,128)(2,1)S(1)} %pair_up.1), channel_id=1, source_target_pairs={{0,32},{16,48},{32,0},{48,16},{64,96},{80,112},{96,64},{112,80},{1... | collective-permute-start | bytes 589832 | tf_op jit(solution)/shard_map/ppermute | solution.py:48
  15.7 45.0 %collective-permute-start.14 = (bf16[1024,512]{1,0:T(8,128)(2,1)S(1)}, bf16[1024,512]{1,0:T(8,128)(2,1)S(1)}, u32[]{:S(2)}, u32[]{:S(2)}) collective-permute-start(bf16[1024,512]{1,0:T(8,128)(2,1)S(1)} %copy-done.11), channel_id=1, source_target_pairs={{0,1},{1,0},{2,3},{3,2},{4,5},{5,4},{6,7},{7,6},{8,9},{9,8},{10,11... | collective-permute-start | bytes 3145736 | tf_op jit(solution)/shard_map/ppermute | solution.py:52
  21.7 10.4 %collective-permute-start.2 = (bf16[432,128]{1,0:T(8,128)(2,1)S(1)}, bf16[432,128]{1,0:T(8,128)(2,1)S(1)}, u32[]{:S(2)}, u32[]{:S(2)}) collective-permute-start(bf16[432,128]{1,0:T(8,128)(2,1)S(1)} %prefix_part.7.refs_0_), channel_id=1, source_target_pairs={{0,64},{16,80},{32,96},{48,112},{64,0},{80,16},{96,32},{112,48},{1... | collective-permute-start | bytes 331784 | tf_op jit(solution)/shard_map/ppermute | solution.py:48
  25.3 11.8 %collective-permute-start.6 = (bf16[432,128]{1,0:T(8,128)(2,1)S(1)}, bf16[432,128]{1,0:T(8,128)(2,1)S(1)}, u32[]{:S(2)}, u32[]{:S(2)}) collective-permute-start(bf16[432,128]{1,0:T(8,128)(2,1)S(1)} %prefix_part.8.refs_0_), channel_id=1, source_target_pairs={{0,112},{16,64},{32,80},{48,96},{64,48},{80,0},{96,16},{112,32},{1... | collective-permute-start | bytes 331784 | tf_op jit(solution)/shard_map/ppermute | solution.py:48
  28.9 9.9 %collective-permute-start.7 = (bf16[432,128]{1,0:T(8,128)(2,1)S(1)}, bf16[432,128]{1,0:T(8,128)(2,1)S(1)}, u32[]{:S(2)}, u32[]{:S(2)}) collective-permute-start(bf16[432,128]{1,0:T(8,128)(2,1)S(1)} %prefix_part.9.refs_0_), channel_id=1, source_target_pairs={{0,48},{16,0},{32,16},{48,32},{64,112},{80,64},{96,80},{112,96},{1... | collective-permute-start | bytes 331784 | tf_op jit(solution)/shard_map/ppermute | solution.py:48
  32.2 15.9 %collective-permute-start.9 = (bf16[432,128]{1,0:T(8,128)(2,1)S(1)}, bf16[432,128]{1,0:T(8,128)(2,1)S(1)}, u32[]{:S(2)}, u32[]{:S(2)}) collective-permute-start(bf16[432,128]{1,0:T(8,128)(2,1)S(1)} %prefix_part.10.refs_0_), channel_id=1, source_target_pairs={{0,80},{16,96},{32,112},{48,64},{64,16},{80,32},{96,48},{112,0},{1... | collective-permute-start | bytes 331784 | tf_op jit(solution)/shard_map/ppermute | solution.py:48
  35.8 12.3 %collective-permute-start.10 = (bf16[432,128]{1,0:T(8,128)(2,1)S(1)}, bf16[432,128]{1,0:T(8,128)(2,1)S(1)}, u32[]{:S(2)}, u32[]{:S(2)}) collective-permute-start(bf16[432,128]{1,0:T(8,128)(2,1)S(1)} %prefix_part.11.refs_0_), channel_id=1, source_target_pairs={{0,16},{16,32},{32,48},{48,0},{64,80},{80,96},{96,112},{112,64},{1... | collective-permute-start | bytes 331784 | tf_op jit(solution)/shard_map/ppermute | solution.py:48
  54.9 14.7 %all-to-all-start = ((bf16[8,48,1024]{2,1,0:T(8,128)(2,1)}), bf16[8,48,1024]{2,1,0:T(8,128)(2,1)S(1)}, u32[]{:S(2)}, u32[]{:S(2)}) async-start(bf16[8,48,1024]{2,1,0:T(8,128)(2,1)} %merge_parts.1), calls=%async_computation | async-start | bytes 1572864 | tf_op jit(solution)/shard_map/all_to_all | solution.py:573
  89.1 11.2 %collective-permute-start.20 = (bf16[96,1024]{1,0:T(8,128)(2,1)S(1)}, bf16[96,1024]{1,0:T(8,128)(2,1)S(1)}, u32[]{:S(2)}, u32[]{:S(2)}) collective-permute-start(bf16[96,1024]{1,0:T(8,128)(2,1)S(1)} %add_convert_fusion.refs_0_._), channel_id=1, source_target_pairs={{0,16},{16,32},{32,48},{48,0},{64,80},{80,96},{96,112},{112,64},{1... | collective-permute-start | bytes 589832 | tf_op jit(solution)/shard_map/ppermute | solution.py:48
  89.2 11.2 %collective-permute-start.21 = (bf16[96,1024]{1,0:T(8,128)(2,1)S(1)}, bf16[96,1024]{1,0:T(8,128)(2,1)S(1)}, u32[]{:S(2)}, u32[]{:S(2)}) collective-permute-start(bf16[96,1024]{1,0:T(8,128)(2,1)S(1)} %add_convert_fusion.refs_0_._), channel_id=1, source_target_pairs={{0,48},{16,0},{32,16},{48,32},{64,112},{80,64},{96,80},{112,96},{1... | collective-permute-start | bytes 589832 | tf_op jit(solution)/shard_map/ppermute | solution.py:48
  107.3 31.2 %collective-permute-start.24 = (bf16[4,2,48,1536]{3,2,1,0:T(8,128)(2,1)S(1)}, bf16[4,2,48,1536]{3,2,1,0:T(8,128)(2,1)S(1)}, u32[]{:S(2)}, u32[]{:S(2)}) collective-permute-start(bf16[4,2,48,1536]{3,2,1,0:T(8,128)(2,1)S(1)} %get-tuple-element.65), channel_id=1, source_target_pairs={{0,8},{1,9},{2,10},{3,11},{4,12},{5,13},{6,14},{7,15},{8,0},{9,1},... | collective-permute-start | bytes 3538952 | tf_op jit(solution)/shard_map/ppermute | solution.py:52
  111.1 12.7 %collective-permute-start.25 = (bf16[96,2176]{1,0:T(8,128)(2,1)S(1)}, bf16[96,2176]{1,0:T(8,128)(2,1)S(1)}, u32[]{:S(2)}, u32[]{:S(2)}) collective-permute-start(bf16[96,2176]{1,0:T(8,128)(2,1)S(1)} %get-tuple-element.69), channel_id=1, source_target_pairs={{0,2},{1,3},{2,4},{3,5},{4,6},{5,7},{6,0},{7,1},{8,10},{9,11},{10,... | collective-permute-start | bytes 1253384 | tf_op jit(solution)/shard_map/ppermute | solution.py:52
  111.1 12.7 %collective-permute-start.26 = (bf16[96,2048]{1,0:T(8,128)(2,1)S(1)}, bf16[96,2048]{1,0:T(8,128)(2,1)S(1)}, u32[]{:S(2)}, u32[]{:S(2)}) collective-permute-start(bf16[96,2048]{1,0:T(8,128)(2,1)S(1)} %get-tuple-element.63.refs_0_), channel_id=1, source_target_pairs={{0,6},{1,7},{2,0},{3,1},{4,2},{5,3},{6,4},{7,5},{8,14},{9,15},{10,... | collective-permute-start | bytes 1179656 | tf_op jit(solution)/shard_map/ppermute | solution.py:52
  114.3 11.7 %collective-permute-start.23 = (bf16[384,512]{1,0:T(8,128)(2,1)S(1)}, bf16[384,512]{1,0:T(8,128)(2,1)S(1)}, u32[]{:S(2)}, u32[]{:S(2)}) collective-permute-start(bf16[384,512]{1,0:T(8,128)(2,1)S(1)} %get-tuple-element.53), channel_id=1, source_target_pairs={{0,1},{1,0},{2,3},{3,2},{4,5},{5,4},{6,7},{7,6},{8,9},{9,8},{10,11... | collective-permute-start | bytes 1179656 | tf_op jit(solution)/shard_map/ppermute | solution.py:52
  114.3 23.7 %collective-permute-start.29 = (bf16[96,2176]{1,0:T(8,128)(2,1)S(1)}, bf16[96,2176]{1,0:T(8,128)(2,1)S(1)}, u32[]{:S(2)}, u32[]{:S(2)}) collective-permute-start(bf16[96,2176]{1,0:T(8,128)(2,1)S(1)} %get-tuple-element.73), channel_id=1, source_target_pairs={{0,6},{1,7},{2,0},{3,1},{4,2},{5,3},{6,4},{7,5},{8,14},{9,15},{10,... | collective-permute-start | bytes 1253384 | tf_op jit(solution)/shard_map/ppermute | solution.py:52
  124.0 14.0 %collective-permute-start.27 = (bf16[96,2176]{1,0:T(8,128)(2,1)S(1)}, bf16[96,2176]{1,0:T(8,128)(2,1)S(1)}, u32[]{:S(2)}, u32[]{:S(2)}) collective-permute-start(bf16[96,2176]{1,0:T(8,128)(2,1)S(1)} %get-tuple-element.71), channel_id=1, source_target_pairs={{0,2},{1,3},{2,4},{3,5},{4,6},{5,7},{6,0},{7,1},{8,10},{9,11},{10,... | collective-permute-start | bytes 1253384 | tf_op jit(solution)/shard_map/ppermute | solution.py:52
  124.1 13.9 %collective-permute-start.28 = (bf16[96,2048]{1,0:T(8,128)(2,1)S(1)}, bf16[96,2048]{1,0:T(8,128)(2,1)S(1)}, u32[]{:S(2)}, u32[]{:S(2)}) collective-permute-start(bf16[96,2048]{1,0:T(8,128)(2,1)S(1)} %get-tuple-element.72), channel_id=1, source_target_pairs={{0,2},{1,3},{2,4},{3,5},{4,6},{5,7},{6,0},{7,1},{8,10},{9,11},{10,... | collective-permute-start | bytes 1179656 | tf_op jit(solution)/shard_map/ppermute | solution.py:52
  126.0 12.0 %collective-permute-start.30 = (bf16[96,2048]{1,0:T(8,128)(2,1)S(1)}, bf16[96,2048]{1,0:T(8,128)(2,1)S(1)}, u32[]{:S(2)}, u32[]{:S(2)}) collective-permute-start(bf16[96,2048]{1,0:T(8,128)(2,1)S(1)} %get-tuple-element.74), channel_id=1, source_target_pairs={{0,6},{1,7},{2,0},{3,1},{4,2},{5,3},{6,4},{7,5},{8,14},{9,15},{10,... | collective-permute-start | bytes 1179656 | tf_op jit(solution)/shard_map/ppermute | solution.py:52
  138.8 10.3 %collective-permute-start.31 = (bf16[2,48,1536]{2,1,0:T(8,128)(2,1)S(1)}, bf16[2,48,1536]{2,1,0:T(8,128)(2,1)S(1)}, u32[]{:S(2)}, u32[]{:S(2)}) collective-permute-start(bf16[2,48,1536]{2,1,0:T(8,128)(2,1)S(1)} %get-tuple-element.78), channel_id=1, source_target_pairs={{0,4},{1,5},{2,6},{3,7},{4,0},{5,1},{6,2},{7,3},{8,12},{9,13},{10,... | collective-permute-start | bytes 884744 | tf_op jit(solution)/shard_map/ppermute | solution.py:52
  141.0 10.2 %collective-permute-start.32 = (bf16[2,48,1536]{2,1,0:T(8,128)(2,1)S(1)}, bf16[2,48,1536]{2,1,0:T(8,128)(2,1)S(1)}, u32[]{:S(2)}, u32[]{:S(2)}) collective-permute-start(bf16[2,48,1536]{2,1,0:T(8,128)(2,1)S(1)} %get-tuple-element.79), channel_id=1, source_target_pairs={{0,2},{1,3},{2,4},{3,5},{4,6},{5,7},{6,0},{7,1},{8,10},{9,11},{10,... | collective-permute-start | bytes 884744 | tf_op jit(solution)/shard_map/ppermute | solution.py:52
  (26 other events, 171.0 us)

commit v6 on v5

--- a/solution.py
+++ b/solution.py
@@ -601,7 +601,7 @@
     stream, token = assemble(place, pieces, over_batch(their_columns, 0, 0, 1))
     b_keep, b_send = finish_y(b_first[0], received, token)
     b_part, rms = finish_b(b_keep, over_batch(b_send, 1, 0))
-    mine, *sends = add_got(a_first[0], over_batch(a_first[1], 1, 0), b_send)
+    mine, *sends = add_got(a_first[0], over_batch(a_first[1], 1, 0), token)
     activation = finish_a(mine, [over_batch(sends[s - 1], 0, s) for s in (2, 1, 3)], b_part, rms)
     return (stream, activation)
 

time: 153 us -> 153 us (level)
  no operation moved by 1% of the time
where the time goes in v6:
time: 153 us; the launch traced here: 152 us
  starting transfers between devices  53.5 us (35%)
  waiting for transfers between devices  50 us (33%)
  Pallas kernels  37.3 us (24%)
  local copies, waits for them, and re-layouts  10.3 us (7%)
    ppermute x18, starting transfers between devices, over_ctx(): return lax.ppermute(v, 'ctx', ctx_perm(flip, s))  31.7 us
    ppermute x17, waiting for transfers between devices, over_batch(): return lax.ppermute(v, 'batch', batch_perm(flip_x, s, flip_core))  27.2 us
    ppermute x17, starting transfers between devices, over_batch(): return lax.ppermute(v, 'batch', batch_perm(flip_x, s, flip_core))  17.3 us
    ppermute x18, waiting for transfers between devices, over_ctx(): return lax.ppermute(v, 'ctx', ctx_perm(flip, s))  13.8 us
    pallas_call x7, Pallas kernels, prefix_part(): pl.pallas_call(functools.partial(prefix_kernel, which), in_specs=[pl.Bloc...  11.7 us
    unnamed x28, local copies, waits for them, and re-layouts  9.17 us
    all_to_all x1, waiting for transfers between devices, on_device(): lax.all_to_all(attended, 'batch', 0, 0, axis_index_groups=SAME_CORE, tile...  8.9 us
    pallas_call x2, Pallas kernels, hidden_call(): pl.pallas_call(functools.partial(kernel, first, columns), in_specs=[pl.Bl...  6 us
  transfers between devices with their start and end apart: 36, of which 13 were waited for; matrix products, arithmetic and copies ran while one was open for 1% of the time, Pallas kernels for 18%

profile of v6, /device:TPU:0, one launch (start us, length us, event | category | flops | bytes accessed | tf_op | source)
XLA Modules:
  0.0 152.2 jit_solution(17196795075099938311)
XLA Ops:
  1.2 3.1 %collective-permute-start.1 = (bf16[48,1024]{1,0:T(8,128)(2,1)}, bf16[48,1024]{1,0:T(8,128)(2,1)S(1)}, u32[]{:S(2)}, u32[]{:S(2)}) collective-permute-start(bf16[48,1024]{1,0:T(8,128)(2,1)} %q_ref.3), channel_id=1, source_target_pairs={{0,64},{16,80},{32,96},{48,112},{64,0},{80,16},{96,32},{112,48},{1... | collective-permute-start | bytes 294920 | tf_op jit(solution)/shard_map/ppermute | solution.py:48
  4.3 4.6 %own_prefix.1 = (bf16[432,128]{1,0:T(8,128)(2,1)}, f32[8,128]{1,0:T(8,128)}) custom-call(s32[1]{0:T(128)} %bitcast.21.group_ref, bf16[48,1024]{1,0:T(8,128)(2,1)} %q_ref.3, bf16[2048,1024]{1,0:T(8,128)(2,1)} %k_ref.15, bf16[2048,1024]{1,0:T(8,128)(2,1)} %v_ref.15), custom_call_target="tpu_custom_call" | custom-call | flops 402653184 | bytes 1048576 | tf_op jit(solution)/shard_map/own_prefix/pallas_call | solution.py:126
  11.7 2.2 %collective-permute-start.8 = (bf16[2,48,1024]{2,1,0:T(8,128)(2,1)S(1)}, bf16[2,48,1024]{2,1,0:T(8,128)(2,1)S(1)}, u32[]{:S(2)}, u32[]{:S(2)}) collective-permute-start(bf16[2,48,1024]{2,1,0:T(8,128)(2,1)S(1)} %pair_up.1), channel_id=1, source_target_pairs={{0,48},{16,0},{32,16},{48,32},{64,112},{80,64},{96,80},{112,96},{1... | collective-permute-start | bytes 589832 | tf_op jit(solution)/shard_map/ppermute | solution.py:48
  17.9 2.2 %copy-done.1 = bf16[2048,1024]{1,0:T(8,128)(2,1)S(1)} copy-done((bf16[2048,1024]{1,0:T(8,128)(2,1)S(1)}, bf16[2048,1024]{1,0:T(8,128)(2,1)}, u32[]{:S(2)}) %copy-start.1) | copy-done | bytes 4194328
  40.6 3.0 %collective-permute-start.13 = (bf16[432,128]{1,0:T(8,128)(2,1)S(1)}, bf16[432,128]{1,0:T(8,128)(2,1)S(1)}, u32[]{:S(2)}, u32[]{:S(2)}) collective-permute-start(bf16[432,128]{1,0:T(8,128)(2,1)S(1)} %prefix_part.13), channel_id=1, source_target_pairs={{0,32},{16,48},{32,0},{48,16},{64,96},{80,112},{96,64},{112,80},{1... | collective-permute-start | bytes 331784 | tf_op jit(solution)/shard_map/ppermute | solution.py:48
  45.4 2.7 %suffix_part.1 = (f32[8,48,128]{2,1,0:T(8,128)S(1)}, f32[8,48,128]{2,1,0:T(8,128)S(1)}) custom-call(bf16[48,1024]{1,0:T(8,128)(2,1)S(1)} %copy-done.6, bf16[6144,128]{1,0:T(8,128)(2,1)S(1)} %bitcast.38, bf16[6144,128]{1,0:T(8,128)(2,1)S(1)} %bitcast.39, bf16[48,128]{1,0:T(8,128)(2,1)S(1)} %copy-done.8, bf16[48,128]{1,0:T(8,128)(2,1)S(1)} %copy-done.9, ...), custom_call_target="tpu_custom_call" | custom-call | flops 402653184 | bytes 4194304 | tf_op jit(solution)/shard_map/suffix_part/pallas_call | solution.py:200
  48.1 4.1 %collective-permute-done.12.refs_6_ = bf16[432,128]{1,0:T(8,128)(2,1)S(1)} collective-permute-done((bf16[432,128]{1,0:T(8,128)(2,1)S(1)}, bf16[432,128]{1,0:T(8,128)(2,1)S(1)}, u32[]{:S(2)}, u32[]{:S(2)}) %collective-permute-start.12) | collective-permute-done | bytes 110624 | tf_op jit(solution)/shard_map/ppermute | solution.py:48
  52.2 2.8 %merge_parts.1 = bf16[8,48,1024]{2,1,0:T(8,128)(2,1)} custom-call(bf16[432,128]{1,0:T(8,128)(2,1)S(1)} %copy-done.7, bf16[432,128]{1,0:T(8,128)(2,1)S(1)} %collective-permute-done.2.refs_1_, bf16[432,128]{1,0:T(8,128)(2,1)S(1)} %collective-permute-done.6.refs_1_.refs_2_, bf16[432,128]{1,0:T(8,128)(2,1)S(1)} %collective-permute-done.7.refs_1_.refs_3_, ...), custom_call_target="tpu_custom_call" | custom-call | flops 983040 | bytes 2097152 | tf_op jit(solution)/shard_map/merge_parts/pallas_call | solution.py:243
  54.9 4.5 %all-to-all-start = ((bf16[8,48,1024]{2,1,0:T(8,128)(2,1)}), bf16[8,48,1024]{2,1,0:T(8,128)(2,1)S(1)}, u32[]{:S(2)}, u32[]{:S(2)}) async-start(bf16[8,48,1024]{2,1,0:T(8,128)(2,1)} %merge_parts.1), calls=%async_computation | async-start | bytes 1572864 | tf_op jit(solution)/shard_map/all_to_all | solution.py:573
  60.7 8.9 %all-to-all-done = bf16[8,48,1024]{2,1,0:T(8,128)(2,1)S(1)} async-done(((bf16[8,48,1024]{2,1,0:T(8,128)(2,1)}), bf16[8,48,1024]{2,1,0:T(8,128)(2,1)S(1)}, u32[]{:S(2)}, u32[]{:S(2)}) %all-to-all-start) | async-done | bytes 786464 | tf_op jit(solution)/shard_map/all_to_all | solution.py:573
  71.3 3.2 %collective-permute-start.17 = (bf16[96,1024]{1,0:T(8,128)(2,1)}, bf16[96,1024]{1,0:T(8,128)(2,1)S(1)}, u32[]{:S(2)}, u32[]{:S(2)}) collective-permute-start(bf16[96,1024]{1,0:T(8,128)(2,1)} %get-tuple-element.50), channel_id=1, source_target_pairs={{0,48},{16,0},{32,16},{48,32},{64,112},{80,64},{96,80},{112,96},{1... | collective-permute-start | bytes 589832 | tf_op jit(solution)/shard_map/ppermute | solution.py:48
  74.5 3.9 %collective-permute-done.16 = bf16[96,1024]{1,0:T(8,128)(2,1)S(1)} collective-permute-done((bf16[96,1024]{1,0:T(8,128)(2,1)}, bf16[96,1024]{1,0:T(8,128)(2,1)S(1)}, u32[]{:S(2)}, u32[]{:S(2)}) %collective-permute-start.16) | collective-permute-done | bytes 196640 | tf_op jit(solution)/shard_map/ppermute | solution.py:48
  81.8 2.4 %collective-permute-start.19 = (bf16[96,1024]{1,0:T(8,128)(2,1)S(1)}, bf16[96,1024]{1,0:T(8,128)(2,1)S(1)}, u32[]{:S(2)}, u32[]{:S(2)}) collective-permute-start(bf16[96,1024]{1,0:T(8,128)(2,1)S(1)} %add_convert_fusion.1), channel_id=1, source_target_pairs={{0,64},{16,80},{32,96},{48,112},{64,0},{80,16},{96,32},{112,48},{1... | collective-permute-start | bytes 589832 | tf_op jit(solution)/shard_map/ppermute | solution.py:48
  86.5 2.5 %collective-permute-done.19 = bf16[96,1024]{1,0:T(8,128)(2,1)S(1)} collective-permute-done((bf16[96,1024]{1,0:T(8,128)(2,1)S(1)}, bf16[96,1024]{1,0:T(8,128)(2,1)S(1)}, u32[]{:S(2)}, u32[]{:S(2)}) %collective-permute-start.19) | collective-permute-done | bytes 196640 | tf_op jit(solution)/shard_map/ppermute | solution.py:48
  89.2 3.2 %collective-permute-start.21 = (bf16[96,1024]{1,0:T(8,128)(2,1)S(1)}, bf16[96,1024]{1,0:T(8,128)(2,1)S(1)}, u32[]{:S(2)}, u32[]{:S(2)}) collective-permute-start(bf16[96,1024]{1,0:T(8,128)(2,1)S(1)} %add_convert_fusion.refs_0_._), channel_id=1, source_target_pairs={{0,48},{16,0},{32,16},{48,32},{64,112},{80,64},{96,80},{112,96},{1... | collective-permute-start | bytes 589832 | tf_op jit(solution)/shard_map/ppermute | solution.py:48
  96.9 3.5 %hold_weights.1 = (bf16[512,3584]{1,0:T(8,128)(2,1)S(1)}, bf16[512,3584]{1,0:T(8,128)(2,1)S(1)}, bf16[512,3584]{1,0:T(8,128)(2,1)S(1)}, bf16[512,3584]{1,0:T(8,128)(2,1)S(1)}) custom-call(bf16[96,1024]{1,0:T(8,128)(2,1)S(1)} %add_convert_fusion.refs_0_._, bf16[512,3584]{1,0:T(8,128)(2,1)S(1)} %copy-done.2, bf16[512,3584]{1,0:T(8,128)(2,1)} %collective-permute-done.3.refs_1_, ...), custom_call_target="tpu_custom_call" | custom-call | bytes 29360128 | tf_op jit(solution)/shard_map/hold_weights/pallas_call | solution.py:344
  101.3 3.4 %hidden_y_first.1 = (bf16[96,4224]{1,0:T(8,128)(2,1)S(1)}, bf16[96,2176]{1,0:T(8,128)(2,1)S(1)}, bf16[96,2048]{1,0:T(8,128)(2,1)S(1)}, bf16[96,2048]{1,0:T(8,128...) custom-call(bf16[384,1024]{1,0:T(8,128)(2,1)S(1)} %get-tuple-element.55.s_ref, ...), custom_call_target="tpu_custom_call" | custom-call | flops 1000000000 | bytes 1000000 | tf_op jit(solution)/shard_map/hidden_y_first/pallas_call | solution.py:400
  104.7 2.6 %hidden_x_first.1 = (bf16[4,2,48,1536]{3,2,1,0:T(8,128)(2,1)S(1)}, bf16[4,2,48,1536]{3,2,1,0:T(8,128)(2,1)S(1)}, f32[8,128]{1,0:T(8,128)S(1)}) custom-call(bf16[384,1024]{1,0:T(8,128)(2,1)S(1)} %get-tuple-element.55.s_ref, bf16[512,3584]{1,0:T(8,128)(2,1)S(1)} %get-tuple-element.58.g0, bf16[512,3584]{1,0:T(8,128)(2,1)S(1)} %get-tuple-element.59.g1, ...), custom_call_target="tpu_custom_call" | custom-call | flops 100000000 | bytes 100000 | tf_op jit(solution)/shard_map/hidden_x_first/pallas_call | solution.py:400
  107.3 3.8 %collective-permute-start.24 = (bf16[4,2,48,1536]{3,2,1,0:T(8,128)(2,1)S(1)}, bf16[4,2,48,1536]{3,2,1,0:T(8,128)(2,1)S(1)}, u32[]{:S(2)}, u32[]{:S(2)}) collective-permute-start(bf16[4,2,48,1536]{3,2,1,0:T(8,128)(2,1)S(1)} %get-tuple-element.65), channel_id=1, source_target_pairs={{0,8},{1,9},{2,10},{3,11},{4,12},{5,13},{6,14},{7,15},{8,0},{9,1},... | collective-permute-start | bytes 3538952 | tf_op jit(solution)/shard_map/ppermute | solution.py:52
  111.1 3.2 %collective-permute-start.29 = (bf16[96,2048]{1,0:T(8,128)(2,1)S(1)}, bf16[96,2048]{1,0:T(8,128)(2,1)S(1)}, u32[]{:S(2)}, u32[]{:S(2)}) collective-permute-start(bf16[96,2048]{1,0:T(8,128)(2,1)S(1)} %get-tuple-element.63.refs_0_), channel_id=1, source_target_pairs={{0,6},{1,7},{2,0},{3,1},{4,2},{5,3},{6,4},{7,5},{8,14},{9,15},{10,... | collective-permute-start | bytes 1179656 | tf_op jit(solution)/shard_map/ppermute | solution.py:52
  114.3 9.5 %collective-permute-done.29.above = bf16[96,2048]{1,0:T(8,128)(2,1)S(1)} collective-permute-done((bf16[96,2048]{1,0:T(8,128)(2,1)S(1)}, bf16[96,2048]{1,0:T(8,128)(2,1)S(1)}, u32[]{:S(2)}, u32[]{:S(2)}) %collective-permute-start.29) | collective-permute-done | bytes 393248 | tf_op jit(solution)/shard_map/ppermute | solution.py:52
  129.4 8.6 %collective-permute-done.31.below_up = bf16[96,2048]{1,0:T(8,128)(2,1)S(1)} collective-permute-done((bf16[96,2048]{1,0:T(8,128)(2,1)S(1)}, bf16[96,2048]{1,0:T(8,128)(2,1)S(1)}, u32[]{:S(2)}, u32[]{:S(2)}) %collective-permute-start.31) | collective-permute-done | bytes 393248 | tf_op jit(solution)/shard_map/ppermute | solution.py:52
  138.8 2.2 %collective-permute-start.25 = (bf16[2,48,1536]{2,1,0:T(8,128)(2,1)S(1)}, bf16[2,48,1536]{2,1,0:T(8,128)(2,1)S(1)}, u32[]{:S(2)}, u32[]{:S(2)}) collective-permute-start(bf16[2,48,1536]{2,1,0:T(8,128)(2,1)S(1)} %get-tuple-element.68), channel_id=1, source_target_pairs={{0,4},{1,5},{2,6},{3,7},{4,0},{5,1},{6,2},{7,3},{8,12},{9,13},{10,... | collective-permute-start | bytes 884744 | tf_op jit(solution)/shard_map/ppermute | solution.py:52
  146.5 2.6 %collective-permute-done.25.refs_0_ = bf16[2,48,1536]{2,1,0:T(8,128)(2,1)S(1)} collective-permute-done((bf16[2,48,1536]{2,1,0:T(8,128)(2,1)S(1)}, bf16[2,48,1536]{2,1,0:T(8,128)(2,1)S(1)}, u32[]{:S(2)}, u32[]{:S(2)}) %collective-permute-start.25) | collective-permute-done | bytes 294944 | tf_op jit(solution)/shard_map/ppermute | solution.py:52
  (104 shorter events, 58.7 us)
Async XLA Ops:
  0.6 15.1 %collective-permute-start.3 = (bf16[512,3584]{1,0:T(8,128)(2,1)}, bf16[512,3584]{1,0:T(8,128)(2,1)}, u32[]{:S(2)}, u32[]{:S(2)}) collective-permute-start(bf16[512,3584]{1,0:T(8,128)(2,1)} %refs_0_.1), channel_id=1, source_target_pairs={{0,1},{1,0},{2,3},{3,2},{4,5},{5,4},{6,7},{7,6},{8,9},{9,8},{10,11... | collective-permute-start | bytes 11010056 | tf_op jit(solution)/shard_map/ppermute | solution.py:52
  0.7 21.0 %collective-permute-start.4 = (bf16[512,3584]{1,0:T(8,128)(2,1)}, bf16[512,3584]{1,0:T(8,128)(2,1)}, u32[]{:S(2)}, u32[]{:S(2)}) collective-permute-start(bf16[512,3584]{1,0:T(8,128)(2,1)} %refs_2_.1), channel_id=1, source_target_pairs={{0,1},{1,0},{2,3},{3,2},{4,5},{5,4},{6,7},{7,6},{8,9},{9,8},{10,11... | collective-permute-start | bytes 11010056 | tf_op jit(solution)/shard_map/ppermute | solution.py:52
  9.7 13.9 %collective-permute-start.5 = (bf16[2,48,1024]{2,1,0:T(8,128)(2,1)S(1)}, bf16[2,48,1024]{2,1,0:T(8,128)(2,1)S(1)}, u32[]{:S(2)}, u32[]{:S(2)}) collective-permute-start(bf16[2,48,1024]{2,1,0:T(8,128)(2,1)S(1)} %pair_up.1), channel_id=1, source_target_pairs={{0,16},{16,32},{32,48},{48,0},{64,80},{80,96},{96,112},{112,64},{1... | collective-permute-start | bytes 589832 | tf_op jit(solution)/shard_map/ppermute | solution.py:48
  11.7 17.2 %collective-permute-start.8 = (bf16[2,48,1024]{2,1,0:T(8,128)(2,1)S(1)}, bf16[2,48,1024]{2,1,0:T(8,128)(2,1)S(1)}, u32[]{:S(2)}, u32[]{:S(2)}) collective-permute-start(bf16[2,48,1024]{2,1,0:T(8,128)(2,1)S(1)} %pair_up.1), channel_id=1, source_target_pairs={{0,48},{16,0},{32,16},{48,32},{64,112},{80,64},{96,80},{112,96},{1... | collective-permute-start | bytes 589832 | tf_op jit(solution)/shard_map/ppermute | solution.py:48
  13.9 21.9 %collective-permute-start.11 = (bf16[2,48,1024]{2,1,0:T(8,128)(2,1)S(1)}, bf16[2,48,1024]{2,1,0:T(8,128)(2,1)S(1)}, u32[]{:S(2)}, u32[]{:S(2)}) collective-permute-start(bf16[2,48,1024]{2,1,0:T(8,128)(2,1)S(1)} %pair_up.1), channel_id=1, source_target_pairs={{0,32},{16,48},{32,0},{48,16},{64,96},{80,112},{96,64},{112,80},{1... | collective-permute-start | bytes 589832 | tf_op jit(solution)/shard_map/ppermute | solution.py:48
  15.7 45.0 %collective-permute-start.14 = (bf16[1024,512]{1,0:T(8,128)(2,1)S(1)}, bf16[1024,512]{1,0:T(8,128)(2,1)S(1)}, u32[]{:S(2)}, u32[]{:S(2)}) collective-permute-start(bf16[1024,512]{1,0:T(8,128)(2,1)S(1)} %copy-done.11), channel_id=1, source_target_pairs={{0,1},{1,0},{2,3},{3,2},{4,5},{5,4},{6,7},{7,6},{8,9},{9,8},{10,11... | collective-permute-start | bytes 3145736 | tf_op jit(solution)/shard_map/ppermute | solution.py:52
  21.7 10.4 %collective-permute-start.2 = (bf16[432,128]{1,0:T(8,128)(2,1)S(1)}, bf16[432,128]{1,0:T(8,128)(2,1)S(1)}, u32[]{:S(2)}, u32[]{:S(2)}) collective-permute-start(bf16[432,128]{1,0:T(8,128)(2,1)S(1)} %prefix_part.7.refs_0_), channel_id=1, source_target_pairs={{0,64},{16,80},{32,96},{48,112},{64,0},{80,16},{96,32},{112,48},{1... | collective-permute-start | bytes 331784 | tf_op jit(solution)/shard_map/ppermute | solution.py:48
  25.3 11.8 %collective-permute-start.6 = (bf16[432,128]{1,0:T(8,128)(2,1)S(1)}, bf16[432,128]{1,0:T(8,128)(2,1)S(1)}, u32[]{:S(2)}, u32[]{:S(2)}) collective-permute-start(bf16[432,128]{1,0:T(8,128)(2,1)S(1)} %prefix_part.8.refs_0_), channel_id=1, source_target_pairs={{0,112},{16,64},{32,80},{48,96},{64,48},{80,0},{96,16},{112,32},{1... | collective-permute-start | bytes 331784 | tf_op jit(solution)/shard_map/ppermute | solution.py:48
  28.9 9.9 %collective-permute-start.7 = (bf16[432,128]{1,0:T(8,128)(2,1)S(1)}, bf16[432,128]{1,0:T(8,128)(2,1)S(1)}, u32[]{:S(2)}, u32[]{:S(2)}) collective-permute-start(bf16[432,128]{1,0:T(8,128)(2,1)S(1)} %prefix_part.9.refs_0_), channel_id=1, source_target_pairs={{0,48},{16,0},{32,16},{48,32},{64,112},{80,64},{96,80},{112,96},{1... | collective-permute-start | bytes 331784 | tf_op jit(solution)/shard_map/ppermute | solution.py:48
  32.2 15.9 %collective-permute-start.9 = (bf16[432,128]{1,0:T(8,128)(2,1)S(1)}, bf16[432,128]{1,0:T(8,128)(2,1)S(1)}, u32[]{:S(2)}, u32[]{:S(2)}) collective-permute-start(bf16[432,128]{1,0:T(8,128)(2,1)S(1)} %prefix_part.10.refs_0_), channel_id=1, source_target_pairs={{0,80},{16,96},{32,112},{48,64},{64,16},{80,32},{96,48},{112,0},{1... | collective-permute-start | bytes 331784 | tf_op jit(solution)/shard_map/ppermute | solution.py:48
  35.8 12.3 %collective-permute-start.10 = (bf16[432,128]{1,0:T(8,128)(2,1)S(1)}, bf16[432,128]{1,0:T(8,128)(2,1)S(1)}, u32[]{:S(2)}, u32[]{:S(2)}) collective-permute-start(bf16[432,128]{1,0:T(8,128)(2,1)S(1)} %prefix_part.11.refs_0_), channel_id=1, source_target_pairs={{0,16},{16,32},{32,48},{48,0},{64,80},{80,96},{96,112},{112,64},{1... | collective-permute-start | bytes 331784 | tf_op jit(solution)/shard_map/ppermute | solution.py:48
  54.9 14.7 %all-to-all-start = ((bf16[8,48,1024]{2,1,0:T(8,128)(2,1)}), bf16[8,48,1024]{2,1,0:T(8,128)(2,1)S(1)}, u32[]{:S(2)}, u32[]{:S(2)}) async-start(bf16[8,48,1024]{2,1,0:T(8,128)(2,1)} %merge_parts.1), calls=%async_computation | async-start | bytes 1572864 | tf_op jit(solution)/shard_map/all_to_all | solution.py:573
  89.1 11.2 %collective-permute-start.20 = (bf16[96,1024]{1,0:T(8,128)(2,1)S(1)}, bf16[96,1024]{1,0:T(8,128)(2,1)S(1)}, u32[]{:S(2)}, u32[]{:S(2)}) collective-permute-start(bf16[96,1024]{1,0:T(8,128)(2,1)S(1)} %add_convert_fusion.refs_0_._), channel_id=1, source_target_pairs={{0,16},{16,32},{32,48},{48,0},{64,80},{80,96},{96,112},{112,64},{1... | collective-permute-start | bytes 589832 | tf_op jit(solution)/shard_map/ppermute | solution.py:48
  89.2 11.2 %collective-permute-start.21 = (bf16[96,1024]{1,0:T(8,128)(2,1)S(1)}, bf16[96,1024]{1,0:T(8,128)(2,1)S(1)}, u32[]{:S(2)}, u32[]{:S(2)}) collective-permute-start(bf16[96,1024]{1,0:T(8,128)(2,1)S(1)} %add_convert_fusion.refs_0_._), channel_id=1, source_target_pairs={{0,48},{16,0},{32,16},{48,32},{64,112},{80,64},{96,80},{112,96},{1... | collective-permute-start | bytes 589832 | tf_op jit(solution)/shard_map/ppermute | solution.py:48
  107.3 31.2 %collective-permute-start.24 = (bf16[4,2,48,1536]{3,2,1,0:T(8,128)(2,1)S(1)}, bf16[4,2,48,1536]{3,2,1,0:T(8,128)(2,1)S(1)}, u32[]{:S(2)}, u32[]{:S(2)}) collective-permute-start(bf16[4,2,48,1536]{3,2,1,0:T(8,128)(2,1)S(1)} %get-tuple-element.65), channel_id=1, source_target_pairs={{0,8},{1,9},{2,10},{3,11},{4,12},{5,13},{6,14},{7,15},{8,0},{9,1},... | collective-permute-start | bytes 3538952 | tf_op jit(solution)/shard_map/ppermute | solution.py:52
  111.1 12.7 %collective-permute-start.28 = (bf16[96,2176]{1,0:T(8,128)(2,1)S(1)}, bf16[96,2176]{1,0:T(8,128)(2,1)S(1)}, u32[]{:S(2)}, u32[]{:S(2)}) collective-permute-start(bf16[96,2176]{1,0:T(8,128)(2,1)S(1)} %get-tuple-element.74), channel_id=1, source_target_pairs={{0,2},{1,3},{2,4},{3,5},{4,6},{5,7},{6,0},{7,1},{8,10},{9,11},{10,... | collective-permute-start | bytes 1253384 | tf_op jit(solution)/shard_map/ppermute | solution.py:52
  111.1 12.7 %collective-permute-start.29 = (bf16[96,2048]{1,0:T(8,128)(2,1)S(1)}, bf16[96,2048]{1,0:T(8,128)(2,1)S(1)}, u32[]{:S(2)}, u32[]{:S(2)}) collective-permute-start(bf16[96,2048]{1,0:T(8,128)(2,1)S(1)} %get-tuple-element.63.refs_0_), channel_id=1, source_target_pairs={{0,6},{1,7},{2,0},{3,1},{4,2},{5,3},{6,4},{7,5},{8,14},{9,15},{10,... | collective-permute-start | bytes 1179656 | tf_op jit(solution)/shard_map/ppermute | solution.py:52
  114.3 11.7 %collective-permute-start.23 = (bf16[384,512]{1,0:T(8,128)(2,1)S(1)}, bf16[384,512]{1,0:T(8,128)(2,1)S(1)}, u32[]{:S(2)}, u32[]{:S(2)}) collective-permute-start(bf16[384,512]{1,0:T(8,128)(2,1)S(1)} %get-tuple-element.53), channel_id=1, source_target_pairs={{0,1},{1,0},{2,3},{3,2},{4,5},{5,4},{6,7},{7,6},{8,9},{9,8},{10,11... | collective-permute-start | bytes 1179656 | tf_op jit(solution)/shard_map/ppermute | solution.py:52
  114.3 23.7 %collective-permute-start.32 = (bf16[96,2176]{1,0:T(8,128)(2,1)S(1)}, bf16[96,2176]{1,0:T(8,128)(2,1)S(1)}, u32[]{:S(2)}, u32[]{:S(2)}) collective-permute-start(bf16[96,2176]{1,0:T(8,128)(2,1)S(1)} %get-tuple-element.78), channel_id=1, source_target_pairs={{0,6},{1,7},{2,0},{3,1},{4,2},{5,3},{6,4},{7,5},{8,14},{9,15},{10,... | collective-permute-start | bytes 1253384 | tf_op jit(solution)/shard_map/ppermute | solution.py:52
  124.0 14.0 %collective-permute-start.30 = (bf16[96,2176]{1,0:T(8,128)(2,1)S(1)}, bf16[96,2176]{1,0:T(8,128)(2,1)S(1)}, u32[]{:S(2)}, u32[]{:S(2)}) collective-permute-start(bf16[96,2176]{1,0:T(8,128)(2,1)S(1)} %get-tuple-element.76), channel_id=1, source_target_pairs={{0,2},{1,3},{2,4},{3,5},{4,6},{5,7},{6,0},{7,1},{8,10},{9,11},{10,... | collective-permute-start | bytes 1253384 | tf_op jit(solution)/shard_map/ppermute | solution.py:52
  124.1 13.9 %collective-permute-start.31 = (bf16[96,2048]{1,0:T(8,128)(2,1)S(1)}, bf16[96,2048]{1,0:T(8,128)(2,1)S(1)}, u32[]{:S(2)}, u32[]{:S(2)}) collective-permute-start(bf16[96,2048]{1,0:T(8,128)(2,1)S(1)} %get-tuple-element.77), channel_id=1, source_target_pairs={{0,2},{1,3},{2,4},{3,5},{4,6},{5,7},{6,0},{7,1},{8,10},{9,11},{10,... | collective-permute-start | bytes 1179656 | tf_op jit(solution)/shard_map/ppermute | solution.py:52
  126.0 12.0 %collective-permute-start.33 = (bf16[96,2048]{1,0:T(8,128)(2,1)S(1)}, bf16[96,2048]{1,0:T(8,128)(2,1)S(1)}, u32[]{:S(2)}, u32[]{:S(2)}) collective-permute-start(bf16[96,2048]{1,0:T(8,128)(2,1)S(1)} %get-tuple-element.79), channel_id=1, source_target_pairs={{0,6},{1,7},{2,0},{3,1},{4,2},{5,3},{6,4},{7,5},{8,14},{9,15},{10,... | collective-permute-start | bytes 1179656 | tf_op jit(solution)/shard_map/ppermute | solution.py:52
  138.8 10.3 %collective-permute-start.25 = (bf16[2,48,1536]{2,1,0:T(8,128)(2,1)S(1)}, bf16[2,48,1536]{2,1,0:T(8,128)(2,1)S(1)}, u32[]{:S(2)}, u32[]{:S(2)}) collective-permute-start(bf16[2,48,1536]{2,1,0:T(8,128)(2,1)S(1)} %get-tuple-element.68), channel_id=1, source_target_pairs={{0,4},{1,5},{2,6},{3,7},{4,0},{5,1},{6,2},{7,3},{8,12},{9,13},{10,... | collective-permute-start | bytes 884744 | tf_op jit(solution)/shard_map/ppermute | solution.py:52
  141.0 10.2 %collective-permute-start.26 = (bf16[2,48,1536]{2,1,0:T(8,128)(2,1)S(1)}, bf16[2,48,1536]{2,1,0:T(8,128)(2,1)S(1)}, u32[]{:S(2)}, u32[]{:S(2)}) collective-permute-start(bf16[2,48,1536]{2,1,0:T(8,128)(2,1)S(1)} %get-tuple-element.69), channel_id=1, source_target_pairs={{0,2},{1,3},{2,4},{3,5},{4,6},{5,7},{6,0},{7,1},{8,10},{9,11},{10,... | collective-permute-start | bytes 884744 | tf_op jit(solution)/shard_map/ppermute | solution.py:52
  (26 other events, 171.1 us)
